TPU v7x, 32 devices: a whole 2x2x4 slice. The times are simulated.
32 devices in a mesh: groups: 2 (over y), seq: 4 (over z), head: 2 (over x), rep: 2 (over core).
Axes of the slice: x: 2, y: 2, z: 4, core: 2. Of those that a mesh axis runs over, the one named last changes fastest.
Arguments:
- normed: bfloat16 [2048, 4096], P(('groups', 'seq')), parts along dimension 0, may hold values from -6 to 6
- query_proj: bfloat16 [2048, 2048], P(('groups', 'seq'), ('head', 'rep')), parts along dimension 0, may hold values from -3 to 3
- key_proj: bfloat16 [2048, 2048], P(('groups', 'seq'), ('head', 'rep')), parts along dimension 0, may hold values from -3 to 3
- value_proj: bfloat16 [2048, 2048], P(('groups', 'seq'), ('head', 'rep')), parts along dimension 0, may hold values from -6 to 6
- out_weight: bfloat16 [2048, 4096], P(('head', 'rep'), 'seq'), may hold values from -0.125 to 0.125
- value_probe: bfloat16 [8192, 2048], P(('groups', 'seq'), ('head', 'rep')), parts along dimension 0, may hold values from -0.09375 to 0.09375
- out_probe: bfloat16 [4096, 4096], P(('groups', 'head', 'rep'), 'seq'), parts along dimension 0, may hold values from -0.125 to 0.125
Outputs:
- value_curv: bfloat16 [8192, 2048], P(('groups', 'seq'), ('head', 'rep')), parts along dimension 0
- out_curv: bfloat16 [4096, 4096], P(('groups', 'head', 'rep'), 'seq'), parts along dimension 0
There are 2 independent parts, one for each index of `groups`. A program takes and returns all parts, laid end to end along the dimension named above; an argument that names none is the same for every part. Nothing has to cross between parts.
All inputs are finite; a program needn't handle non-finite values.
Results may differ from a plain program's by a relative error of at most 0.018.
Values may be sent and summed in bfloat16 or wider, within the bound.
No kernel may reach another device: no remote copies, remote signals or barrier semaphores. Data moves between devices by JAX's collectives and lax.ppermute only.
A program may use at most 128 MiB of HBM per device.

v0:
```python
import jax
import jax.numpy as jnp
from jax import lax
from jax.sharding import PartitionSpec as P

DH = 64


def body(normed, query_proj, key_proj, value_proj, out_weight, value_probe, out_probe):
    tok_rows = normed.shape[0]
    col_count = query_proj.shape[1]
    local_heads = col_count // DH
    feature_cols = normed
    value_tangent = jnp.dot(
        feature_cols,
        lax.all_gather(value_probe, "seq", axis=0, tiled=True),
        preferred_element_type=jnp.float32,
    ).astype(jnp.bfloat16)
    query_heads = query_proj.reshape(tok_rows, local_heads, DH)
    run_max = jnp.full((tok_rows, local_heads), -1e30, jnp.float32)
    key_rows = lax.all_gather(key_proj, "seq", axis=0, tiled=True)
    value_rows = lax.all_gather(value_proj, "seq", axis=0, tiled=True)
    tangent_rows = lax.all_gather(value_tangent, "seq", axis=0, tiled=True)
    piece_rows = key_rows.shape[0]
    key_heads = key_rows.reshape(piece_rows, local_heads, DH)
    value_heads = value_rows.reshape(piece_rows, local_heads, DH)
    tangent_heads = tangent_rows.reshape(piece_rows, local_heads, DH)
    scores = jnp.einsum("qhd,khd->qhk", query_heads, key_heads, preferred_element_type=jnp.float32)
    next_max = jnp.maximum(run_max, jnp.max(scores, axis=2))
    exp_rows = jnp.exp(scores - next_max[:, :, None])
    run_sum = jnp.sum(exp_rows, axis=2)
    prob_bf = exp_rows.astype(jnp.bfloat16)
    accum_v = jnp.einsum("qhk,khd->qhd", prob_bf, value_heads, preferred_element_type=jnp.float32)
    accum_t = jnp.einsum("qhk,khd->qhd", prob_bf, tangent_heads, preferred_element_type=jnp.float32)
    run_max, run_sum, accum_v, accum_t = (next_max, run_sum, accum_v, accum_t)
    row_lse = run_max + jnp.log(run_sum)
    attended = (accum_v / run_sum[:, :, None]).reshape(tok_rows, col_count).astype(jnp.bfloat16)
    attended_tan = (accum_t / run_sum[:, :, None]).reshape(tok_rows, col_count).astype(jnp.bfloat16)
    weight_full, probe_full = (
        lax.all_gather(out_weight, "seq", axis=1, tiled=True),
        lax.all_gather(out_probe, "seq", axis=1, tiled=True),
    )
    partial_out = jnp.dot(attended_tan, weight_full, preferred_element_type=jnp.float32) + jnp.dot(
        attended, probe_full, preferred_element_type=jnp.float32
    )
    tangent_out = lax.psum(partial_out.astype(jnp.bfloat16), ("head", "rep"))
    out_term = jnp.einsum("tc,td->cd", attended, tangent_out, preferred_element_type=jnp.float32)
    out_curv = lax.psum_scatter(
        out_term.astype(jnp.bfloat16), "seq", scatter_dimension=1, tiled=True
    )
    grad_out = jnp.einsum(
        "td,cd->tc", tangent_out, weight_full, preferred_element_type=jnp.float32
    ).astype(jnp.bfloat16)
    grad_heads = grad_out.reshape(tok_rows, local_heads, DH)
    every_key = lax.all_gather(key_proj, "seq", axis=0, tiled=True)
    key_rows = every_key.reshape(tok_rows * lax.axis_size("seq"), local_heads, DH)
    scores = jnp.einsum("qhd,khd->qhk", query_heads, key_rows, preferred_element_type=jnp.float32)
    prob_bf = jnp.exp(scores - row_lse[:, :, None]).astype(jnp.bfloat16)
    value_grad = lax.psum_scatter(
        jnp.einsum("qhk,qhd->khd", prob_bf, grad_heads, preferred_element_type=jnp.float32)
        .reshape(tok_rows * lax.axis_size("seq"), col_count)
        .astype(jnp.bfloat16),
        "seq",
        scatter_dimension=0,
        tiled=True,
    )
    feature_cols = normed
    value_curv = lax.psum_scatter(
        jnp.einsum(
            "tr,tc->rc", feature_cols, value_grad, preferred_element_type=jnp.float32
        ).astype(jnp.bfloat16),
        "seq",
        scatter_dimension=0,
        tiled=True,
    )
    return (value_curv, out_curv)


def solution(mesh):
    in_specs = (
        P(("groups", "seq"), None),
        P(("groups", "seq"), ("head", "rep")),
        P(("groups", "seq"), ("head", "rep")),
        P(("groups", "seq"), ("head", "rep")),
        P(("head", "rep"), "seq"),
        P(("groups", "seq"), ("head", "rep")),
        P(("groups", "head", "rep"), "seq"),
    )
    out_specs = (P(("groups", "seq"), ("head", "rep")), P(("groups", "head", "rep"), "seq"))
    return jax.shard_map(body, mesh=mesh, in_specs=in_specs, out_specs=out_specs, check_vma=False)
```

profile of v0, /device:TPU:0, one launch (start us, length us, event | category | flops | bytes accessed | tf_op | source)
XLA Modules:
  0.0 602.5 jit_solution(16441903193555431618)
XLA Ops:
  7.2 0.0 copy-start
  7.2 0.0 all-gather.7.cloned.1.call-start
  7.2 0.7 all-gather.7.cloned.1.call-update
  7.9 0.0 all-gather.11.cloned.1.call-start
  8.0 0.7 all-gather.11.cloned.1.call-update
  8.7 0.0 all-gather.15.cloned.1.call-start
  8.7 0.7 all-gather.15.cloned.1.call-update
  9.4 0.0 copy-start.2
  9.4 0.0 all-gather.9.cloned.1.call-start
  9.5 83.6 %all-gather.7.cloned.1.call-done = bf16[4096,512]{1,0:T(8,128)(2,1)} async-done(((bf16[1024,512]{1,0:T(8,128)(2,1)}), bf16[4096,512]{1,0:T(8,128)(2,1)}) %all-gather.7.cloned.1.call-update) | async-done | bytes 4194320 | tf_op jit(solution)/shard_map/all_gather | solution.py:16
  93.1 0.0 copy-done
  93.1 4.1 convolution_convert_fusion.3
  97.2 0.0 all-gather.9.cloned.1.call-update
  97.2 0.0 all-gather.13.cloned.1.call-start
  97.3 0.5 all-gather.13.cloned.1.call-update
  97.8 0.0 all-gather.17.cloned.1.call-start
  97.9 0.5 all-gather.17.cloned.1.call-update
  98.4 0.0 all-reduce.2.cloned.1.call-start
  98.5 0.0 copy-done.2
  98.5 0.1 copy.20
  98.6 22.5 %all-gather.11.cloned.1.call-done = bf16[1024,512]{1,0:T(8,128)(2,1)} async-done(((bf16[256,512]{1,0:T(8,128)(2,1)}), bf16[1024,512]{1,0:T(8,128)(2,1)}) %all-gather.11.cloned.1.call-update) | async-done | bytes 1048592 | tf_op jit(solution)/shard_map/all_gather | solution.py:21
  121.1 2.3 copy.19
  123.4 26.8 %all-gather.15.cloned.1.call-done = bf16[1024,512]{1,0:T(8,128)(2,1)} async-done(((bf16[256,512]{1,0:T(8,128)(2,1)}), bf16[1024,512]{1,0:T(8,128)(2,1)}) %all-gather.15.cloned.1.call-update) | async-done | bytes 1048592 | tf_op jit(solution)/shard_map/all_gather | solution.py:22
  150.2 1.5 copy.22
  151.7 2.5 bitcast_reduce_fusion
  154.2 0.0 copy-start.1
  154.2 1.1 fusion.3
  155.3 2.1 copy-done.1
  157.4 1.4 fusion.16
  158.9 20.8 %all-gather.9.cloned.1.call-done = bf16[1024,512]{1,0:T(8,128)(2,1)} async-done(((bf16[256,512]{1,0:T(8,128)(2,1)}), bf16[1024,512]{1,0:T(8,128)(2,1)}) %all-gather.9.cloned.1.call-update) | async-done | bytes 1048592 | tf_op jit(solution)/shard_map/all_gather | solution.py:23
  179.6 1.5 copy.18
  181.1 5.5 fusion.15
  186.6 74.8 %all-gather.13.cloned.1.call-done = bf16[512,4096]{1,0:T(8,128)(2,1)} async-done(((bf16[512,1024]{1,0:T(8,128)(2,1)}), bf16[512,4096]{1,0:T(8,128)(2,1)}) %all-gather.13.cloned.1.call-update) | async-done | bytes 4194320 | tf_op jit(solution)/shard_map/all_gather | solution.py:40
  261.4 5.5 fusion.19
  266.9 75.2 %all-gather.17.cloned.1.call-done = bf16[512,4096]{1,0:T(8,128)(2,1)} async-done(((bf16[512,1024]{1,0:T(8,128)(2,1)}), bf16[512,4096]{1,0:T(8,128)(2,1)}) %all-gather.17.cloned.1.call-update) | async-done | bytes 4194320 | tf_op jit(solution)/shard_map/all_gather | solution.py:41
  342.1 6.1 %fusion.6 = bf16[256,4096]{1,0:T(8,128)(2,1)} fusion(f32[256,4096]{1,0:T(8,128)} %fusion.19, bf16[256,512]{0,1:T(8,128)(2,1)S(1)} %bitcast.64, bf16[512,4096]{1,0:T(8,128)(2,1)} %all-gather.17.cloned.1.call-done), kind=kOutput, calls=%fused_computation.12 | convolution fusion | flops 1075838976 | bytes 10747904 | tf_op jit(solution)/shard_map/dot_general | solution.py:43
  348.3 0.0 all-reduce.2.cloned.1.call-update
  348.3 0.0 reduce-scatter.4.cloned.1.call-start
  348.3 50.0 %all-reduce.2.cloned.1.call-done = bf16[256,4096]{1,0:T(8,128)(2,1)} async-done(((bf16[256,4096]{1,0:T(8,128)(2,1)}), bf16[256,4096]{1,0:T(8,128)(2,1)}) %all-reduce.2.cloned.1.call-update) | async-done | bytes 2097168 | tf_op jit(solution)/shard_map/psum | solution.py:46
  398.3 4.1 convolution_convert_fusion.2
  402.4 0.1 copy.24
  402.6 5.8 fusion.10
  408.4 0.0 reduce-scatter.4.cloned.1.call-update
  408.4 0.2 reduce-scatter.6.cloned.1.call-start
  408.6 27.1 %reduce-scatter.4.cloned.1.call-done = bf16[256,512]{0,1:T(8,128)(2,1)} async-done(((bf16[1024,512]{0,1:T(8,128)(2,1)}), bf16[256,512]{0,1:T(8,128)(2,1)}) %reduce-scatter.4.cloned.1.call-update) | async-done | bytes 262160 | tf_op jit(solution)/shard_map/reduce_scatter | solution.py:59
  435.8 4.2 fusion.5
  439.9 0.0 reduce-scatter.6.cloned.1.call-update
  440.0 0.0 reduce-scatter.8.cloned.1.call-start
  440.0 4.8 convolution_convert_fusion
  444.8 0.0 reduce-scatter.8.cloned.1.call-update
  444.9 70.7 %reduce-scatter.6.cloned.1.call-done = bf16[1024,512]{0,1:T(8,128)(2,1)} async-done(((bf16[4096,512]{0,1:T(8,128)(2,1)}), bf16[1024,512]{0,1:T(8,128)(2,1)}) %reduce-scatter.6.cloned.1.call-update) | async-done | bytes 1048592 | tf_op jit(solution)/shard_map/reduce_scatter | solution.py:68
  515.5 2.3 copy.26
  517.8 77.8 %reduce-scatter.8.cloned.1.call-done = bf16[512,1024]{1,0:T(8,128)(2,1)} async-done(((bf16[512,4096]{1,0:T(8,128)(2,1)}), bf16[512,1024]{1,0:T(8,128)(2,1)}) %reduce-scatter.8.cloned.1.call-update) | async-done | bytes 1048592 | tf_op jit(solution)/shard_map/reduce_scatter | solution.py:48
  (2 shorter events, 0.0 us)
Async XLA Ops:
  7.2 85.9 %copy-start = (bf16[256,4096]{1,0:T(8,128)(2,1)S(1)}, bf16[256,4096]{1,0:T(8,128)(2,1)}, u32[]{:S(2)}) copy-start(bf16[256,4096]{1,0:T(8,128)(2,1)} %param.7) | copy-start | bytes 6291460
  7.2 85.9 %all-gather.7.cloned.1.call-start = ((), (), s32[]{:S(2)}) async-start(), calls=%async_computation.3 | async-start | bytes 5242880 | tf_op jit(solution)/shard_map/all_gather | solution.py:16
  7.9 113.2 %all-gather.11.cloned.1.call-start = ((), (), s32[]{:S(2)}) async-start(), calls=%async_computation.5 | async-start | bytes 1310720 | tf_op jit(solution)/shard_map/all_gather | solution.py:21
  8.7 141.5 %all-gather.15.cloned.1.call-start = ((), (), s32[]{:S(2)}) async-start(), calls=%async_computation.7 | async-start | bytes 1310720 | tf_op jit(solution)/shard_map/all_gather | solution.py:22
  9.4 89.1 %copy-start.2 = (bf16[256,512]{1,0:T(8,128)(2,1)S(1)}, bf16[256,512]{1,0:T(8,128)(2,1)}, u32[]{:S(2)}) copy-start(bf16[256,512]{1,0:T(8,128)(2,1)} %param.8) | copy-start | bytes 786436
  9.4 170.2 %all-gather.9.cloned.1.call-start = ((), (), s32[]{:S(2)}) async-start(), calls=%async_computation.4 | async-start | bytes 1310720 | tf_op jit(solution)/shard_map/all_gather | solution.py:23
  97.2 164.1 %all-gather.13.cloned.1.call-start = ((), (), s32[]{:S(2)}) async-start(), calls=%async_computation.6 | async-start | bytes 5242880 | tf_op jit(solution)/shard_map/all_gather | solution.py:40
  97.8 244.3 %all-gather.17.cloned.1.call-start = ((), (), s32[]{:S(2)}) async-start(), calls=%async_computation.8 | async-start | bytes 5242880 | tf_op jit(solution)/shard_map/all_gather | solution.py:41
  98.4 299.9 %all-reduce.2.cloned.1.call-start = ((), (), s32[]{:S(2)}) async-start(), calls=%async_computation.9 | async-start | bytes 4194304 | tf_op jit(solution)/shard_map/psum | solution.py:46
  154.2 3.2 copy-start.1
  348.3 87.5 %reduce-scatter.4.cloned.1.call-start = ((), (), s32[]{:S(2)}) async-start(), calls=%async_computation.10 | async-start | bytes 1310720 | tf_op jit(solution)/shard_map/reduce_scatter | solution.py:59
  408.4 107.2 %reduce-scatter.6.cloned.1.call-start = ((), (), s32[]{:S(2)}) async-start(), calls=%async_computation.11 | async-start | bytes 5242880 | tf_op jit(solution)/shard_map/reduce_scatter | solution.py:68
  440.0 155.7 %reduce-scatter.8.cloned.1.call-start = ((), (), s32[]{:S(2)}) async-start(), calls=%async_computation.12 | async-start | bytes 5242880 | tf_op jit(solution)/shard_map/reduce_scatter | solution.py:48
Sparse Core Ops, SparseCore 0:
  9.6 83.4 all-gather.6
  94.6 26.4 all-gather.10
  122.7 27.4 all-gather.14
  152.2 27.4 all-gather.8
  181.0 80.2 all-gather.12
  262.8 79.2 all-gather.16
  348.4 49.8 all-reduce.1
  408.5 27.2 reduce-scatter.3
  440.1 75.4 reduce-scatter.5
  518.4 77.2 reduce-scatter.7
where the time goes:
time: 603 us; the launch traced here: 602 us
  waiting for transfers between devices  533 us (88%)
  matrix products  44.1 us (7%)
  between operations  14.3 us (2%)
  local copies, waits for them, and re-layouts  9.88 us (2%)
    all_gather x1, waiting for transfers between devices, body(): lax.all_gather(value_probe, 'seq', axis=0, tiled=True)  83.6 us
    reduce_scatter x1, waiting for transfers between devices, body(): lax.psum_scatter(out_term.astype(jnp.bfloat16), 'seq', scatter_dimension=...  77.8 us
    all_gather x1, waiting for transfers between devices, body(): lax.all_gather(out_probe, 'seq', axis=1, tiled=True)  75.2 us
    all_gather x1, waiting for transfers between devices, body(): lax.all_gather(out_weight, 'seq', axis=1, tiled=True)  74.8 us
    reduce_scatter x1, waiting for transfers between devices, body(): lax.psum_scatter(jnp.einsum('tr,tc->rc', feature_cols, value_grad, prefer...  70.7 us
    psum x1, waiting for transfers between devices, body(): tangent_out = lax.psum(partial_out.astype(jnp.bfloat16), ('head', 'rep'))  50 us
    reduce_scatter x1, waiting for transfers between devices, body(): lax.psum_scatter(jnp.einsum('qhk,qhd->khd', prob_bf, grad_heads, preferre...  27.1 us
    all_gather x1, waiting for transfers between devices, body(): value_rows = lax.all_gather(value_proj, 'seq', axis=0, tiled=True)  26.8 us
  transfers between devices with their start and end apart: 10, of which 10 were waited for; matrix products, arithmetic and copies ran while one was open for 5% of the time, Pallas kernels for 0%

commit v1 on v0

--- a/solution.py
+++ b/solution.py
@@ -6,7 +6,93 @@
 DH = 64
 
 
-def body(normed, query_proj, key_proj, value_proj, out_weight, value_probe, out_probe):
+def swap(x, axis):
+    return lax.ppermute(x, axis, [(0, 1), (1, 0)])
+
+
+def in_order(own, other, at):
+    return jnp.where(at == 0, jnp.concatenate([own, other]), jnp.concatenate([other, own]))
+
+
+def to_heads(x):
+    n = lax.axis_size("seq")
+    rows, cols = x.shape
+    blocks = x.reshape(rows, n, cols // n).transpose(1, 0, 2)
+    return lax.all_to_all(blocks, "seq", 0, 0).reshape(n * rows, cols // n)
+
+
+def scatter_sum(x):
+    n = lax.axis_size("seq")
+    rows, cols = x.shape
+    blocks = x.astype(jnp.bfloat16).reshape(rows, n, cols // n).transpose(1, 0, 2)
+    got = lax.all_to_all(blocks, "seq", 0, 0)
+    return jnp.sum(got.astype(jnp.float32), axis=0).astype(jnp.bfloat16)
+
+
+def gather_cols(x):
+    n = lax.axis_size("seq")
+    me = lax.axis_index("seq")
+    full = jnp.zeros((x.shape[0], n * x.shape[1]), x.dtype)
+    for k in range(n):
+        block = x if k == 0 else lax.ppermute(x, "seq", [(i, (i + k) % n) for i in range(n)])
+        full = lax.dynamic_update_slice(full, block, (0, lax.rem(me - k + n, n) * x.shape[1]))
+    return full
+
+
+def dot(spec, a, b):
+    return jnp.einsum(spec, a, b, preferred_element_type=jnp.float32)
+
+
+def by_heads(normed, query_proj, key_proj, value_proj, out_weight, value_probe, out_probe):
+    n = lax.axis_size("seq")
+    at_head, at_rep = lax.axis_index("head"), lax.axis_index("rep")
+    tok, width = normed.shape
+    quarter = tok // 4
+    slab = width // n
+    mine = lax.dynamic_slice(normed, ((at_head * 2 + at_rep) * quarter, 0), (quarter, width))
+    got = lax.all_to_all(mine.reshape(quarter, n, slab).transpose(1, 0, 2), "seq", 0, 0)
+    pair = in_order(got[None], swap(got, "head")[None], at_head)
+    four = in_order(pair[None], swap(pair, "rep")[None], at_rep)
+    feats = four.transpose(2, 1, 0, 3, 4).reshape(n * tok, slab)
+    query, key, value = to_heads(query_proj), to_heads(key_proj), to_heads(value_proj)
+    tokens, cols = query.shape
+    heads = cols // DH
+    tangent = scatter_sum(dot("td,dc->tc", feats, value_probe))
+
+    def split(x):
+        return x.reshape(tokens, heads, DH)
+
+    scores = dot("qhd,khd->hqk", split(query), split(key))
+    top = jnp.max(scores, axis=2, keepdims=True)
+    row_lse = top + jnp.log(jnp.sum(jnp.exp(scores - top), axis=2, keepdims=True))
+    probs = jnp.exp(scores - row_lse).astype(jnp.bfloat16)
+    attended = dot("hqk,khd->qhd", probs, split(value)).reshape(tokens, cols).astype(jnp.bfloat16)
+    attended_tan = dot("hqk,khd->qhd", probs, split(tangent)).reshape(tokens, cols).astype(jnp.bfloat16)
+    att, att_tan = gather_cols(attended), gather_cols(attended_tan)
+    term = (dot("tc,cd->td", att, out_probe) + dot("tc,cd->td", att_tan, out_weight)).astype(jnp.bfloat16)
+    half = tokens // 2
+    away = lax.dynamic_slice(term, ((1 - at_rep) * half, 0), (half, slab))
+    home = lax.dynamic_slice(term, (at_rep * half, 0), (half, slab))
+    two = (home.astype(jnp.float32) + swap(away, "rep").astype(jnp.float32)).astype(jnp.bfloat16)
+    all4 = (two.astype(jnp.float32) + swap(two, "head").astype(jnp.float32)).astype(jnp.bfloat16)
+    tangent_out = in_order(all4, swap(all4, "rep"), at_rep)
+    out_curv = dot("tc,td->cd", att, tangent_out).astype(jnp.bfloat16)
+    grad_out = scatter_sum(dot("td,cd->tc", tangent_out, out_weight))
+    value_grad = dot("hqk,qhd->khd", probs, split(grad_out)).reshape(tokens, cols).astype(jnp.bfloat16)
+    value_curv = dot("td,tc->dc", feats, gather_cols(value_grad)).astype(jnp.bfloat16)
+    return value_curv, out_curv
+
+
+def body(*args):
+    cols = args[1].shape[1]
+    n = lax.axis_size("seq")
+    even = cols % (n * 128) == 0 and args[0].shape[0] % 64 == 0
+    if even and lax.axis_size("head") == 2 and lax.axis_size("rep") == 2:
+        return by_heads(*args)
+    return by_tokens(*args)
+
+
+def by_tokens(normed, query_proj, key_proj, value_proj, out_weight, value_probe, out_probe):
     tok_rows = normed.shape[0]
     col_count = query_proj.shape[1]
     local_heads = col_count // DH

time: 603 us -> 242 us (0.40)
  waiting for transfers between devices: 533 us -> 77.1 us
  blocking collectives: 0 us -> 51.5 us
  starting transfers between devices: 0.58 us -> 40.6 us
  matrix products: 44.1 us -> 26.5 us
  local copies, waits for them, and re-layouts: 9.88 us -> 25.5 us
  other arithmetic: 1.11 us -> 16 us
  between operations: 14.3 us -> 1.07 us
    all_gather x6 -> x0, waiting for transfers between devices: 304 us -> none  [the longest x1 83.6 us: body(): lax.all_gather(value_probe, 'seq', axis=0, tiled=True)]
    reduce_scatter x3 -> x0, waiting for transfers between devices: 176 us -> none  [the longest x1 77.8 us: body(): lax.psum_scatter(out_term.astype(jnp.bfloat16), 'seq', scatter_dimension=...]
    ppermute x0 -> x14, waiting for transfers between devices: none -> 61.8 us  [the longest x9 31.7 us: gather_cols(): lax.ppermute(x, 'seq', [(i, (i + k) % n) for i in range(n)])]
    all_to_all x0 -> x2, blocking collectives: none -> 51.5 us  [the longest x1 30.9 us: scatter_sum(): got = lax.all_to_all(blocks, 'seq', 0, 0)]
    psum x1 -> x0, waiting for transfers between devices: 50 us -> none  [body(): tangent_out = lax.psum(partial_out.astype(jnp.bfloat16), ('head', 'rep'))]
    ppermute x0 -> x14, starting transfers between devices: none -> 24.1 us  [the longest x9 21.8 us: gather_cols(): lax.ppermute(x, 'seq', [(i, (i + k) % n) for i in range(n)])]
    dot_general x10, matrix products: 44.1 us -> 26.5 us  [dot(): return jnp.einsum(spec, a, b, preferred_element_type=jnp.float32)]
    all_to_all x0 -> x4, starting transfers between devices: none -> 16.5 us  [the longest x3 11.5 us: to_heads(): return lax.all_to_all(blocks, 'seq', 0, 0).reshape(n * rows, cols // n)]
  transfers between devices with their start and end apart: 10 -> 18, of which waited for: 10 -> 11; matrix products, arithmetic and copies ran while one was open for 5% -> 20% of each run, Pallas kernels for 0% -> 0%
where the time goes in v1:
time: 242 us; the launch traced here: 238 us
  waiting for transfers between devices  77.1 us (32%)
  blocking collectives  51.5 us (21%)
  starting transfers between devices  40.6 us (17%)
  matrix products  26.5 us (11%)
  local copies, waits for them, and re-layouts  25.5 us (11%)
  other arithmetic  16 us (7%)
    ppermute x9, waiting for transfers between devices, gather_cols(): lax.ppermute(x, 'seq', [(i, (i + k) % n) for i in range(n)])  31.7 us
    all_to_all x1, blocking collectives, scatter_sum(): got = lax.all_to_all(blocks, 'seq', 0, 0)  30.9 us
    ppermute x5, waiting for transfers between devices, swap(): return lax.ppermute(x, axis, [(0, 1), (1, 0)])  30.1 us
    dot_general x10, matrix products, dot(): return jnp.einsum(spec, a, b, preferred_element_type=jnp.float32)  26.5 us
    ppermute x9, starting transfers between devices, gather_cols(): lax.ppermute(x, 'seq', [(i, (i + k) % n) for i in range(n)])  21.8 us
    all_to_all x1, blocking collectives, by_heads(): lax.all_to_all(mine.reshape(quarter, n, slab).transpose(1, 0, 2), 'seq',...  20.6 us
    all_to_all x3, starting transfers between devices, to_heads(): return lax.all_to_all(blocks, 'seq', 0, 0).reshape(n * rows, cols // n)  11.5 us
    unnamed x33, local copies, waits for them, and re-layouts  9.9 us
  transfers between devices with their start and end apart: 18, of which 11 were waited for; matrix products, arithmetic and copies ran while one was open for 20% of the time, Pallas kernels for 0%

profile of v1, /device:TPU:0, one launch (start us, length us, event | category | flops | bytes accessed | tf_op | source)
XLA Modules:
  0.0 238.4 jit_solution(1593363326158565617)
XLA Ops:
  0.7 1.6 copy-done
  2.3 0.4 reshape.105
  2.8 20.6 %all_to_all.30 = bf16[4,64,1024]{2,1,0:T(8,128)(2,1)S(1)} all-to-all(bf16[4,64,1024]{2,1,0:T(8,128)(2,1)S(1)} %copy.30), channel_id=1, replica_groups=mesh['groups'=2,'seq'=4,'head'=2,'rep'=2] {'seq'}, dimensions={0} | all-to-all | bytes 1048576 | tf_op jit(solution)/shard_map/all_to_all | solution.py:53
  23.4 1.5 collective-permute-start
  24.9 0.8 copy.35
  25.8 3.4 %all-to-all-start.2 = ((bf16[4,256,128]{1,2,0:T(8,128)(2,1)}), bf16[4,256,128]{1,2,0:T(8,128)(2,1)S(1)}, u32[]{:S(2)}, u32[]{:S(2)}) async-start(bf16[4,256,128]{1,2,0:T(8,128)(2,1)} %bitcast.84), calls=%async_computation.2 | async-start | bytes 524288 | tf_op jit(solution)/shard_map/all_to_all | solution.py:21
  29.2 1.8 copy.33
  31.0 6.1 %all-to-all-done.2 = bf16[4,256,128]{1,2,0:T(8,128)(2,1)S(1)} async-done(((bf16[4,256,128]{1,2,0:T(8,128)(2,1)}), bf16[4,256,128]{1,2,0:T(8,128)(2,1)S(1)}, u32[]{:S(2)}, u32[]{:S(2)}) %all-to-all-start.2) | async-done | bytes 262176 | tf_op jit(solution)/shard_map/all_to_all | solution.py:21
  37.1 4.0 %all-to-all-start.1 = ((bf16[4,256,128]{1,2,0:T(8,128)(2,1)}), bf16[4,256,128]{1,2,0:T(8,128)(2,1)}, u32[]{:S(2)}, u32[]{:S(2)}) async-start(bf16[4,256,128]{1,2,0:T(8,128)(2,1)} %bitcast.83), calls=%async_computation.1 | async-start | bytes 524288 | tf_op jit(solution)/shard_map/all_to_all | solution.py:21
  41.1 1.1 maximum_select_fusion.2
  42.2 1.8 copy.37
  44.0 0.9 copy.36
  44.9 1.1 reshape_reshape.10
  46.0 1.9 all-to-all-done.1
  48.0 4.0 %all-to-all-start.3 = ((bf16[4,256,128]{1,2,0:T(8,128)(2,1)}), bf16[4,256,128]{1,2,0:T(8,128)(2,1)}, u32[]{:S(2)}, u32[]{:S(2)}) async-start(bf16[4,256,128]{1,2,0:T(8,128)(2,1)} %bitcast.82), calls=%async_computation.3 | async-start | bytes 524288 | tf_op jit(solution)/shard_map/all_to_all | solution.py:21
  52.0 1.9 copy.34
  53.9 1.8 reshape_reshape.9
  55.7 5.5 %fusion.2 = (f32[2,1024]{1,0:T(2,128)S(1)}, f32[2,1024,1024]{1,2,0:T(8,128)}) fusion(bf16[1024,2,64]{0,2,1:T(8,128)(2,1)} %reshape_reshape.9, bf16[1024,2,64]{0,2,1:T(8,128)(2,1)S(1)} %reshape_reshape.10), kind=kOutput, calls=%fused_computation.35 | convolution fusion | flops 270530560 | bytes 8921088 | tf_op jit(solution)/shard_map/qhd,khd->hqk/dot_general | solution.py:43
  61.5 2.0 maximum_select_fusion
  63.5 1.4 copy-done.4
  64.9 2.3 convolution_convert_fusion.3
  67.2 5.1 %all-to-all-start.4 = ((bf16[4,1024,128]{1,2,0:T(8,128)(2,1)}), bf16[4,1024,128]{1,2,0:T(8,128)(2,1)S(1)}, u32[]{:S(2)}, u32[]{:S(2)}) async-start(bf16[4,1024,128]{1,2,0:T(8,128)(2,1)} %bitcast.80), calls=%async_computation.4 | async-start | bytes 2097152 | tf_op jit(solution)/shard_map/all_to_all | solution.py:28
  72.2 4.5 %exponential_reduce_fusion = f32[2,1024]{1,0:T(2,128)S(1)} fusion(f32[2,1024,1024]{1,2,0:T(8,128)} %get-tuple-element.5, f32[2,1024]{1,0:T(2,128)S(1)} %get-tuple-element.4), kind=kLoop, calls=%fused_computation.1 | loop fusion | flops 4192256 | bytes 8404992 | tf_op jit(solution)/shard_map/reduce_sum | solution.py:67
  76.7 1.2 copy.38
  77.9 0.9 reshape_reshape.11
  78.8 4.7 %exponential_convert_fusion = bf16[2,1024,1024]{1,2,0:T(8,128)(2,1)S(1)} fusion(f32[2,1024,1024]{1,2,0:T(8,128)} %get-tuple-element.5, f32[2,1024]{1,0:T(2,128)S(1)} %log_add_fusion), kind=kLoop, calls=%fused_computation | loop fusion | flops 4194304 | bytes 12591104 | tf_op jit(solution)/shard_map/convert_element_type | solution.py:68
  83.5 0.8 convolution_convert_fusion.4
  84.4 1.1 copy-done.1
  85.5 2.0 collective-permute-start.2
  87.5 2.4 collective-permute-start.3
  89.8 1.5 collective-permute-start.4
  91.3 1.1 broadcast.15.clone.1
  92.4 0.7 constant_dynamic-update-slice_fusion.11
  93.1 7.4 %collective-permute-done.2 = bf16[1024,128]{0,1:T(8,128)(2,1)} collective-permute-done((bf16[1024,128]{0,1:T(8,128)(2,1)S(1)}, bf16[1024,128]{0,1:T(8,128)(2,1)}, u32[]{:S(2)}, u32[]{:S(2)}) %collective-permute-start.2) | collective-permute-done | bytes 262176 | tf_op jit(solution)/shard_map/ppermute | solution.py:37
  100.6 1.7 constant_dynamic-update-slice_fusion.10
  102.2 7.3 %all-to-all-done.4 = bf16[4,1024,128]{1,2,0:T(8,128)(2,1)S(1)} async-done(((bf16[4,1024,128]{1,2,0:T(8,128)(2,1)}), bf16[4,1024,128]{1,2,0:T(8,128)(2,1)S(1)}, u32[]{:S(2)}, u32[]{:S(2)}) %all-to-all-start.4) | async-done | bytes 1048608 | tf_op jit(solution)/shard_map/all_to_all | solution.py:28
  109.5 0.9 reduce_sum.34
  110.5 3.1 %convolution_convert_fusion.6 = bf16[2,64,1024]{2,1,0:T(8,128)(2,1)S(1)} fusion(bf16[1024,2,64]{0,2,1:T(8,128)(2,1)} %bitcast.69, bf16[2,1024,1024]{1,2,0:T(8,128)(2,1)} %copy-done.1), kind=kOutput, calls=%fused_computation.13 | convolution fusion | flops 268566528 | bytes 4718592 | tf_op jit(solution)/shard_map/hqk,khd->qhd/dot_general | solution.py:43
  113.6 7.2 %collective-permute-start.5 = (bf16[1024,128]{0,1:T(8,128)(2,1)S(1)}, bf16[1024,128]{0,1:T(8,128)(2,1)S(1)}, u32[]{:S(2)}, u32[]{:S(2)}) collective-permute-start(bf16[1024,128]{0,1:T(8,128)(2,1)S(1)} %bitcast.65), channel_id=1, source_target_pairs={{0,4},{4,8},{8,12},{12,0},{1,5},{5,9},{9,13},{13,1},{2,6},{6,10},{... | collective-permute-start | bytes 786440 | tf_op jit(solution)/shard_map/ppermute | solution.py:37
  120.8 1.7 constant_dynamic-update-slice_fusion.9
  122.4 2.1 collective-permute-start.6
  124.6 1.7 constant_dynamic-update-slice_fusion.8
  126.2 2.8 %collective-permute-start.7 = (bf16[1024,128]{0,1:T(8,128)(2,1)S(1)}, bf16[1024,128]{0,1:T(8,128)(2,1)S(1)}, u32[]{:S(2)}, u32[]{:S(2)}) collective-permute-start(bf16[1024,128]{0,1:T(8,128)(2,1)S(1)} %bitcast.67), channel_id=1, source_target_pairs={{0,12},{4,0},{8,4},{12,8},{1,13},{5,1},{9,5},{13,9},{2,14},{6,2},{... | collective-permute-start | bytes 786440 | tf_op jit(solution)/shard_map/ppermute | solution.py:37
  129.3 8.4 %collective-permute-done.6 = bf16[1024,128]{0,1:T(8,128)(2,1)S(1)} collective-permute-done((bf16[1024,128]{0,1:T(8,128)(2,1)S(1)}, bf16[1024,128]{0,1:T(8,128)(2,1)S(1)}, u32[]{:S(2)}, u32[]{:S(2)}) %collective-permute-start.6) | collective-permute-done | bytes 262176 | tf_op jit(solution)/shard_map/ppermute | solution.py:37
  137.7 2.9 %collective-permute-done.7 = bf16[1024,128]{0,1:T(8,128)(2,1)S(1)} collective-permute-done((bf16[1024,128]{0,1:T(8,128)(2,1)S(1)}, bf16[1024,128]{0,1:T(8,128)(2,1)S(1)}, u32[]{:S(2)}, u32[]{:S(2)}) %collective-permute-start.7) | collective-permute-done | bytes 262176 | tf_op jit(solution)/shard_map/ppermute | solution.py:37
  140.7 1.3 fusion.3
  142.0 2.6 %add_convert_fusion = bf16[1024,1024]{1,0:T(8,128)(2,1)S(1)} fusion(f32[1024,1024]{1,0:T(8,128)S(1)} %fusion.3, bf16[1024,512]{0,1:T(8,128)(2,1)} %constant_dynamic-update-slice_fusion.8, bf16[512,1024]{1,0:T(8,128)(2,1)S(1)} %copy-done.8), kind=kOutput, calls=%fused_computation.2 | convolution fusion | flops 1075838976 | bytes 8388608 | tf_op jit(solution)/shard_map/tc,cd->td/dot_general | solution.py:43
  144.6 1.3 copy-done.2
  146.1 2.8 %collective-permute-done.8 = bf16[512,1024]{1,0:T(8,128)(2,1)} collective-permute-done((bf16[512,1024]{1,0:T(8,128)(2,1)S(1)}, bf16[512,1024]{1,0:T(8,128)(2,1)}, u32[]{:S(2)}, u32[]{:S(2)}) %collective-permute-start.8) | collective-permute-done | bytes 1048608 | tf_op jit(solution)/shard_map/ppermute | solution.py:10
  148.9 1.9 add_convert_fusion.2
  150.8 0.6 collective-permute-start.9
  151.4 24.7 %collective-permute-done.9 = bf16[512,1024]{1,0:T(8,128)(2,1)S(1)} collective-permute-done((bf16[512,1024]{1,0:T(8,128)(2,1)S(1)}, bf16[512,1024]{1,0:T(8,128)(2,1)S(1)}, u32[]{:S(2)}, u32[]{:S(2)}) %collective-permute-start.9) | collective-permute-done | bytes 1048608 | tf_op jit(solution)/shard_map/ppermute | solution.py:10
  176.1 0.4 add_convert_fusion.1
  176.6 2.6 %collective-permute-done.10 = bf16[512,1024]{1,0:T(8,128)(2,1)S(1)} collective-permute-done((bf16[512,1024]{1,0:T(8,128)(2,1)S(1)}, bf16[512,1024]{1,0:T(8,128)(2,1)S(1)}, u32[]{:S(2)}, u32[]{:S(2)}) %collective-permute-start.10) | collective-permute-done | bytes 1048608 | tf_op jit(solution)/shard_map/ppermute | solution.py:10
  179.2 1.3 convolution_convert_fusion.2
  180.6 30.9 %all_to_all.31 = bf16[4,1024,128]{1,2,0:T(8,128)(2,1)S(1)} all-to-all(bf16[4,1024,128]{1,2,0:T(8,128)(2,1)S(1)} %bitcast.81), channel_id=1, replica_groups=mesh['groups'=2,'seq'=4,'head'=2,'rep'=2] {'seq'}, dimensions={0} | all-to-all | bytes 2097152 | tf_op jit(solution)/shard_map/all_to_all | solution.py:28
  211.7 3.7 %convolution_convert_fusion.5 = bf16[2,64,1024]{2,1,0:T(8,128)(2,1)S(1)} fusion(bf16[1024,2,64]{0,2,1:T(8,128)(2,1)S(1)} %bitcast.75, bf16[2,1024,1024]{1,2,0:T(8,128)(2,1)} %copy-done.1), kind=kOutput, calls=%fused_computation.12 | convolution fusion | flops 268566528 | bytes 4718592 | tf_op jit(solution)/shard_map/hqk,qhd->khd/dot_general | solution.py:43
  215.4 0.3 collective-permute-start.11
  215.7 1.8 collective-permute-start.12
  217.5 3.5 %convolution_convert_fusion = bf16[512,1024]{1,0:T(8,128)(2,1)} fusion(bf16[1024,512]{0,1:T(8,128)(2,1)} %constant_dynamic-update-slice_fusion.8, bf16[512,1024]{1,0:T(8,128)(2,1)S(1)} %copy-done.14, bf16[512,1024]{1,0:T(8,128)(2,1)S(1)} %copy-done.7, pred[]{:T(512)S(6)} %eq.7), kind=kOutput, calls=%fused_computation.7 | convolution fusion | flops 1083703296 | bytes 4194305 | tf_op jit(solution)/shard_map/tc,td->cd/dot_general | solution.py:43
  221.0 1.8 collective-permute-start.13
  223.0 3.6 %collective-permute-done.11 = bf16[1024,128]{0,1:T(8,128)(2,1)S(1)} collective-permute-done((bf16[1024,128]{0,1:T(8,128)(2,1)S(1)}, bf16[1024,128]{0,1:T(8,128)(2,1)S(1)}, u32[]{:S(2)}, u32[]{:S(2)}) %collective-permute-start.11) | collective-permute-done | bytes 262176 | tf_op jit(solution)/shard_map/ppermute | solution.py:37
  226.6 9.4 %collective-permute-done.12 = bf16[1024,128]{0,1:T(8,128)(2,1)S(1)} collective-permute-done((bf16[1024,128]{0,1:T(8,128)(2,1)S(1)}, bf16[1024,128]{0,1:T(8,128)(2,1)S(1)}, u32[]{:S(2)}, u32[]{:S(2)}) %collective-permute-start.12) | collective-permute-done | bytes 262176 | tf_op jit(solution)/shard_map/ppermute | solution.py:37
  236.1 2.3 convolution_convert_fusion.1
  (53 shorter events, 1.4 us)
Async XLA Ops:
  0.6 1.6 copy-start
  2.2 22.7 %copy-start.11 = (bf16[256,512]{1,0:T(8,128)(2,1)S(1)}, bf16[256,512]{1,0:T(8,128)(2,1)}, u32[]{:S(2)}) copy-start(bf16[256,512]{1,0:T(8,128)(2,1)} %param.9) | copy-start | bytes 786436
  23.4 17.7 %collective-permute-start = (bf16[4,64,1024]{2,1,0:T(8,128)(2,1)S(1)}, bf16[4,64,1024]{2,1,0:T(8,128)(2,1)S(1)}, u32[]{:S(2)}, u32[]{:S(2)}) collective-permute-start(bf16[4,64,1024]{2,1,0:T(8,128)(2,1)S(1)} %all_to_all.30), channel_id=1, source_target_pairs={{0,2},{2,0},{1,3},{3,1},{4,6},{6,4},{5,7},{7,5},{8,10},{10,8},{9,1... | collective-permute-start | bytes 1572872 | tf_op jit(solution)/shard_map/ppermute | solution.py:10
  25.8 11.3 %all-to-all-start.2 = ((bf16[4,256,128]{1,2,0:T(8,128)(2,1)}), bf16[4,256,128]{1,2,0:T(8,128)(2,1)S(1)}, u32[]{:S(2)}, u32[]{:S(2)}) async-start(bf16[4,256,128]{1,2,0:T(8,128)(2,1)} %bitcast.84), calls=%async_computation.2 | async-start | bytes 524288 | tf_op jit(solution)/shard_map/all_to_all | solution.py:21
  37.1 10.9 %all-to-all-start.1 = ((bf16[4,256,128]{1,2,0:T(8,128)(2,1)}), bf16[4,256,128]{1,2,0:T(8,128)(2,1)}, u32[]{:S(2)}, u32[]{:S(2)}) async-start(bf16[4,256,128]{1,2,0:T(8,128)(2,1)} %bitcast.83), calls=%async_computation.1 | async-start | bytes 524288 | tf_op jit(solution)/shard_map/all_to_all | solution.py:21
  42.2 19.3 %collective-permute-start.1 = (bf16[2,4,64,1024]{3,2,0,1:T(8,128)(2,1)}, bf16[2,4,64,1024]{3,2,0,1:T(8,128)(2,1)}, u32[]{:S(2)}, u32[]{:S(2)}) collective-permute-start(bf16[2,4,64,1024]{3,2,0,1:T(8,128)(2,1)} %maximum_select_fusion.2), channel_id=1, source_target_pairs={{0,1},{1,0},{2,3},{3,2},{4,5},{5,4},{6,7},{7,6},{8,9},{9,8},{10,11... | collective-permute-start | bytes 3145736 | tf_op jit(solution)/shard_map/ppermute | solution.py:10
  48.0 19.2 %all-to-all-start.3 = ((bf16[4,256,128]{1,2,0:T(8,128)(2,1)}), bf16[4,256,128]{1,2,0:T(8,128)(2,1)}, u32[]{:S(2)}, u32[]{:S(2)}) async-start(bf16[4,256,128]{1,2,0:T(8,128)(2,1)} %bitcast.82), calls=%async_computation.3 | async-start | bytes 524288 | tf_op jit(solution)/shard_map/all_to_all | solution.py:21
  61.5 3.4 %copy-start.12 = (bf16[1024,512]{1,0:T(8,128)(2,1)S(1)}, bf16[1024,512]{1,0:T(8,128)(2,1)}, u32[]{:S(2)}) copy-start(bf16[1024,512]{1,0:T(8,128)(2,1)} %param.12) | copy-start | bytes 3145732
  63.5 1.4 copy-start.4
  67.2 42.4 %all-to-all-start.4 = ((bf16[4,1024,128]{1,2,0:T(8,128)(2,1)}), bf16[4,1024,128]{1,2,0:T(8,128)(2,1)S(1)}, u32[]{:S(2)}, u32[]{:S(2)}) async-start(bf16[4,1024,128]{1,2,0:T(8,128)(2,1)} %bitcast.80), calls=%async_computation.4 | async-start | bytes 2097152 | tf_op jit(solution)/shard_map/all_to_all | solution.py:28
  78.7 4.8 %copy-start.3 = (bf16[1024,2,64]{0,2,1:T(8,128)(2,1)S(1)}, bf16[1024,2,64]{0,2,1:T(8,128)(2,1)}, u32[]{:S(2)}) copy-start(bf16[1024,2,64]{0,2,1:T(8,128)(2,1)} %reshape_reshape.11) | copy-start | bytes 786436
  83.5 2.0 copy-start.1
  85.5 15.1 %collective-permute-start.2 = (bf16[1024,128]{0,1:T(8,128)(2,1)S(1)}, bf16[1024,128]{0,1:T(8,128)(2,1)}, u32[]{:S(2)}, u32[]{:S(2)}) collective-permute-start(bf16[1024,128]{0,1:T(8,128)(2,1)S(1)} %bitcast.61), channel_id=1, source_target_pairs={{0,4},{4,8},{8,12},{12,0},{1,5},{5,9},{9,13},{13,1},{2,6},{6,10},{... | collective-permute-start | bytes 786440 | tf_op jit(solution)/shard_map/ppermute | solution.py:37
  87.5 33.3 %collective-permute-start.3 = (bf16[1024,128]{0,1:T(8,128)(2,1)S(1)}, bf16[1024,128]{0,1:T(8,128)(2,1)}, u32[]{:S(2)}, u32[]{:S(2)}) collective-permute-start(bf16[1024,128]{0,1:T(8,128)(2,1)S(1)} %bitcast.62), channel_id=1, source_target_pairs={{0,8},{4,12},{8,0},{12,4},{1,9},{5,13},{9,1},{13,5},{2,10},{6,14},... | collective-permute-start | bytes 786440 | tf_op jit(solution)/shard_map/ppermute | solution.py:37
  89.8 34.7 %collective-permute-start.4 = (bf16[1024,128]{0,1:T(8,128)(2,1)S(1)}, bf16[1024,128]{0,1:T(8,128)(2,1)}, u32[]{:S(2)}, u32[]{:S(2)}) collective-permute-start(bf16[1024,128]{0,1:T(8,128)(2,1)S(1)} %bitcast.63), channel_id=1, source_target_pairs={{0,12},{4,0},{8,4},{12,8},{1,13},{5,1},{9,5},{13,9},{2,14},{6,2},{... | collective-permute-start | bytes 786440 | tf_op jit(solution)/shard_map/ppermute | solution.py:37
  113.6 27.1 %copy-start.9 = (bf16[512,1024]{1,0:T(8,128)(2,1)S(1)}, bf16[512,1024]{1,0:T(8,128)(2,1)}, u32[]{:S(2)}) copy-start(bf16[512,1024]{1,0:T(8,128)(2,1)} %param.11) | copy-start | bytes 3145732
  113.6 15.6 %collective-permute-start.5 = (bf16[1024,128]{0,1:T(8,128)(2,1)S(1)}, bf16[1024,128]{0,1:T(8,128)(2,1)S(1)}, u32[]{:S(2)}, u32[]{:S(2)}) collective-permute-start(bf16[1024,128]{0,1:T(8,128)(2,1)S(1)} %bitcast.65), channel_id=1, source_target_pairs={{0,4},{4,8},{8,12},{12,0},{1,5},{5,9},{9,13},{13,1},{2,6},{6,10},{... | collective-permute-start | bytes 786440 | tf_op jit(solution)/shard_map/ppermute | solution.py:37
  122.4 15.2 %collective-permute-start.6 = (bf16[1024,128]{0,1:T(8,128)(2,1)S(1)}, bf16[1024,128]{0,1:T(8,128)(2,1)S(1)}, u32[]{:S(2)}, u32[]{:S(2)}) collective-permute-start(bf16[1024,128]{0,1:T(8,128)(2,1)S(1)} %bitcast.66), channel_id=1, source_target_pairs={{0,8},{4,12},{8,0},{12,4},{1,9},{5,13},{9,1},{13,5},{2,10},{6,14},... | collective-permute-start | bytes 786440 | tf_op jit(solution)/shard_map/ppermute | solution.py:37
  126.2 14.4 %collective-permute-start.7 = (bf16[1024,128]{0,1:T(8,128)(2,1)S(1)}, bf16[1024,128]{0,1:T(8,128)(2,1)S(1)}, u32[]{:S(2)}, u32[]{:S(2)}) collective-permute-start(bf16[1024,128]{0,1:T(8,128)(2,1)S(1)} %bitcast.67), channel_id=1, source_target_pairs={{0,12},{4,0},{8,4},{12,8},{1,13},{5,1},{9,5},{13,9},{2,14},{6,2},{... | collective-permute-start | bytes 786440 | tf_op jit(solution)/shard_map/ppermute | solution.py:37
  140.7 1.3 copy-start.8
  144.6 1.4 copy-start.2
  146.0 2.9 %collective-permute-start.8 = (bf16[512,1024]{1,0:T(8,128)(2,1)S(1)}, bf16[512,1024]{1,0:T(8,128)(2,1)}, u32[]{:S(2)}, u32[]{:S(2)}) collective-permute-start(bf16[512,1024]{1,0:T(8,128)(2,1)S(1)} %constant_dynamic-slice_fusion), channel_id=1, source_target_pairs={{0,1},{1,0},{2,3},{3,2},{4,5},{5,4},{6,7},{7,6},{8,9},{9,8},{10,11... | collective-permute-start | bytes 3145736 | tf_op jit(solution)/shard_map/ppermute | solution.py:10
  150.8 28.4 %copy-start.10 = (bf16[512,1024]{1,0:T(8,128)(2,1)S(1)}, bf16[512,1024]{1,0:T(8,128)(2,1)}, u32[]{:S(2)}) copy-start(bf16[512,1024]{1,0:T(8,128)(2,1)} %param.11) | copy-start | bytes 3145732
  150.8 25.3 %collective-permute-start.9 = (bf16[512,1024]{1,0:T(8,128)(2,1)S(1)}, bf16[512,1024]{1,0:T(8,128)(2,1)S(1)}, u32[]{:S(2)}, u32[]{:S(2)}) collective-permute-start(bf16[512,1024]{1,0:T(8,128)(2,1)S(1)} %add_convert_fusion.2), channel_id=1, source_target_pairs={{0,2},{2,0},{1,3},{3,1},{4,6},{6,4},{5,7},{7,5},{8,10},{10,8},{9,1... | collective-permute-start | bytes 3145736 | tf_op jit(solution)/shard_map/ppermute | solution.py:10
  176.5 4.1 %copy-start.6 = (bf16[512,1024]{1,0:T(8,128)(2,1)}, bf16[512,1024]{1,0:T(8,128)(2,1)S(1)}, u32[]{:S(2)}) copy-start(bf16[512,1024]{1,0:T(8,128)(2,1)S(1)} %add_convert_fusion.1) | copy-start | bytes 3145732
  176.5 2.7 %collective-permute-start.10 = (bf16[512,1024]{1,0:T(8,128)(2,1)S(1)}, bf16[512,1024]{1,0:T(8,128)(2,1)S(1)}, u32[]{:S(2)}, u32[]{:S(2)}) collective-permute-start(bf16[512,1024]{1,0:T(8,128)(2,1)S(1)} %add_convert_fusion.1), channel_id=1, source_target_pairs={{0,1},{1,0},{2,3},{3,2},{4,5},{5,4},{6,7},{7,6},{8,9},{9,8},{10,11... | collective-permute-start | bytes 3145736 | tf_op jit(solution)/shard_map/ppermute | solution.py:10
  179.2 1.3 copy-start.13
  211.7 5.8 %copy-start.7 = (bf16[512,1024]{1,0:T(8,128)(2,1)S(1)}, bf16[512,1024]{1,0:T(8,128)(2,1)}, u32[]{:S(2)}) copy-start(bf16[512,1024]{1,0:T(8,128)(2,1)} %copy-done.6) | copy-start | bytes 3145732
  211.7 5.8 %copy-start.14 = (bf16[512,1024]{1,0:T(8,128)(2,1)S(1)}, bf16[512,1024]{1,0:T(8,128)(2,1)}, u32[]{:S(2)}) copy-start(bf16[512,1024]{1,0:T(8,128)(2,1)} %copy-done.13) | copy-start | bytes 3145732
  215.4 11.1 %collective-permute-start.11 = (bf16[1024,128]{0,1:T(8,128)(2,1)S(1)}, bf16[1024,128]{0,1:T(8,128)(2,1)S(1)}, u32[]{:S(2)}, u32[]{:S(2)}) collective-permute-start(bf16[1024,128]{0,1:T(8,128)(2,1)S(1)} %bitcast.76), channel_id=1, source_target_pairs={{0,4},{4,8},{8,12},{12,0},{1,5},{5,9},{9,13},{13,1},{2,6},{6,10},{... | collective-permute-start | bytes 786440 | tf_op jit(solution)/shard_map/ppermute | solution.py:37
  215.7 20.3 %collective-permute-start.12 = (bf16[1024,128]{0,1:T(8,128)(2,1)S(1)}, bf16[1024,128]{0,1:T(8,128)(2,1)S(1)}, u32[]{:S(2)}, u32[]{:S(2)}) collective-permute-start(bf16[1024,128]{0,1:T(8,128)(2,1)S(1)} %bitcast.77), channel_id=1, source_target_pairs={{0,8},{4,12},{8,0},{12,4},{1,9},{5,13},{9,1},{13,5},{2,10},{6,14},... | collective-permute-start | bytes 786440 | tf_op jit(solution)/shard_map/ppermute | solution.py:37
  221.0 15.0 %copy-start.5 = (bf16[2,2,4,64,1024]{4,3,0,1,2:T(8,128)(2,1)S(1)}, bf16[2,2,4,64,1024]{4,3,0,1,2:T(8,128)(2,1)}, u32[]{:S(2)}) copy-start(bf16[2,2,4,64,1024]{4,3,0,1,2:T(8,128)(2,1)} %copy-done.4) | copy-start | bytes 6291460
  221.0 15.0 %collective-permute-start.13 = (bf16[1024,128]{0,1:T(8,128)(2,1)S(1)}, bf16[1024,128]{0,1:T(8,128)(2,1)S(1)}, u32[]{:S(2)}, u32[]{:S(2)}) collective-permute-start(bf16[1024,128]{0,1:T(8,128)(2,1)S(1)} %bitcast.78), channel_id=1, source_target_pairs={{0,12},{4,0},{8,4},{12,8},{1,13},{5,1},{9,5},{13,9},{2,14},{6,2},{... | collective-permute-start | bytes 786440 | tf_op jit(solution)/shard_map/ppermute | solution.py:37

commit v2 on v0

--- a/solution.py
+++ b/solution.py
@@ -1,12 +1,355 @@
+from functools import partial
+
 import jax
 import jax.numpy as jnp
 from jax import lax
+from jax.experimental import pallas as pl
+from jax.experimental.pallas import tpu as pltpu
 from jax.sharding import PartitionSpec as P
 
 DH = 64
 
 
-def body(normed, query_proj, key_proj, value_proj, out_weight, value_probe, out_probe):
+VMEM = pl.BlockSpec(memory_space=pltpu.VMEM)
+HBM = pl.BlockSpec(memory_space=pltpu.HBM)
+ANY = pl.BlockSpec(memory_space=pl.ANY)
+
+
+class Chain:
+    def __init__(self):
+        self.last = None
+
+    def __call__(self, kernel, outs, ins, scratch=(), in_specs=None, first=(), mib=1):
+        specs = in_specs or [VMEM] * len(ins)
+        out_specs = [HBM] * len(outs) if in_specs and HBM in in_specs and VMEM not in in_specs else [VMEM] * len(outs)
+        count = len(ins)
+        if self.last is not None:
+            first = [*first, self.last]
+        ins, specs = [*ins, *first], [*specs, *[ANY] * len(first)]
+
+        def body(*refs):
+            kernel(*refs[:count], *refs[len(ins) :])
+
+        results = pl.pallas_call(
+            body,
+            out_shape=outs,
+            in_specs=specs,
+            out_specs=out_specs,
+            scratch_shapes=list(scratch),
+            compiler_params=pltpu.CompilerParams(vmem_limit_bytes=44 * 2**20),
+            cost_estimate=pl.CostEstimate(flops=1, bytes_accessed=mib * 2**20, transcendentals=0),
+            name=getattr(kernel, "func", kernel).__name__,
+        )(*ins)
+        self.last = results[0]
+        return results
+
+
+def bf(*shape):
+    return jax.ShapeDtypeStruct(shape, jnp.bfloat16)
+
+
+def dot(a, b, ca=1, cb=0):
+    return lax.dot_general(a, b, (((ca,), (cb,)), ((), ())), preferred_element_type=jnp.float32)
+
+
+def at(index, size):
+    return pl.ds(pl.multiple_of(index * size, size), size)
+
+
+def ahead(x, k):
+    n = lax.axis_size("seq")
+    return lax.ppermute(x, "seq", [(i, (i + k) % n) for i in range(n)])
+
+
+def swap(x, axis):
+    return lax.ppermute(x, axis, [(0, 1), (1, 0)])
+
+
+def after(x, *first):
+    return lax.optimization_barrier((x, *first))[0]
+
+
+def pack(*refs):
+    out = refs[-1]
+    for j, piece in enumerate(refs[:-1]):
+        out[j] = piece[...]
+
+
+def tangent_term(n, own, packed, peer, probe, feats, *refs):
+    outs, whole = refs[:n], refs[n]
+    me, head, rep = lax.axis_index("seq"), lax.axis_index("head"), lax.axis_index("rep")
+    tok = own.shape[0]
+    part = packed.shape[1]
+    cols = outs[0].shape[1]
+    for k in range(n):
+        block = lax.rem(me - k + n, n)
+        if k == 0:
+            feats[at(block, tok), :] = own[...]
+        else:
+            for rows, core in ((packed, rep), (peer, 1 - rep)):
+                for row, side in ((k - 1, head), (n - 2 + k, 1 - head)):
+                    start = block * tok + (core * 2 + side) * part
+                    feats[pl.ds(pl.multiple_of(start, part), part), :] = rows[row]
+        whole[at(block, tok), :] = dot(feats[at(block, tok), :], probe[...]).astype(jnp.bfloat16)
+    for k in range(n):
+        outs[k][...] = whole[:, at(lax.rem(me + k, n), cols)]
+
+
+def flip(feats, out):
+    out[...] = feats[...].T
+
+
+def keep_heads(parts):
+    return jnp.concatenate([part[h * DH : (h + 1) * DH] for h, part in enumerate(parts)], axis=0)
+
+
+def attend(n, *refs):
+    own, pieces, (probs, attended, home, away, *all3) = refs[:3], refs[3 : n + 2], refs[n + 2 :]
+    q_all, k_all, v_all = all3
+    me = lax.axis_index("seq")
+    tok, cols = pieces[0].shape[1:]
+    for j in range(3):
+        all3[j][at(me, tok), :] = own[j][:, at(me, cols)]
+        for k in range(1, n):
+            all3[j][at(lax.rem(me - k + n, n), tok), :] = pieces[k - 1][j]
+    heads = cols // DH
+    v_flip = v_all[...].T
+    lane = lax.broadcasted_iota(jnp.int32, (tok, cols), 1) // DH
+
+    @pl.loop(0, n)
+    def _(c):
+        rows = at(c, tok)
+        parts = []
+        for h in range(heads):
+            query = jnp.where(lane == h, q_all[rows, :], 0)
+            scores = dot(k_all[...], query, 1, 1)
+            exps = jnp.exp(scores - jnp.max(scores, axis=0, keepdims=True))
+            prob = (exps * (1.0 / jnp.sum(exps, axis=0, keepdims=True))).astype(jnp.bfloat16)
+            probs[h, :, rows] = prob
+            parts.append(dot(v_flip, prob))
+        attended[rows, :] = keep_heads(parts).T.astype(jnp.bfloat16)
+
+    halves(attended, home, away)
+
+
+def halves(rows, home, away):
+    head = lax.axis_index("head")
+    half = home.shape[0]
+    home[...] = rows[at(head, half), :]
+    away[...] = rows[at(1 - head, half), :]
+
+
+def attend_tan(n, *refs):
+    terms, probs, (home, away, held, result, sems) = refs[:n], refs[n], refs[n + 1 :]
+    heads = probs.shape[0]
+    copies = [pltpu.make_async_copy(probs.at[h], held.at[h], sems.at[h]) for h in range(heads)]
+    for copy in copies:
+        copy.start()
+    total = terms[0][...].astype(jnp.float32)
+    for term in terms[1:]:
+        total = total + term[...].astype(jnp.float32)
+    flipped = total.T.astype(jnp.bfloat16)
+    parts = []
+    for h in range(heads):
+        copies[h].wait()
+        parts.append(dot(flipped, held[h]))
+    result[...] = keep_heads(parts).T.astype(jnp.bfloat16)
+    halves(result, home, away)
+
+
+def add(one, two, out):
+    out[...] = (one[...].astype(jnp.float32) + two[...].astype(jnp.float32)).astype(jnp.bfloat16)
+
+
+def join(home, other, out):
+    cols = home.shape[1]
+    out[:, :cols] = home[...]
+    out[:, cols:] = other[...]
+
+
+def both_columns(n, pieces, lhs):
+    me = lax.axis_index("seq")
+    cols = pieces[0].shape[1] // 2
+    for k in range(n):
+        where = at(lax.rem(me - k + n, n), cols)
+        for d in range(2):
+            lhs[d, :, where] = pieces[k][:, d * cols : (d + 1) * cols]
+
+
+def out_term(n, *refs):
+    pieces, (probe, other, total, theirs, lhs) = refs[:n], refs[n:]
+    both_columns(n, pieces, lhs)
+    total[...] = dot(lhs[0], probe[...])
+    total[...] += dot(lhs[1], other[...])
+    theirs[...] = lhs[1]
+
+
+def out_sum(n, *refs):
+    base, pieces, weight, other, out, lhs = refs[0], refs[1 : n + 1], refs[n + 1], refs[n + 2], refs[n + 3], refs[n + 4]
+    both_columns(n, pieces, lhs)
+    total = base[...] + dot(lhs[0], weight[...])
+    out[...] = (total + dot(lhs[1], other[...])).astype(jnp.bfloat16)
+
+
+def grad_term(n, mine, other_core, weight, other, tangent_out, share, *refs):
+    outs, grad = refs[:n], refs[n]
+    me = lax.axis_index("seq")
+    cols = outs[0].shape[1] // 2
+    tangent_out[...] = (mine[...].astype(jnp.float32) + other_core[...].astype(jnp.float32)).astype(jnp.bfloat16)
+    share[...] = tangent_out[at(lax.axis_index("rep"), share.shape[0]), :]
+    for d, rows in enumerate((weight, other)):
+        grad[d] = dot(tangent_out[...], rows[...], 1, 1).astype(jnp.bfloat16)
+        for k in range(n):
+            outs[k][:, d * cols : (d + 1) * cols] = grad[d, :, at(lax.rem(me + k, n), cols)]
+
+
+def add_grad(n, *refs):
+    terms, home, away = refs[:n], refs[n], refs[n + 1]
+    total = terms[0][...].astype(jnp.float32)
+    for term in terms[1:]:
+        total = total + term[...].astype(jnp.float32)
+    cols = home.shape[1]
+    home[...] = total[:, :cols].astype(jnp.bfloat16)
+    away[...] = total[:, cols:].astype(jnp.bfloat16)
+
+
+def key_grad(mine, theirs, probs, out, grad, held, sems):
+    heads, tokens, _ = probs.shape
+    half, cols = mine.shape
+    parts = held.shape[0]
+    rows = tokens // parts
+    copies = [pltpu.make_async_copy(probs.at[:, pl.ds(c * rows, rows)], held.at[c], sems.at[c]) for c in range(parts)]
+    for copy in copies:
+        copy.start()
+    head = lax.axis_index("head")
+    grad[at(head, half), :] = mine[...]
+    grad[at(1 - head, half), :] = theirs[...]
+    lane = lax.broadcasted_iota(jnp.int32, (rows, cols), 1) // DH
+    for c in range(parts):
+        copies[c].wait()
+        value = dot(held[c, 0], grad[...])
+        for h in range(1, heads):
+            value = jnp.where(lane == h, dot(held[c, h], grad[...]), value)
+        out[pl.ds(c * rows, rows), :] = value.astype(jnp.bfloat16)
+
+
+def value_product(n, *refs):
+    flipped, blocks, out, rhs = refs[0], refs[1 : n + 1], refs[n + 1], refs[n + 2]
+    me = lax.axis_index("seq")
+    cols = blocks[0].shape[1]
+    for k in range(n):
+        rhs[:, at(lax.rem(me - k + n, n), cols)] = blocks[k][...]
+    out[...] = dot(flipped[...], rhs[...]).astype(jnp.bfloat16)
+
+
+def out_product(n, *refs):
+    pieces, (theirs, mine, one, two, out, other) = refs[:n], refs[n:]
+    me, rep = lax.axis_index("seq"), lax.axis_index("rep")
+    cols = pieces[0].shape[1] // 2
+    other[at(rep, one.shape[0]), :] = one[...]
+    other[at(1 - rep, one.shape[0]), :] = two[...]
+    for k in range(n):
+        where = at(lax.rem(me - k + n, n), cols)
+        total = dot(pieces[k][:, :cols].T, mine[...])
+        out[where, :] = (total + dot(theirs[:, where].T, other[...])).astype(jnp.bfloat16)
+
+
+def by_heads(normed, query_proj, key_proj, value_proj, out_weight, value_probe, out_probe):
+    n = lax.axis_size("seq")
+    me, head, rep = lax.axis_index("seq"), lax.axis_index("head"), lax.axis_index("rep")
+    tok, width = normed.shape
+    block = query_proj.shape[1]
+    slab, cols, tokens = width // n, block // n, tok * n
+    half, heads = tokens // 2, block // n // DH
+    call = Chain()
+    part = partial
+    dma = pltpu.SemaphoreType.DMA
+    f32 = jnp.float32
+
+    def held(*shape):
+        return pltpu.VMEM(shape, jnp.bfloat16)
+
+    def gathered(x):
+        pieces = [x] + [None] * (n - 1)
+        for k in range(1, (n - 1) // 2 + 1):
+            pieces[k] = ahead(pieces[k - 1], 1)
+        for k in range(1, n // 2 + 1):
+            pieces[n - k] = ahead(pieces[(n - k + 1) % n], n - 1)
+        return pieces
+
+    def summed(terms):
+        sums = [terms[0]]
+        for step, far in ((1, n // 2), (-1, (n - 1) // 2)):
+            total = ahead(terms[step * far], step)
+            for k in range(far - 1, 0, -1):
+                (total,) = call(add, [bf(*total.shape)], [total, terms[step * k]])
+                total = ahead(total, step)
+            sums.append(total)
+        return sums
+
+    quarter = tok // 4
+    start = (rep * 2 + head) * quarter
+    got = [
+        ahead(lax.dynamic_slice(normed, (start, lax.rem(me + k, n) * slab), (quarter, slab)), k) for k in range(1, n)]
+    own = lax.dynamic_slice(normed, (0, me * slab), (tok, slab))
+    proj = (query_proj, key_proj, value_proj)
+    qkv = []
+    for k in range(1, n):
+        piece = jnp.stack([lax.dynamic_slice(x, (0, lax.rem(me + k, n) * cols), (tok, cols)) for x in proj])
+        qkv.append(ahead(piece, k))
+    other = [swap(x, "head") for x in got]
+    (packed,) = call(pack, [bf(2 * (n - 1), quarter, slab)], [*got, *other], first=qkv)
+    feats, *terms = call(
+        part(tangent_term, n), [bf(tokens, slab)] + [bf(tokens, cols)] * n,
+        [own, packed, swap(packed, "rep"), value_probe], scratch=[held(tokens, block)])
+    probs, _, home, away = call(
+        part(attend, n), [bf(heads, tokens, tokens), bf(tokens, cols)] + [bf(half, cols)] * 2, [*proj, *qkv],
+        scratch=[held(tokens, cols)] * 3, mib=32)
+    away = swap(away, "head")
+    tangent = summed(terms)
+    other_probe = swap(after(out_probe, feats), "head")
+    tan, tan_away = call(
+        part(attend_tan, 3), [bf(half, cols)] * 2, [*tangent, probs],
+        scratch=[held(heads, tokens, tokens), held(tokens, cols), dma((heads,))], in_specs=[VMEM] * 3 + [ANY])
+    (att,) = call(join, [bf(half, 2 * cols)], [home, away])
+    att = gathered(att)
+    (tan,) = call(join, [bf(half, 2 * cols)], [tan, swap(after(tan_away, att[0]), "head")], first=[att[1], att[-1]])
+    other_weight = swap(after(out_weight, tan), "head")
+    tan = gathered(tan)
+    base, theirs = call(
+        part(out_term, n), [jax.ShapeDtypeStruct((half, slab), f32), bf(half, block)], [*att, out_probe, other_probe],
+        scratch=[held(2, half, block)])
+    (mine,) = call(
+        part(out_sum, n), [bf(half, slab)], [base, *tan, out_weight, other_weight], scratch=[held(2, half, block)])
+    tangent_out, share, *grads = call(
+        part(grad_term, n), [bf(half, slab), bf(half // 2, slab)] + [bf(half, 2 * cols)] * n,
+        [mine, swap(mine, "rep"), out_weight, other_weight],
+        scratch=[held(2, half, block)])
+    home, away = call(part(add_grad, 3), [bf(half, cols)] * 2, summed(grads))
+    (value_grad,) = call(
+        key_grad, [bf(tokens, cols)], [home, swap(away, "head"), probs],
+        scratch=[held(tokens, cols), held(4, heads, tokens // 4, tokens), dma((4,))], in_specs=[VMEM] * 2 + [ANY])
+    value_grad = gathered(value_grad)
+    share = swap(share, "head")
+    (out_curv,) = call(
+        part(out_product, n), [bf(block, slab)], [*att, swap(theirs, "head"), tangent_out, share, swap(share, "rep")],
+        scratch=[held(half, slab)])
+    (flipped,) = call(flip, [bf(slab, tokens)], [feats])
+    (value_curv,) = call(
+        part(value_product, n), [bf(slab, block)], [flipped, *value_grad], scratch=[held(tokens, block)])
+    return value_curv, out_curv
+
+
+def body(*args):
+    tok, cols = args[1].shape
+    n = lax.axis_size("seq")
+    even = cols % (n * 128) == 0 and tok % 64 == 0 and tok * n % 64 == 0
+    if even and lax.axis_size("head") == 2 and lax.axis_size("rep") == 2:
+        return by_heads(*args)
+    return by_tokens(*args)
+
+
+def by_tokens(normed, query_proj, key_proj, value_proj, out_weight, value_probe, out_probe):
     tok_rows = normed.shape[0]
     col_count = query_proj.shape[1]
     local_heads = col_count // DH

time: 603 us -> 171 us (0.28)
  waiting for transfers between devices: 533 us -> 92.3 us
  starting transfers between devices: 0.58 us -> 48.9 us
  matrix products: 44.1 us -> 0 us
  Pallas kernels: 0 us -> 23.5 us
  between operations: 14.3 us -> 0.9 us
    all_gather x6 -> x0, waiting for transfers between devices: 304 us -> none  [the longest x1 83.6 us: body(): lax.all_gather(value_probe, 'seq', axis=0, tiled=True)]
    reduce_scatter x3 -> x0, waiting for transfers between devices: 176 us -> none  [the longest x1 77.8 us: body(): lax.psum_scatter(out_term.astype(jnp.bfloat16), 'seq', scatter_dimension=...]
    ppermute x0 -> x34, waiting for transfers between devices: none -> 92.3 us  [the longest x21 63 us: ahead(): return lax.ppermute(x, 'seq', [(i, (i + k) % n) for i in range(n)])]
    psum x1 -> x0, waiting for transfers between devices: 50 us -> none  [body(): tangent_out = lax.psum(partial_out.astype(jnp.bfloat16), ('head', 'rep'))]
    ppermute x0 -> x34, starting transfers between devices: none -> 48.9 us  [the longest x21 36.6 us: ahead(): return lax.ppermute(x, 'seq', [(i, (i + k) % n) for i in range(n)])]
    dot_general x10 -> x0, matrix products: 44.1 us -> none  [the longest x1 6.11 us: body(): jnp.dot(attended, probe_full, preferred_element_type=jnp.float32)]
    pallas_call x0 -> x16, Pallas kernels: none -> 23.5 us  [__call__(): pl.pallas_call(body, out_shape=outs, in_specs=specs, out_specs=out_specs,...]
  transfers between devices with their start and end apart: 10 -> 34, of which waited for: 10 -> 21; matrix products, arithmetic and copies ran while one was open for 5% -> 2% of each run, Pallas kernels for 0% -> 10%
where the time goes in v2:
time: 171 us
  waiting for transfers between devices  92.3 us (54%)
  starting transfers between devices  48.9 us (29%)
  Pallas kernels  23.5 us (14%)
  local copies, waits for them, and re-layouts  5.37 us (3%)
    ppermute x21, waiting for transfers between devices, ahead(): return lax.ppermute(x, 'seq', [(i, (i + k) % n) for i in range(n)])  63 us
    ppermute x21, starting transfers between devices, ahead(): return lax.ppermute(x, 'seq', [(i, (i + k) % n) for i in range(n)])  36.6 us
    ppermute x13, waiting for transfers between devices, swap(): return lax.ppermute(x, axis, [(0, 1), (1, 0)])  29.3 us
    pallas_call x16, Pallas kernels, __call__(): pl.pallas_call(body, out_shape=outs, in_specs=specs, out_specs=out_specs,...  23.5 us
    ppermute x13, starting transfers between devices, swap(): return lax.ppermute(x, axis, [(0, 1), (1, 0)])  12.4 us
  transfers between devices with their start and end apart: 34, of which 21 were waited for; matrix products, arithmetic and copies ran while one was open for 2% of the time, Pallas kernels for 10%

profile of v2, /device:TPU:0, one launch (start us, length us, event | category | flops | bytes accessed | tf_op | source)
XLA Modules:
  0.0 171.0 jit_solution(18108324186025344798)
XLA Ops:
  0.7 1.1 fusion
  1.7 5.1 %collective-permute-start.2 = (bf16[64,1024]{1,0:T(8,128)(2,1)S(1)}, bf16[64,1024]{1,0:T(8,128)(2,1)S(1)}, u32[]{:S(2)}, u32[]{:S(2)}) collective-permute-start(bf16[64,1024]{1,0:T(8,128)(2,1)S(1)} %get-tuple-element.48), channel_id=1, source_target_pairs={{0,12},{4,0},{8,4},{12,8},{1,13},{5,1},{9,5},{13,9},{2,14},{6,2},{... | collective-permute-start | bytes 393224 | tf_op jit(solution)/shard_map/ppermute | solution.py:61
  6.8 1.0 collective-permute-start.1
  7.8 0.9 dynamic-slice_bitcast_fusion.2
  8.8 1.0 dynamic-slice_bitcast_fusion
  9.9 3.4 %collective-permute-start.6 = (bf16[3,256,128]{2,1,0:T(8,128)(2,1)S(1)}, bf16[3,256,128]{2,1,0:T(8,128)(2,1)S(1)}, u32[]{:S(2)}, u32[]{:S(2)}) collective-permute-start(bf16[3,256,128]{2,1,0:T(8,128)(2,1)S(1)} %pad_maximum_fusion), channel_id=1, source_target_pairs={{0,4},{4,8},{8,12},{12,0},{1,5},{5,9},{9,13},{13,1},{2,6},{6,10},{... | collective-permute-start | bytes 589832 | tf_op jit(solution)/shard_map/ppermute | solution.py:61
  13.4 2.4 %collective-permute-start.8 = (bf16[3,256,128]{2,1,0:T(8,128)(2,1)S(1)}, bf16[3,256,128]{2,1,0:T(8,128)(2,1)S(1)}, u32[]{:S(2)}, u32[]{:S(2)}) collective-permute-start(bf16[3,256,128]{2,1,0:T(8,128)(2,1)S(1)} %pad_maximum_fusion.2), channel_id=1, source_target_pairs={{0,12},{4,0},{8,4},{12,8},{1,13},{5,1},{9,5},{13,9},{2,14},{6,2},{... | collective-permute-start | bytes 589832 | tf_op jit(solution)/shard_map/ppermute | solution.py:61
  15.9 1.5 collective-permute-start.5
  17.4 10.4 %collective-permute-done.1.refs_1_ = bf16[64,1024]{1,0:T(8,128)(2,1)S(1)} collective-permute-done((bf16[64,1024]{1,0:T(8,128)(2,1)S(1)}, bf16[64,1024]{1,0:T(8,128)(2,1)S(1)}, u32[]{:S(2)}, u32[]{:S(2)}) %collective-permute-start.1) | collective-permute-done | bytes 131104 | tf_op jit(solution)/shard_map/ppermute | solution.py:61
  27.8 1.5 collective-permute-start.3
  29.3 0.5 collective-permute-start.4
  29.8 2.2 %collective-permute-done.7.refs_7_.refs_4_ = bf16[3,256,128]{2,1,0:T(8,128)(2,1)S(1)} collective-permute-done((bf16[3,256,128]{2,1,0:T(8,128)(2,1)S(1)}, bf16[3,256,128]{2,1,0:T(8,128)(2,1)S(1)}, u32[]{:S(2)}, u32[]{:S(2)}) %collective-permute-start.7) | collective-permute-done | bytes 196640 | tf_op jit(solution)/shard_map/ppermute | solution.py:61
  32.0 0.7 collective-permute-done.3.refs_3_
  32.8 1.5 collective-permute-done.4.refs_4_
  34.4 1.1 constant_dynamic-slice_fusion.refs_0_
  35.5 1.1 collective-permute-done.9.refs_2_
  36.7 1.4 tangent_term.1
  38.1 1.8 %collective-permute-start.11 = (bf16[1024,128]{1,0:T(8,128)(2,1)S(1)}, bf16[1024,128]{1,0:T(8,128)(2,1)S(1)}, u32[]{:S(2)}, u32[]{:S(2)}) collective-permute-start(bf16[1024,128]{1,0:T(8,128)(2,1)S(1)} %get-tuple-element.29), channel_id=1, source_target_pairs={{0,4},{4,8},{8,12},{12,0},{1,5},{5,9},{9,13},{13,1},{2,6},{6,10},{... | collective-permute-start | bytes 786440 | tf_op jit(solution)/shard_map/ppermute | solution.py:61
  39.9 2.1 %collective-permute-start.13 = (bf16[1024,128]{1,0:T(8,128)(2,1)S(1)}, bf16[1024,128]{1,0:T(8,128)(2,1)S(1)}, u32[]{:S(2)}, u32[]{:S(2)}) collective-permute-start(bf16[1024,128]{1,0:T(8,128)(2,1)S(1)} %get-tuple-element.32), channel_id=1, source_target_pairs={{0,12},{4,0},{8,4},{12,8},{1,13},{5,1},{9,5},{13,9},{2,14},{6,2},{... | collective-permute-start | bytes 786440 | tf_op jit(solution)/shard_map/ppermute | solution.py:61
  42.0 8.5 %attend.1 = (bf16[2,1024,1024]{2,1,0:T(8,128)(2,1)S(1)}, bf16[1024,128]{1,0:T(8,128)(2,1)}, bf16[512,128]{1,0:T(8,128)(2,1)S(1)}, bf16[512,128]{1,0:T(8,128)(2,1)S(1)}) custom-call(bf16[256,512]{1,0:T(8,128)(2,1)S(1)} %copy-done.4, bf16[256,512]{1,0:T(8,128)(2,1)S(1)} %copy-done.6, bf16[256,512]{1,0:T(8,128)(2,1)S(1)} %copy-done.5, ...), custom_call_target="tpu_custom_call" | custom-call | flops 1 | bytes 33554432 | tf_op jit(solution)/shard_map/attend/pallas_call | solution.py:33
  50.5 3.5 %collective-permute-start.12 = (bf16[1024,128]{1,0:T(8,128)(2,1)S(1)}, bf16[1024,128]{1,0:T(8,128)(2,1)S(1)}, u32[]{:S(2)}, u32[]{:S(2)}) collective-permute-start(bf16[1024,128]{1,0:T(8,128)(2,1)S(1)} %add.67.refs_4_), channel_id=1, source_target_pairs={{0,4},{4,8},{8,12},{12,0},{1,5},{5,9},{9,13},{13,1},{2,6},{6,10},{... | collective-permute-start | bytes 786440 | tf_op jit(solution)/shard_map/ppermute | solution.py:61
  54.0 1.5 collective-permute-start.10
  55.5 4.6 %collective-permute-done.12.refs_1_ = bf16[1024,128]{1,0:T(8,128)(2,1)S(1)} collective-permute-done((bf16[1024,128]{1,0:T(8,128)(2,1)S(1)}, bf16[1024,128]{1,0:T(8,128)(2,1)S(1)}, u32[]{:S(2)}, u32[]{:S(2)}) %collective-permute-start.12) | collective-permute-done | bytes 262176 | tf_op jit(solution)/shard_map/ppermute | solution.py:61
  60.2 1.5 attend_tan.1
  61.7 2.8 %collective-permute-start.15 = (bf16[512,256]{1,0:T(8,128)(2,1)S(1)}, bf16[512,256]{1,0:T(8,128)(2,1)S(1)}, u32[]{:S(2)}, u32[]{:S(2)}) collective-permute-start(bf16[512,256]{1,0:T(8,128)(2,1)S(1)} %join.2.refs_4_.refs_0_), channel_id=1, source_target_pairs={{0,12},{4,0},{8,4},{12,8},{1,13},{5,1},{9,5},{13,9},{2,14},{6,2},{... | collective-permute-start | bytes 786440 | tf_op jit(solution)/shard_map/ppermute | solution.py:61
  64.5 1.5 collective-permute-start.18
  66.0 0.5 collective-permute-start.17
  66.6 4.4 %collective-permute-done.18.refs_1_ = bf16[512,128]{1,0:T(8,128)(2,1)S(1)} collective-permute-done((bf16[512,128]{1,0:T(8,128)(2,1)S(1)}, bf16[512,128]{1,0:T(8,128)(2,1)S(1)}, u32[]{:S(2)}, u32[]{:S(2)}) %collective-permute-start.18) | collective-permute-done | bytes 131104 | tf_op jit(solution)/shard_map/ppermute | solution.py:65
  71.0 0.3 collective-permute-done.15.refs_3_
  71.3 4.9 %collective-permute-done.14.refs_2_.refs_1_ = bf16[512,256]{1,0:T(8,128)(2,1)S(1)} collective-permute-done((bf16[512,256]{1,0:T(8,128)(2,1)S(1)}, bf16[512,256]{1,0:T(8,128)(2,1)S(1)}, u32[]{:S(2)}, u32[]{:S(2)}) %collective-permute-start.14) | collective-permute-done | bytes 262176 | tf_op jit(solution)/shard_map/ppermute | solution.py:61
  76.3 1.6 collective-permute-start.23
  77.9 1.7 %collective-permute-start.21 = (bf16[512,256]{1,0:T(8,128)(2,1)S(1)}, bf16[512,256]{1,0:T(8,128)(2,1)S(1)}, u32[]{:S(2)}, u32[]{:S(2)}) collective-permute-start(bf16[512,256]{1,0:T(8,128)(2,1)S(1)} %join.3.refs_6_.refs_1_), channel_id=1, source_target_pairs={{0,12},{4,0},{8,4},{12,8},{1,13},{5,1},{9,5},{13,9},{2,14},{6,2},{... | collective-permute-start | bytes 786440 | tf_op jit(solution)/shard_map/ppermute | solution.py:61
  79.6 0.3 collective-permute-start.16
  80.0 1.7 collective-permute-start.20
  81.6 5.3 %collective-permute-done.21.refs_4_ = bf16[512,256]{1,0:T(8,128)(2,1)S(1)} collective-permute-done((bf16[512,256]{1,0:T(8,128)(2,1)S(1)}, bf16[512,256]{1,0:T(8,128)(2,1)S(1)}, u32[]{:S(2)}, u32[]{:S(2)}) %collective-permute-start.21) | collective-permute-done | bytes 262176 | tf_op jit(solution)/shard_map/ppermute | solution.py:61
  87.0 3.8 %collective-permute-start.22 = (bf16[512,256]{1,0:T(8,128)(2,1)S(1)}, bf16[512,256]{1,0:T(8,128)(2,1)S(1)}, u32[]{:S(2)}, u32[]{:S(2)}) collective-permute-start(bf16[512,256]{1,0:T(8,128)(2,1)S(1)} %collective-permute-done.21.refs_4_), channel_id=1, source_target_pairs={{0,12},{4,0},{8,4},{12,8},{1,13},{5,1},{9,5},{13,9},{2,14},{6,2},{... | collective-permute-start | bytes 786440 | tf_op jit(solution)/shard_map/ppermute | solution.py:61
  90.8 2.6 %collective-permute-done.17.refs_5_ = bf16[512,1024]{1,0:T(8,128)(2,1)S(1)} collective-permute-done((bf16[512,1024]{1,0:T(8,128)(2,1)S(1)}, bf16[512,1024]{1,0:T(8,128)(2,1)S(1)}, u32[]{:S(2)}, u32[]{:S(2)}) %collective-permute-start.17) | collective-permute-done | bytes 1048608 | tf_op jit(solution)/shard_map/ppermute | solution.py:65
  93.4 3.7 %collective-permute-done.16.refs_2_ = bf16[512,256]{1,0:T(8,128)(2,1)S(1)} collective-permute-done((bf16[512,256]{1,0:T(8,128)(2,1)S(1)}, bf16[512,256]{1,0:T(8,128)(2,1)S(1)}, u32[]{:S(2)}, u32[]{:S(2)}) %collective-permute-start.16) | collective-permute-done | bytes 262176 | tf_op jit(solution)/shard_map/ppermute | solution.py:61
  97.1 1.3 out_term.1
  98.5 2.8 %collective-permute-done.22.refs_3_ = bf16[512,256]{1,0:T(8,128)(2,1)S(1)} collective-permute-done((bf16[512,256]{1,0:T(8,128)(2,1)S(1)}, bf16[512,256]{1,0:T(8,128)(2,1)S(1)}, u32[]{:S(2)}, u32[]{:S(2)}) %collective-permute-start.22) | collective-permute-done | bytes 262176 | tf_op jit(solution)/shard_map/ppermute | solution.py:61
  101.2 11.8 %collective-permute-done.23.refs_6_.refs_3_ = bf16[512,1024]{1,0:T(8,128)(2,1)S(1)} collective-permute-done((bf16[512,1024]{1,0:T(8,128)(2,1)S(1)}, bf16[512,1024]{1,0:T(8,128)(2,1)S(1)}, u32[]{:S(2)}, u32[]{:S(2)}) %collective-permute-start.23) | collective-permute-done | bytes 1048608 | tf_op jit(solution)/shard_map/ppermute | solution.py:65
  113.0 1.3 out_sum.1.refs_0_.refs_4_
  114.4 2.6 %collective-permute-done.24.refs_1_ = bf16[512,1024]{1,0:T(8,128)(2,1)S(1)} collective-permute-done((bf16[512,1024]{1,0:T(8,128)(2,1)S(1)}, bf16[512,1024]{1,0:T(8,128)(2,1)S(1)}, u32[]{:S(2)}, u32[]{:S(2)}) %collective-permute-start.24) | collective-permute-done | bytes 1048608 | tf_op jit(solution)/shard_map/ppermute | solution.py:65
  117.1 1.6 grad_term.1
  118.7 0.7 collective-permute-start.27
  119.4 1.5 collective-permute-start.25
  120.9 3.2 %collective-permute-start.29 = (bf16[512,256]{1,0:T(8,128)(2,1)S(1)}, bf16[512,256]{1,0:T(8,128)(2,1)S(1)}, u32[]{:S(2)}, u32[]{:S(2)}) collective-permute-start(bf16[512,256]{1,0:T(8,128)(2,1)S(1)} %get-tuple-element.45), channel_id=1, source_target_pairs={{0,12},{4,0},{8,4},{12,8},{1,13},{5,1},{9,5},{13,9},{2,14},{6,2},{... | collective-permute-start | bytes 786440 | tf_op jit(solution)/shard_map/ppermute | solution.py:61
  124.1 5.7 %collective-permute-done.27.refs_0_ = bf16[512,256]{1,0:T(8,128)(2,1)S(1)} collective-permute-done((bf16[512,256]{1,0:T(8,128)(2,1)S(1)}, bf16[512,256]{1,0:T(8,128)(2,1)S(1)}, u32[]{:S(2)}, u32[]{:S(2)}) %collective-permute-start.27) | collective-permute-done | bytes 262176 | tf_op jit(solution)/shard_map/ppermute | solution.py:61
  129.9 0.2 collective-permute-start.28
  130.1 4.3 %collective-permute-done.29.refs_2_ = bf16[512,256]{1,0:T(8,128)(2,1)S(1)} collective-permute-done((bf16[512,256]{1,0:T(8,128)(2,1)S(1)}, bf16[512,256]{1,0:T(8,128)(2,1)S(1)}, u32[]{:S(2)}, u32[]{:S(2)}) %collective-permute-start.29) | collective-permute-done | bytes 262176 | tf_op jit(solution)/shard_map/ppermute | solution.py:61
  134.4 7.7 %collective-permute-done.28.refs_1_ = bf16[512,256]{1,0:T(8,128)(2,1)S(1)} collective-permute-done((bf16[512,256]{1,0:T(8,128)(2,1)S(1)}, bf16[512,256]{1,0:T(8,128)(2,1)S(1)}, u32[]{:S(2)}, u32[]{:S(2)}) %collective-permute-start.28) | collective-permute-done | bytes 262176 | tf_op jit(solution)/shard_map/ppermute | solution.py:61
  142.2 1.6 collective-permute-start.30
  143.8 0.5 collective-permute-start.19
  144.3 4.4 %collective-permute-done.30.refs_1_ = bf16[512,128]{1,0:T(8,128)(2,1)S(1)} collective-permute-done((bf16[512,128]{1,0:T(8,128)(2,1)S(1)}, bf16[512,128]{1,0:T(8,128)(2,1)S(1)}, u32[]{:S(2)}, u32[]{:S(2)}) %collective-permute-start.30) | collective-permute-done | bytes 131104 | tf_op jit(solution)/shard_map/ppermute | solution.py:65
  148.7 2.1 %key_grad.1.refs_8_.refs_1_ = bf16[1024,128]{1,0:T(8,128)(2,1)S(1)} custom-call(bf16[512,128]{1,0:T(8,128)(2,1)S(1)} %get-tuple-element.46.refs_0_.refs_3_, bf16[512,128]{1,0:T(8,128)(2,1)S(1)} %collective-permute-done.30.refs_1_, bf16[2,1024,1024]{2,1,0:T(8,128)(2,1)S(1)} %get-tuple-element.31.refs_2_.refs_3_, ...), custom_call_target="tpu_custom_call" | custom-call | flops 1 | bytes 1048576 | tf_op jit(solution)/shard_map/key_grad/pallas_call | solution.py:33
  150.8 1.8 %collective-permute-start.32 = (bf16[1024,128]{1,0:T(8,128)(2,1)S(1)}, bf16[1024,128]{1,0:T(8,128)(2,1)S(1)}, u32[]{:S(2)}, u32[]{:S(2)}) collective-permute-start(bf16[1024,128]{1,0:T(8,128)(2,1)S(1)} %key_grad.1.refs_8_.refs_1_), channel_id=1, source_target_pairs={{0,12},{4,0},{8,4},{12,8},{1,13},{5,1},{9,5},{13,9},{2,14},{6,2},{... | collective-permute-start | bytes 786440 | tf_op jit(solution)/shard_map/ppermute | solution.py:61
  152.6 0.3 collective-permute-start.31
  152.9 9.5 %collective-permute-done.32.refs_4_ = bf16[1024,128]{1,0:T(8,128)(2,1)S(1)} collective-permute-done((bf16[1024,128]{1,0:T(8,128)(2,1)S(1)}, bf16[1024,128]{1,0:T(8,128)(2,1)S(1)}, u32[]{:S(2)}, u32[]{:S(2)}) %collective-permute-start.32) | collective-permute-done | bytes 262176 | tf_op jit(solution)/shard_map/ppermute | solution.py:61
  162.3 0.6 collective-permute-start.33
  162.9 2.4 %out_product.1.refs_1_ = bf16[512,1024]{1,0:T(8,128)(2,1)} custom-call(bf16[512,256]{1,0:T(8,128)(2,1)S(1)} %join.2.refs_4_.refs_0_, bf16[512,256]{1,0:T(8,128)(2,1)S(1)} %collective-permute-done.14.refs_2_.refs_1_, bf16[512,256]{1,0:T(8,128)(2,1)S(1)} %collective-permute-done.16.refs_2_, bf16[512,256]{1,0:T(8,128)(2,1)S(1)} %collective-permute-done.15.refs_3_, ...), custom_call_target="tpu_custom_call" | custom-call | flops 1 | bytes 1048576 | tf_op jit(solution)/shard_map/out_product/pallas_call | solution.py:33
  165.3 1.2 copy-done
  166.5 0.6 flip.1.refs_0_.refs_5_
  167.2 1.5 collective-permute-done.33.refs_3_
  168.7 2.3 %value_product.1 = bf16[1024,512]{1,0:T(8,128)(2,1)} custom-call(bf16[1024,1024]{1,0:T(8,128)(2,1)S(1)} %flip.1.refs_0_.refs_5_, bf16[1024,128]{1,0:T(8,128)(2,1)S(1)} %key_grad.1.refs_8_.refs_1_, bf16[1024,128]{1,0:T(8,128)(2,1)S(1)} %collective-permute-done.31.refs_2_, bf16[1024,128]{1,0:T(8,128)(2,1)S(1)} %collective-permute-done.33.refs_3_, ...), custom_call_target="tpu_custom_call" | custom-call | flops 1 | bytes 1048576 | tf_op jit(solution)/shard_map/value_product/pallas_call | solution.py:33
  (41 shorter events, 0.8 us)
Async XLA Ops:
  1.7 11.7 %collective-permute-start.2 = (bf16[64,1024]{1,0:T(8,128)(2,1)S(1)}, bf16[64,1024]{1,0:T(8,128)(2,1)S(1)}, u32[]{:S(2)}, u32[]{:S(2)}) collective-permute-start(bf16[64,1024]{1,0:T(8,128)(2,1)S(1)} %get-tuple-element.48), channel_id=1, source_target_pairs={{0,12},{4,0},{8,4},{12,8},{1,13},{5,1},{9,5},{13,9},{2,14},{6,2},{... | collective-permute-start | bytes 393224 | tf_op jit(solution)/shard_map/ppermute | solution.py:61
  6.8 9.0 %collective-permute-start = (bf16[64,1024]{1,0:T(8,128)(2,1)S(1)}, bf16[64,1024]{1,0:T(8,128)(2,1)S(1)}, u32[]{:S(2)}, u32[]{:S(2)}) collective-permute-start(bf16[64,1024]{1,0:T(8,128)(2,1)S(1)} %get-tuple-element.49), channel_id=1, source_target_pairs={{0,4},{4,8},{8,12},{12,0},{1,5},{5,9},{9,13},{13,1},{2,6},{6,10},{... | collective-permute-start | bytes 393224 | tf_op jit(solution)/shard_map/ppermute | solution.py:61
  6.8 20.9 %collective-permute-start.1 = (bf16[64,1024]{1,0:T(8,128)(2,1)S(1)}, bf16[64,1024]{1,0:T(8,128)(2,1)S(1)}, u32[]{:S(2)}, u32[]{:S(2)}) collective-permute-start(bf16[64,1024]{1,0:T(8,128)(2,1)S(1)} %get-tuple-element.50), channel_id=1, source_target_pairs={{0,8},{4,12},{8,0},{12,4},{1,9},{5,13},{9,1},{13,5},{2,10},{6,14},... | collective-permute-start | bytes 393224 | tf_op jit(solution)/shard_map/ppermute | solution.py:61
  9.9 26.8 %copy-start.3 = (bf16[1024,512]{1,0:T(8,128)(2,1)S(1)}, bf16[1024,512]{1,0:T(8,128)(2,1)}, u32[]{:S(2)}) copy-start(bf16[1024,512]{1,0:T(8,128)(2,1)} %refs_3_.1) | copy-start | bytes 3145732
  9.9 19.4 %collective-permute-start.6 = (bf16[3,256,128]{2,1,0:T(8,128)(2,1)S(1)}, bf16[3,256,128]{2,1,0:T(8,128)(2,1)S(1)}, u32[]{:S(2)}, u32[]{:S(2)}) collective-permute-start(bf16[3,256,128]{2,1,0:T(8,128)(2,1)S(1)} %pad_maximum_fusion), channel_id=1, source_target_pairs={{0,4},{4,8},{8,12},{12,0},{1,5},{5,9},{9,13},{13,1},{2,6},{6,10},{... | collective-permute-start | bytes 589832 | tf_op jit(solution)/shard_map/ppermute | solution.py:61
  13.3 18.7 %collective-permute-start.7 = (bf16[3,256,128]{2,1,0:T(8,128)(2,1)S(1)}, bf16[3,256,128]{2,1,0:T(8,128)(2,1)S(1)}, u32[]{:S(2)}, u32[]{:S(2)}) collective-permute-start(bf16[3,256,128]{2,1,0:T(8,128)(2,1)S(1)} %pad_maximum_fusion.1), channel_id=1, source_target_pairs={{0,8},{4,12},{8,0},{12,4},{1,9},{5,13},{9,1},{13,5},{2,10},{6,14},... | collective-permute-start | bytes 589832 | tf_op jit(solution)/shard_map/ppermute | solution.py:61
  13.4 18.6 %collective-permute-start.8 = (bf16[3,256,128]{2,1,0:T(8,128)(2,1)S(1)}, bf16[3,256,128]{2,1,0:T(8,128)(2,1)S(1)}, u32[]{:S(2)}, u32[]{:S(2)}) collective-permute-start(bf16[3,256,128]{2,1,0:T(8,128)(2,1)S(1)} %pad_maximum_fusion.2), channel_id=1, source_target_pairs={{0,12},{4,0},{8,4},{12,8},{1,13},{5,1},{9,5},{13,9},{2,14},{6,2},{... | collective-permute-start | bytes 589832 | tf_op jit(solution)/shard_map/ppermute | solution.py:61
  15.9 16.1 %collective-permute-start.5 = (bf16[64,1024]{1,0:T(8,128)(2,1)S(1)}, bf16[64,1024]{1,0:T(8,128)(2,1)S(1)}, u32[]{:S(2)}, u32[]{:S(2)}) collective-permute-start(bf16[64,1024]{1,0:T(8,128)(2,1)S(1)} %collective-permute-done.2.refs_2_), channel_id=1, source_target_pairs={{0,2},{2,0},{1,3},{3,1},{4,6},{6,4},{5,7},{7,5},{8,10},{10,8},{9,1... | collective-permute-start | bytes 393224 | tf_op jit(solution)/shard_map/ppermute | solution.py:65
  27.8 5.0 %collective-permute-start.3 = (bf16[64,1024]{1,0:T(8,128)(2,1)S(1)}, bf16[64,1024]{1,0:T(8,128)(2,1)S(1)}, u32[]{:S(2)}, u32[]{:S(2)}) collective-permute-start(bf16[64,1024]{1,0:T(8,128)(2,1)S(1)} %collective-permute-done.refs_0_), channel_id=1, source_target_pairs={{0,2},{2,0},{1,3},{3,1},{4,6},{6,4},{5,7},{7,5},{8,10},{10,8},{9,1... | collective-permute-start | bytes 393224 | tf_op jit(solution)/shard_map/ppermute | solution.py:65
  29.3 5.0 %collective-permute-start.4 = (bf16[64,1024]{1,0:T(8,128)(2,1)S(1)}, bf16[64,1024]{1,0:T(8,128)(2,1)S(1)}, u32[]{:S(2)}, u32[]{:S(2)}) collective-permute-start(bf16[64,1024]{1,0:T(8,128)(2,1)S(1)} %collective-permute-done.1.refs_1_), channel_id=1, source_target_pairs={{0,2},{2,0},{1,3},{3,1},{4,6},{6,4},{5,7},{7,5},{8,10},{10,8},{9,1... | collective-permute-start | bytes 393224 | tf_op jit(solution)/shard_map/ppermute | solution.py:65
  34.3 2.4 %collective-permute-start.9 = (bf16[6,64,1024]{2,1,0:T(8,128)(2,1)S(1)}, bf16[6,64,1024]{2,1,0:T(8,128)(2,1)S(1)}, u32[]{:S(2)}, u32[]{:S(2)}) collective-permute-start(bf16[6,64,1024]{2,1,0:T(8,128)(2,1)S(1)} %pack.1.refs_1_.refs_4_), channel_id=1, source_target_pairs={{0,1},{1,0},{2,3},{3,2},{4,5},{5,4},{6,7},{7,6},{8,9},{9,8},{10,11... | collective-permute-start | bytes 2359304 | tf_op jit(solution)/shard_map/ppermute | solution.py:65
  35.5 6.5 %copy-start.4 = (bf16[256,512]{1,0:T(8,128)(2,1)S(1)}, bf16[256,512]{1,0:T(8,128)(2,1)}, u32[]{:S(2)}) copy-start(bf16[256,512]{1,0:T(8,128)(2,1)} %refs_0_.1) | copy-start | bytes 786436
  35.5 6.5 %copy-start.5 = (bf16[256,512]{1,0:T(8,128)(2,1)S(1)}, bf16[256,512]{1,0:T(8,128)(2,1)}, u32[]{:S(2)}) copy-start(bf16[256,512]{1,0:T(8,128)(2,1)} %refs_2_.2) | copy-start | bytes 786436
  35.5 6.5 %copy-start.6 = (bf16[256,512]{1,0:T(8,128)(2,1)S(1)}, bf16[256,512]{1,0:T(8,128)(2,1)}, u32[]{:S(2)}) copy-start(bf16[256,512]{1,0:T(8,128)(2,1)} %refs_1_.1) | copy-start | bytes 786436
  38.1 12.4 %collective-permute-start.11 = (bf16[1024,128]{1,0:T(8,128)(2,1)S(1)}, bf16[1024,128]{1,0:T(8,128)(2,1)S(1)}, u32[]{:S(2)}, u32[]{:S(2)}) collective-permute-start(bf16[1024,128]{1,0:T(8,128)(2,1)S(1)} %get-tuple-element.29), channel_id=1, source_target_pairs={{0,4},{4,8},{8,12},{12,0},{1,5},{5,9},{9,13},{13,1},{2,6},{6,10},{... | collective-permute-start | bytes 786440 | tf_op jit(solution)/shard_map/ppermute | solution.py:61
  39.9 15.6 %collective-permute-start.13 = (bf16[1024,128]{1,0:T(8,128)(2,1)S(1)}, bf16[1024,128]{1,0:T(8,128)(2,1)S(1)}, u32[]{:S(2)}, u32[]{:S(2)}) collective-permute-start(bf16[1024,128]{1,0:T(8,128)(2,1)S(1)} %get-tuple-element.32), channel_id=1, source_target_pairs={{0,12},{4,0},{8,4},{12,8},{1,13},{5,1},{9,5},{13,9},{2,14},{6,2},{... | collective-permute-start | bytes 786440 | tf_op jit(solution)/shard_map/ppermute | solution.py:61
  50.5 9.6 %collective-permute-start.12 = (bf16[1024,128]{1,0:T(8,128)(2,1)S(1)}, bf16[1024,128]{1,0:T(8,128)(2,1)S(1)}, u32[]{:S(2)}, u32[]{:S(2)}) collective-permute-start(bf16[1024,128]{1,0:T(8,128)(2,1)S(1)} %add.67.refs_4_), channel_id=1, source_target_pairs={{0,4},{4,8},{8,12},{12,0},{1,5},{5,9},{9,13},{13,1},{2,6},{6,10},{... | collective-permute-start | bytes 786440 | tf_op jit(solution)/shard_map/ppermute | solution.py:61
  54.0 7.6 %collective-permute-start.10 = (bf16[512,128]{1,0:T(8,128)(2,1)S(1)}, bf16[512,128]{1,0:T(8,128)(2,1)S(1)}, u32[]{:S(2)}, u32[]{:S(2)}) collective-permute-start(bf16[512,128]{1,0:T(8,128)(2,1)S(1)} %get-tuple-element.27), channel_id=1, source_target_pairs={{0,2},{2,0},{1,3},{3,1},{4,6},{6,4},{5,7},{7,5},{8,10},{10,8},{9,1... | collective-permute-start | bytes 393224 | tf_op jit(solution)/shard_map/ppermute | solution.py:65
  60.2 5.9 %copy-start.2 = (bf16[512,1024]{1,0:T(8,128)(2,1)S(1)}, bf16[512,1024]{1,0:T(8,128)(2,1)}, u32[]{:S(2)}) copy-start(bf16[512,1024]{1,0:T(8,128)(2,1)} %refs_4_.1) | copy-start | bytes 3145732
  60.2 16.1 %copy-start.1 = (bf16[512,1024]{1,0:T(8,128)(2,1)S(1)}, bf16[512,1024]{1,0:T(8,128)(2,1)}, u32[]{:S(2)}) copy-start(bf16[512,1024]{1,0:T(8,128)(2,1)} %refs_2_.3) | copy-start | bytes 3145732
  61.7 9.6 %collective-permute-start.15 = (bf16[512,256]{1,0:T(8,128)(2,1)S(1)}, bf16[512,256]{1,0:T(8,128)(2,1)S(1)}, u32[]{:S(2)}, u32[]{:S(2)}) collective-permute-start(bf16[512,256]{1,0:T(8,128)(2,1)S(1)} %join.2.refs_4_.refs_0_), channel_id=1, source_target_pairs={{0,12},{4,0},{8,4},{12,8},{1,13},{5,1},{9,5},{13,9},{2,14},{6,2},{... | collective-permute-start | bytes 786440 | tf_op jit(solution)/shard_map/ppermute | solution.py:61
  64.5 11.7 %collective-permute-start.14 = (bf16[512,256]{1,0:T(8,128)(2,1)S(1)}, bf16[512,256]{1,0:T(8,128)(2,1)S(1)}, u32[]{:S(2)}, u32[]{:S(2)}) collective-permute-start(bf16[512,256]{1,0:T(8,128)(2,1)S(1)} %join.2.refs_4_.refs_0_), channel_id=1, source_target_pairs={{0,4},{4,8},{8,12},{12,0},{1,5},{5,9},{9,13},{13,1},{2,6},{6,10},{... | collective-permute-start | bytes 786440 | tf_op jit(solution)/shard_map/ppermute | solution.py:61
  64.5 6.4 %collective-permute-start.18 = (bf16[512,128]{1,0:T(8,128)(2,1)S(1)}, bf16[512,128]{1,0:T(8,128)(2,1)S(1)}, u32[]{:S(2)}, u32[]{:S(2)}) collective-permute-start(bf16[512,128]{1,0:T(8,128)(2,1)S(1)} %get-tuple-element.36), channel_id=1, source_target_pairs={{0,2},{2,0},{1,3},{3,1},{4,6},{6,4},{5,7},{7,5},{8,10},{10,8},{9,1... | collective-permute-start | bytes 393224 | tf_op jit(solution)/shard_map/ppermute | solution.py:65
  66.0 27.4 %collective-permute-start.17 = (bf16[512,1024]{1,0:T(8,128)(2,1)S(1)}, bf16[512,1024]{1,0:T(8,128)(2,1)S(1)}, u32[]{:S(2)}, u32[]{:S(2)}) collective-permute-start(bf16[512,1024]{1,0:T(8,128)(2,1)S(1)} %copy-done.2), channel_id=1, source_target_pairs={{0,2},{2,0},{1,3},{3,1},{4,6},{6,4},{5,7},{7,5},{8,10},{10,8},{9,1... | collective-permute-start | bytes 3145736 | tf_op jit(solution)/shard_map/ppermute | solution.py:65
  76.3 36.7 %collective-permute-start.23 = (bf16[512,1024]{1,0:T(8,128)(2,1)S(1)}, bf16[512,1024]{1,0:T(8,128)(2,1)S(1)}, u32[]{:S(2)}, u32[]{:S(2)}) collective-permute-start(bf16[512,1024]{1,0:T(8,128)(2,1)S(1)} %copy-done.1), channel_id=1, source_target_pairs={{0,2},{2,0},{1,3},{3,1},{4,6},{6,4},{5,7},{7,5},{8,10},{10,8},{9,1... | collective-permute-start | bytes 3145736 | tf_op jit(solution)/shard_map/ppermute | solution.py:65
  77.9 9.1 %collective-permute-start.21 = (bf16[512,256]{1,0:T(8,128)(2,1)S(1)}, bf16[512,256]{1,0:T(8,128)(2,1)S(1)}, u32[]{:S(2)}, u32[]{:S(2)}) collective-permute-start(bf16[512,256]{1,0:T(8,128)(2,1)S(1)} %join.3.refs_6_.refs_1_), channel_id=1, source_target_pairs={{0,12},{4,0},{8,4},{12,8},{1,13},{5,1},{9,5},{13,9},{2,14},{6,2},{... | collective-permute-start | bytes 786440 | tf_op jit(solution)/shard_map/ppermute | solution.py:61
  79.6 17.5 %collective-permute-start.16 = (bf16[512,256]{1,0:T(8,128)(2,1)S(1)}, bf16[512,256]{1,0:T(8,128)(2,1)S(1)}, u32[]{:S(2)}, u32[]{:S(2)}) collective-permute-start(bf16[512,256]{1,0:T(8,128)(2,1)S(1)} %collective-permute-done.15.refs_3_), channel_id=1, source_target_pairs={{0,12},{4,0},{8,4},{12,8},{1,13},{5,1},{9,5},{13,9},{2,14},{6,2},{... | collective-permute-start | bytes 786440 | tf_op jit(solution)/shard_map/ppermute | solution.py:61
  80.0 18.5 %collective-permute-start.20 = (bf16[512,256]{1,0:T(8,128)(2,1)S(1)}, bf16[512,256]{1,0:T(8,128)(2,1)S(1)}, u32[]{:S(2)}, u32[]{:S(2)}) collective-permute-start(bf16[512,256]{1,0:T(8,128)(2,1)S(1)} %join.3.refs_6_.refs_1_), channel_id=1, source_target_pairs={{0,4},{4,8},{8,12},{12,0},{1,5},{5,9},{9,13},{13,1},{2,6},{6,10},{... | collective-permute-start | bytes 786440 | tf_op jit(solution)/shard_map/ppermute | solution.py:61
  87.0 14.3 %collective-permute-start.22 = (bf16[512,256]{1,0:T(8,128)(2,1)S(1)}, bf16[512,256]{1,0:T(8,128)(2,1)S(1)}, u32[]{:S(2)}, u32[]{:S(2)}) collective-permute-start(bf16[512,256]{1,0:T(8,128)(2,1)S(1)} %collective-permute-done.21.refs_4_), channel_id=1, source_target_pairs={{0,12},{4,0},{8,4},{12,8},{1,13},{5,1},{9,5},{13,9},{2,14},{6,2},{... | collective-permute-start | bytes 786440 | tf_op jit(solution)/shard_map/ppermute | solution.py:61
  114.3 2.7 %collective-permute-start.24 = (bf16[512,1024]{1,0:T(8,128)(2,1)S(1)}, bf16[512,1024]{1,0:T(8,128)(2,1)S(1)}, u32[]{:S(2)}, u32[]{:S(2)}) collective-permute-start(bf16[512,1024]{1,0:T(8,128)(2,1)S(1)} %out_sum.1.refs_0_.refs_4_), channel_id=1, source_target_pairs={{0,1},{1,0},{2,3},{3,2},{4,5},{5,4},{6,7},{7,6},{8,9},{9,8},{10,11... | collective-permute-start | bytes 3145736 | tf_op jit(solution)/shard_map/ppermute | solution.py:65
  118.7 11.1 %collective-permute-start.27 = (bf16[512,256]{1,0:T(8,128)(2,1)S(1)}, bf16[512,256]{1,0:T(8,128)(2,1)S(1)}, u32[]{:S(2)}, u32[]{:S(2)}) collective-permute-start(bf16[512,256]{1,0:T(8,128)(2,1)S(1)} %get-tuple-element.43), channel_id=1, source_target_pairs={{0,4},{4,8},{8,12},{12,0},{1,5},{5,9},{9,13},{13,1},{2,6},{6,10},{... | collective-permute-start | bytes 786440 | tf_op jit(solution)/shard_map/ppermute | solution.py:61
  119.4 24.9 %collective-permute-start.25 = (bf16[256,1024]{1,0:T(8,128)(2,1)S(1)}, bf16[256,1024]{1,0:T(8,128)(2,1)S(1)}, u32[]{:S(2)}, u32[]{:S(2)}) collective-permute-start(bf16[256,1024]{1,0:T(8,128)(2,1)S(1)} %get-tuple-element.41), channel_id=1, source_target_pairs={{0,2},{2,0},{1,3},{3,1},{4,6},{6,4},{5,7},{7,5},{8,10},{10,8},{9,1... | collective-permute-start | bytes 1572872 | tf_op jit(solution)/shard_map/ppermute | solution.py:65
  120.9 13.5 %collective-permute-start.29 = (bf16[512,256]{1,0:T(8,128)(2,1)S(1)}, bf16[512,256]{1,0:T(8,128)(2,1)S(1)}, u32[]{:S(2)}, u32[]{:S(2)}) collective-permute-start(bf16[512,256]{1,0:T(8,128)(2,1)S(1)} %get-tuple-element.45), channel_id=1, source_target_pairs={{0,12},{4,0},{8,4},{12,8},{1,13},{5,1},{9,5},{13,9},{2,14},{6,2},{... | collective-permute-start | bytes 786440 | tf_op jit(solution)/shard_map/ppermute | solution.py:61
  129.9 12.3 %collective-permute-start.28 = (bf16[512,256]{1,0:T(8,128)(2,1)S(1)}, bf16[512,256]{1,0:T(8,128)(2,1)S(1)}, u32[]{:S(2)}, u32[]{:S(2)}) collective-permute-start(bf16[512,256]{1,0:T(8,128)(2,1)S(1)} %add.68.refs_3_), channel_id=1, source_target_pairs={{0,4},{4,8},{8,12},{12,0},{1,5},{5,9},{9,13},{13,1},{2,6},{6,10},{... | collective-permute-start | bytes 786440 | tf_op jit(solution)/shard_map/ppermute | solution.py:61
  142.2 6.5 %collective-permute-start.30 = (bf16[512,128]{1,0:T(8,128)(2,1)S(1)}, bf16[512,128]{1,0:T(8,128)(2,1)S(1)}, u32[]{:S(2)}, u32[]{:S(2)}) collective-permute-start(bf16[512,128]{1,0:T(8,128)(2,1)S(1)} %get-tuple-element.47), channel_id=1, source_target_pairs={{0,2},{2,0},{1,3},{3,1},{4,6},{6,4},{5,7},{7,5},{8,10},{10,8},{9,1... | collective-permute-start | bytes 393224 | tf_op jit(solution)/shard_map/ppermute | solution.py:65
  143.8 19.1 %collective-permute-start.19 = (bf16[512,512]{1,0:T(8,128)(2,1)S(1)}, bf16[512,512]{1,0:T(8,128)(2,1)S(1)}, u32[]{:S(2)}, u32[]{:S(2)}) collective-permute-start(bf16[512,512]{1,0:T(8,128)(2,1)S(1)} %get-tuple-element.37), channel_id=1, source_target_pairs={{0,2},{2,0},{1,3},{3,1},{4,6},{6,4},{5,7},{7,5},{8,10},{10,8},{9,1... | collective-permute-start | bytes 1572872 | tf_op jit(solution)/shard_map/ppermute | solution.py:65
  144.3 18.6 %collective-permute-start.26 = (bf16[256,1024]{1,0:T(8,128)(2,1)S(1)}, bf16[256,1024]{1,0:T(8,128)(2,1)S(1)}, u32[]{:S(2)}, u32[]{:S(2)}) collective-permute-start(bf16[256,1024]{1,0:T(8,128)(2,1)S(1)} %collective-permute-done.25.refs_6_), channel_id=1, source_target_pairs={{0,1},{1,0},{2,3},{3,2},{4,5},{5,4},{6,7},{7,6},{8,9},{9,8},{10,11... | collective-permute-start | bytes 1572872 | tf_op jit(solution)/shard_map/ppermute | solution.py:65
  150.8 11.5 %collective-permute-start.32 = (bf16[1024,128]{1,0:T(8,128)(2,1)S(1)}, bf16[1024,128]{1,0:T(8,128)(2,1)S(1)}, u32[]{:S(2)}, u32[]{:S(2)}) collective-permute-start(bf16[1024,128]{1,0:T(8,128)(2,1)S(1)} %key_grad.1.refs_8_.refs_1_), channel_id=1, source_target_pairs={{0,12},{4,0},{8,4},{12,8},{1,13},{5,1},{9,5},{13,9},{2,14},{6,2},{... | collective-permute-start | bytes 786440 | tf_op jit(solution)/shard_map/ppermute | solution.py:61
  152.6 14.6 %collective-permute-start.31 = (bf16[1024,128]{1,0:T(8,128)(2,1)S(1)}, bf16[1024,128]{1,0:T(8,128)(2,1)S(1)}, u32[]{:S(2)}, u32[]{:S(2)}) collective-permute-start(bf16[1024,128]{1,0:T(8,128)(2,1)S(1)} %key_grad.1.refs_8_.refs_1_), channel_id=1, source_target_pairs={{0,4},{4,8},{8,12},{12,0},{1,5},{5,9},{9,13},{13,1},{2,6},{6,10},{... | collective-permute-start | bytes 786440 | tf_op jit(solution)/shard_map/ppermute | solution.py:61
  162.3 6.4 %collective-permute-start.33 = (bf16[1024,128]{1,0:T(8,128)(2,1)S(1)}, bf16[1024,128]{1,0:T(8,128)(2,1)S(1)}, u32[]{:S(2)}, u32[]{:S(2)}) collective-permute-start(bf16[1024,128]{1,0:T(8,128)(2,1)S(1)} %collective-permute-done.32.refs_4_), channel_id=1, source_target_pairs={{0,12},{4,0},{8,4},{12,8},{1,13},{5,1},{9,5},{13,9},{2,14},{6,2},{... | collective-permute-start | bytes 786440 | tf_op jit(solution)/shard_map/ppermute | solution.py:61
  165.3 1.2 copy-start

commit v3 on v2

--- a/solution.py
+++ b/solution.py
@@ -19,7 +19,7 @@
     def __init__(self):
         self.last = None
 
-    def __call__(self, kernel, outs, ins, scratch=(), in_specs=None, first=(), mib=1):
+    def __call__(self, kernel, outs, ins, scratch=(), in_specs=None, first=()):
         specs = in_specs or [VMEM] * len(ins)
         out_specs = [HBM] * len(outs) if in_specs and HBM in in_specs and VMEM not in in_specs else [VMEM] * len(outs)
         count = len(ins)
@@ -36,8 +36,8 @@
             in_specs=specs,
             out_specs=out_specs,
             scratch_shapes=list(scratch),
-            compiler_params=pltpu.CompilerParams(vmem_limit_bytes=44 * 2**20),
-            cost_estimate=pl.CostEstimate(flops=1, bytes_accessed=mib * 2**20, transcendentals=0),
+            compiler_params=pltpu.CompilerParams(vmem_limit_bytes=18 * 2**20),
+            cost_estimate=pl.CostEstimate(flops=1, bytes_accessed=1, transcendentals=0),
             name=getattr(kernel, "func", kernel).__name__,
         )(*ins)
         self.last = results[0]
@@ -70,24 +70,29 @@
 
 
 def pack(*refs):
-    out = refs[-1]
-    for j, piece in enumerate(refs[:-1]):
+    *pieces, weight, out, share, sem = refs
+    copy = pltpu.make_async_copy(weight.at[at(lax.axis_index("groups"), share.shape[0])], share, sem)
+    copy.start()
+    for j, piece in enumerate(pieces):
         out[j] = piece[...]
-
-
-def tangent_term(n, own, packed, peer, probe, feats, *refs):
-    outs, whole = refs[:n], refs[n]
+    copy.wait()
+
+
+def tangent_term(n, normed, packed, peer, probe, feats, *refs):
+    outs, whole, sem = refs[:n], refs[n], refs[n + 1]
     me, head, rep = lax.axis_index("seq"), lax.axis_index("head"), lax.axis_index("rep")
-    tok = own.shape[0]
-    part = packed.shape[1]
+    tok = normed.shape[0]
+    part, slab = packed.shape[1:]
+    copy = pltpu.make_async_copy(normed.at[:, at(me, slab)], feats.at[at(me, tok)], sem)
+    copy.start()
     cols = outs[0].shape[1]
-    for k in range(n):
+    for k in [*range(1, n), 0]:
         block = lax.rem(me - k + n, n)
         if k == 0:
-            feats[at(block, tok), :] = own[...]
+            copy.wait()
         else:
             for rows, core in ((packed, rep), (peer, 1 - rep)):
-                for row, side in ((k - 1, head), (n - 2 + k, 1 - head)):
+                for row, side in ((k % (n - 1), head), (n - 1 + k % (n - 1), 1 - head)):
                     start = block * tok + (core * 2 + side) * part
                     feats[pl.ds(pl.multiple_of(start, part), part), :] = rows[row]
         whole[at(block, tok), :] = dot(feats[at(block, tok), :], probe[...]).astype(jnp.bfloat16)
@@ -104,7 +109,7 @@
 
 
 def attend(n, *refs):
-    own, pieces, (probs, attended, home, away, *all3) = refs[:3], refs[3 : n + 2], refs[n + 2 :]
+    own, pieces, (probs, attended, *all3) = refs[:3], refs[3 : n + 2], refs[n + 2 :]
     q_all, k_all, v_all = all3
     me = lax.axis_index("seq")
     tok, cols = pieces[0].shape[1:]
@@ -128,8 +133,6 @@
             probs[h, :, rows] = prob
             parts.append(dot(v_flip, prob))
         attended[rows, :] = keep_heads(parts).T.astype(jnp.bfloat16)
-
-    halves(attended, home, away)
 
 
 def halves(rows, home, away):
@@ -167,38 +170,52 @@
     out[:, cols:] = other[...]
 
 
-def both_columns(n, pieces, lhs):
-    me = lax.axis_index("seq")
+def cut_rows(n, *refs):
+    pieces, away = refs[:n], refs[n]
+    me, head = lax.axis_index("seq"), lax.axis_index("head")
+    half = away.shape[0]
+    cols = pieces[0].shape[1]
+    for k in range(n):
+        away[:, at(lax.rem(me - k + n, n), cols)] = pieces[k][at(1 - head, half), :]
+
+
+def out_term(n, *refs):
+    pieces, (theirs, probe, other, total, lhs) = refs[:n], refs[n:]
+    me, head = lax.axis_index("seq"), lax.axis_index("head")
+    half = theirs.shape[0]
+    cols = pieces[0].shape[1]
+    for k in range(n):
+        lhs[:, at(lax.rem(me - k + n, n), cols)] = pieces[k][at(head, half), :]
+    total[...] = dot(lhs[...], probe[...])
+    total[...] += dot(theirs[...], other[...])
+
+
+def out_sum(n, *refs):
+    base, pieces, (weight, one, two, out, lhs) = refs[0], refs[1 : n + 1], refs[n + 1 :]
+    me, group = lax.axis_index("seq"), lax.axis_index("groups")
     cols = pieces[0].shape[1] // 2
     for k in range(n):
         where = at(lax.rem(me - k + n, n), cols)
         for d in range(2):
             lhs[d, :, where] = pieces[k][:, d * cols : (d + 1) * cols]
-
-
-def out_term(n, *refs):
-    pieces, (probe, other, total, theirs, lhs) = refs[:n], refs[n:]
-    both_columns(n, pieces, lhs)
-    total[...] = dot(lhs[0], probe[...])
-    total[...] += dot(lhs[1], other[...])
-    theirs[...] = lhs[1]
-
-
-def out_sum(n, *refs):
-    base, pieces, weight, other, out, lhs = refs[0], refs[1 : n + 1], refs[n + 1], refs[n + 2], refs[n + 3], refs[n + 4]
-    both_columns(n, pieces, lhs)
+    rows = one.shape[0]
     total = base[...] + dot(lhs[0], weight[...])
-    out[...] = (total + dot(lhs[1], other[...])).astype(jnp.bfloat16)
-
-
-def grad_term(n, mine, other_core, weight, other, tangent_out, share, *refs):
+    total = total + dot(lhs[1, :, at(group, rows)], one[...])
+    out[...] = (total + dot(lhs[1, :, at(1 - group, rows)], two[...])).astype(jnp.bfloat16)
+
+
+def grad_term(n, mine, other_core, weight, one, two, tangent_out, share, *refs):
     outs, grad = refs[:n], refs[n]
     me = lax.axis_index("seq")
     cols = outs[0].shape[1] // 2
     tangent_out[...] = (mine[...].astype(jnp.float32) + other_core[...].astype(jnp.float32)).astype(jnp.bfloat16)
     share[...] = tangent_out[at(lax.axis_index("rep"), share.shape[0]), :]
-    for d, rows in enumerate((weight, other)):
-        grad[d] = dot(tangent_out[...], rows[...], 1, 1).astype(jnp.bfloat16)
+    group = lax.axis_index("groups")
+    rows = one.shape[0]
+    grad[0] = dot(tangent_out[...], weight[...], 1, 1).astype(jnp.bfloat16)
+    grad[1, :, at(group, rows)] = dot(tangent_out[...], one[...], 1, 1).astype(jnp.bfloat16)
+    grad[1, :, at(1 - group, rows)] = dot(tangent_out[...], two[...], 1, 1).astype(jnp.bfloat16)
+    for d in range(2):
         for k in range(n):
             outs[k][:, d * cols : (d + 1) * cols] = grad[d, :, at(lax.rem(me + k, n), cols)]
 
@@ -243,15 +260,16 @@
 
 
 def out_product(n, *refs):
-    pieces, (theirs, mine, one, two, out, other) = refs[:n], refs[n:]
-    me, rep = lax.axis_index("seq"), lax.axis_index("rep")
-    cols = pieces[0].shape[1] // 2
-    other[at(rep, one.shape[0]), :] = one[...]
-    other[at(1 - rep, one.shape[0]), :] = two[...]
-    for k in range(n):
-        where = at(lax.rem(me - k + n, n), cols)
-        total = dot(pieces[k][:, :cols].T, mine[...])
-        out[where, :] = (total + dot(theirs[:, where].T, other[...])).astype(jnp.bfloat16)
+    pieces, (mine, one, two, out, rows) = refs[:n], refs[n:]
+    me, head, rep = lax.axis_index("seq"), lax.axis_index("head"), lax.axis_index("rep")
+    cols = pieces[0].shape[1]
+    half, part = mine.shape[0], one.shape[0]
+    rows[at(head, half), :] = mine[...]
+    for index, piece in ((rep, one), (1 - rep, two)):
+        start = (1 - head) * half + index * part
+        rows[pl.ds(pl.multiple_of(start, part), part), :] = piece[...]
+    for k in range(n):
+        out[at(lax.rem(me - k + n, n), cols), :] = dot(pieces[k][...].T, rows[...]).astype(jnp.bfloat16)
 
 
 def by_heads(normed, query_proj, key_proj, value_proj, out_weight, value_probe, out_probe):
@@ -291,39 +309,42 @@
     start = (rep * 2 + head) * quarter
     got = [
         ahead(lax.dynamic_slice(normed, (start, lax.rem(me + k, n) * slab), (quarter, slab)), k) for k in range(1, n)]
-    own = lax.dynamic_slice(normed, (0, me * slab), (tok, slab))
     proj = (query_proj, key_proj, value_proj)
     qkv = []
     for k in range(1, n):
         piece = jnp.stack([lax.dynamic_slice(x, (0, lax.rem(me + k, n) * cols), (tok, cols)) for x in proj])
-        qkv.append(ahead(piece, k))
+        qkv.append(ahead(after(piece, got[0]), k))
+    got = got[-1:] + got[:-1]
     other = [swap(x, "head") for x in got]
-    (packed,) = call(pack, [bf(2 * (n - 1), quarter, slab)], [*got, *other], first=qkv)
+    packed, share = call(
+        pack, [bf(2 * (n - 1), quarter, slab), bf(block // 2, slab)], [*got, *other, out_weight],
+        scratch=[dma(())], in_specs=[VMEM] * (2 * n - 2) + [ANY], first=qkv[:2])
     feats, *terms = call(
         part(tangent_term, n), [bf(tokens, slab)] + [bf(tokens, cols)] * n,
-        [own, packed, swap(packed, "rep"), value_probe], scratch=[held(tokens, block)])
-    probs, _, home, away = call(
-        part(attend, n), [bf(heads, tokens, tokens), bf(tokens, cols)] + [bf(half, cols)] * 2, [*proj, *qkv],
-        scratch=[held(tokens, cols)] * 3, mib=32)
-    away = swap(away, "head")
+        [normed, packed, swap(packed, "rep"), value_probe], scratch=[held(tokens, block), dma(())],
+        in_specs=[ANY] + [VMEM] * 3, first=qkv[2:])
+    other_probe = swap(after(out_probe, packed), "head")
+    weights = [swap(after(share, feats), "head")]
+    probs, attended = call(
+        part(attend, n), [bf(heads, tokens, tokens), bf(tokens, cols)], [*proj, *qkv],
+        scratch=[held(tokens, cols)] * 3)
+    att = gathered(attended)
     tangent = summed(terms)
-    other_probe = swap(after(out_probe, feats), "head")
     tan, tan_away = call(
         part(attend_tan, 3), [bf(half, cols)] * 2, [*tangent, probs],
         scratch=[held(heads, tokens, tokens), held(tokens, cols), dma((heads,))], in_specs=[VMEM] * 3 + [ANY])
-    (att,) = call(join, [bf(half, 2 * cols)], [home, away])
-    att = gathered(att)
-    (tan,) = call(join, [bf(half, 2 * cols)], [tan, swap(after(tan_away, att[0]), "head")], first=[att[1], att[-1]])
-    other_weight = swap(after(out_weight, tan), "head")
+    (tan,) = call(join, [bf(half, 2 * cols)], [tan, swap(tan_away, "head")], first=[att[1], att[-1]])
+    weights.append(swap(weights[0], "groups"))
     tan = gathered(tan)
-    base, theirs = call(
-        part(out_term, n), [jax.ShapeDtypeStruct((half, slab), f32), bf(half, block)], [*att, out_probe, other_probe],
-        scratch=[held(2, half, block)])
+    (away,) = call(part(cut_rows, n), [bf(half, block)], att)
+    (base,) = call(
+        part(out_term, n), [jax.ShapeDtypeStruct((half, slab), f32)],
+        [*att, swap(away, "head"), out_probe, other_probe], scratch=[held(half, block)])
     (mine,) = call(
-        part(out_sum, n), [bf(half, slab)], [base, *tan, out_weight, other_weight], scratch=[held(2, half, block)])
+        part(out_sum, n), [bf(half, slab)], [base, *tan, out_weight, *weights], scratch=[held(2, half, block)])
     tangent_out, share, *grads = call(
         part(grad_term, n), [bf(half, slab), bf(half // 2, slab)] + [bf(half, 2 * cols)] * n,
-        [mine, swap(mine, "rep"), out_weight, other_weight],
+        [mine, swap(mine, "rep"), out_weight, *weights],
         scratch=[held(2, half, block)])
     home, away = call(part(add_grad, 3), [bf(half, cols)] * 2, summed(grads))
     (value_grad,) = call(
@@ -332,8 +353,8 @@
     value_grad = gathered(value_grad)
     share = swap(share, "head")
     (out_curv,) = call(
-        part(out_product, n), [bf(block, slab)], [*att, swap(theirs, "head"), tangent_out, share, swap(share, "rep")],
-        scratch=[held(half, slab)])
+        part(out_product, n), [bf(block, slab)], [*att, tangent_out, share, swap(share, "rep")],
+        scratch=[held(tokens, slab)])
     (flipped,) = call(flip, [bf(slab, tokens)], [feats])
     (value_curv,) = call(
         part(value_product, n), [bf(slab, block)], [flipped, *value_grad], scratch=[held(tokens, block)])
@@ -344,7 +365,7 @@
     tok, cols = args[1].shape
     n = lax.axis_size("seq")
     even = cols % (n * 128) == 0 and tok % 64 == 0 and tok * n % 64 == 0
-    if even and lax.axis_size("head") == 2 and lax.axis_size("rep") == 2:
+    if even and all(lax.axis_size(axis) == 2 for axis in ("groups", "head", "rep")):
         return by_heads(*args)
     return by_tokens(*args)
 

time: 171 us -> 162 us (0.947)
  waiting for transfers between devices: 92.3 us -> 80.7 us
  starting transfers between devices: 48.9 us -> 52 us
    ppermute x13, waiting for transfers between devices: 29.3 us -> 16.3 us  [swap(): return lax.ppermute(x, axis, [(0, 1), (1, 0)])]
    ppermute x21, starting transfers between devices: 36.6 us -> 40.5 us  [ahead(): return lax.ppermute(x, 'seq', [(i, (i + k) % n) for i in range(n)])]
  transfers between devices with their start and end apart: 34 -> 34, of which waited for: 21 -> 18; matrix products, arithmetic and copies ran while one was open for 2% -> 1% of each run, Pallas kernels for 10% -> 10%
where the time goes in v3:
time: 162 us; the launch traced here: 161 us
  waiting for transfers between devices  80.7 us (50%)
  starting transfers between devices  52 us (32%)
  Pallas kernels  23.3 us (14%)
  local copies, waits for them, and re-layouts  4.53 us (3%)
    ppermute x21, waiting for transfers between devices, ahead(): return lax.ppermute(x, 'seq', [(i, (i + k) % n) for i in range(n)])  64.4 us
    ppermute x21, starting transfers between devices, ahead(): return lax.ppermute(x, 'seq', [(i, (i + k) % n) for i in range(n)])  40.5 us
    pallas_call x16, Pallas kernels, __call__(): pl.pallas_call(body, out_shape=outs, in_specs=specs, out_specs=out_specs,...  23.3 us
    ppermute x13, waiting for transfers between devices, swap(): return lax.ppermute(x, axis, [(0, 1), (1, 0)])  16.3 us
    ppermute x13, starting transfers between devices, swap(): return lax.ppermute(x, axis, [(0, 1), (1, 0)])  11.5 us
  transfers between devices with their start and end apart: 34, of which 18 were waited for; matrix products, arithmetic and copies ran while one was open for 1% of the time, Pallas kernels for 10%

profile of v3, /device:TPU:0, one launch (start us, length us, event | category | flops | bytes accessed | tf_op | source)
XLA Modules:
  0.0 161.5 jit_solution(13798137787861164910)
XLA Ops:
  0.7 1.1 fusion
  1.8 3.1 %collective-permute-start.1 = (bf16[64,1024]{1,0:T(8,128)(2,1)S(1)}, bf16[64,1024]{1,0:T(8,128)(2,1)S(1)}, u32[]{:S(2)}, u32[]{:S(2)}) collective-permute-start(bf16[64,1024]{1,0:T(8,128)(2,1)S(1)} %get-tuple-element.51), channel_id=1, source_target_pairs={{0,4},{4,8},{8,12},{12,0},{1,5},{5,9},{9,13},{13,1},{2,6},{6,10},{... | collective-permute-start | bytes 393224 | tf_op jit(solution)/shard_map/ppermute | solution.py:61
  4.9 2.1 %collective-permute-start = (bf16[64,1024]{1,0:T(8,128)(2,1)S(1)}, bf16[64,1024]{1,0:T(8,128)(2,1)S(1)}, u32[]{:S(2)}, u32[]{:S(2)}) collective-permute-start(bf16[64,1024]{1,0:T(8,128)(2,1)S(1)} %get-tuple-element.52), channel_id=1, source_target_pairs={{0,12},{4,0},{8,4},{12,8},{1,13},{5,1},{9,5},{13,9},{2,14},{6,2},{... | collective-permute-start | bytes 393224 | tf_op jit(solution)/shard_map/ppermute | solution.py:61
  7.0 0.9 collective-permute-start.2
  7.9 0.9 dynamic-slice_bitcast_fusion.2
  8.9 1.2 dynamic-slice_bitcast_fusion
  10.1 1.1 collective-permute-done.1.refs_1_
  11.3 8.2 %collective-permute-start.7 = (bf16[3,256,128]{2,1,0:T(8,128)(2,1)S(1)}, bf16[3,256,128]{2,1,0:T(8,128)(2,1)S(1)}, u32[]{:S(2)}, u32[]{:S(2)}) collective-permute-start(bf16[3,256,128]{2,1,0:T(8,128)(2,1)S(1)} %pad_maximum_fusion.1), channel_id=1, source_target_pairs={{0,8},{4,12},{8,0},{12,4},{1,9},{5,13},{9,1},{13,5},{2,10},{6,14},... | collective-permute-start | bytes 589832 | tf_op jit(solution)/shard_map/ppermute | solution.py:61
  19.4 1.5 collective-permute-start.4
  20.9 0.5 collective-permute-start.3
  21.4 5.9 %collective-permute-done.2.refs_2_ = bf16[64,1024]{1,0:T(8,128)(2,1)S(1)} collective-permute-done((bf16[64,1024]{1,0:T(8,128)(2,1)S(1)}, bf16[64,1024]{1,0:T(8,128)(2,1)S(1)}, u32[]{:S(2)}, u32[]{:S(2)}) %collective-permute-start.2) | collective-permute-done | bytes 131104 | tf_op jit(solution)/shard_map/ppermute | solution.py:61
  27.4 1.5 collective-permute-start.5
  28.9 3.8 %collective-permute-done.5.refs_5_ = bf16[64,1024]{1,0:T(8,128)(2,1)S(1)} collective-permute-done((bf16[64,1024]{1,0:T(8,128)(2,1)S(1)}, bf16[64,1024]{1,0:T(8,128)(2,1)S(1)}, u32[]{:S(2)}, u32[]{:S(2)}) %collective-permute-start.5) | collective-permute-done | bytes 131104 | tf_op jit(solution)/shard_map/ppermute | solution.py:65
  32.7 0.1 pack.1
  32.8 0.1 collective-permute-start.8
  33.0 7.3 %collective-permute-done.9.refs_4_.refs_5_ = bf16[3,256,128]{2,1,0:T(8,128)(2,1)S(1)} collective-permute-done((bf16[3,256,128]{2,1,0:T(8,128)(2,1)S(1)}, bf16[3,256,128]{2,1,0:T(8,128)(2,1)S(1)}, u32[]{:S(2)}, u32[]{:S(2)}) %collective-permute-start.9) | collective-permute-done | bytes 196640 | tf_op jit(solution)/shard_map/ppermute | solution.py:61
  40.3 1.7 %tangent_term.1 = (bf16[1024,1024]{1,0:T(8,128)(2,1)S(1)}, bf16[1024,128]{1,0:T(8,128)(2,1)S(1)}, bf16[1024,128]{1,0:T(8,128)(2,1)S(1)}, bf16[1024,128]{1,0:T(8,128)(2,1)S(1)}, bf16[1024,128]{1,0:T(8,128)(2,1)S(1)}) custom-call(bf16[256,4096]{1,0:T(8,128)(2,1)S(1)} %copy-done.2, bf16[6,64,1024]{2,1,0:T(8,128)(2,1)S(1)} %get-tuple-element.28.refs_1_.refs_5_, ...), custom_call_target="tpu_custom_call" | custom-call | flops 1 | bytes 1 | tf_op jit(solution)/shard_map/tangent_term/pallas_call | solution.py:33
  42.1 1.6 collective-permute-start.18
  43.7 3.7 %collective-permute-start.15 = (bf16[1024,128]{1,0:T(8,128)(2,1)S(1)}, bf16[1024,128]{1,0:T(8,128)(2,1)S(1)}, u32[]{:S(2)}, u32[]{:S(2)}) collective-permute-start(bf16[1024,128]{1,0:T(8,128)(2,1)S(1)} %get-tuple-element.36), channel_id=1, source_target_pairs={{0,12},{4,0},{8,4},{12,8},{1,13},{5,1},{9,5},{13,9},{2,14},{6,2},{... | collective-permute-start | bytes 786440 | tf_op jit(solution)/shard_map/ppermute | solution.py:61
  47.4 7.8 %attend.1 = (bf16[2,1024,1024]{2,1,0:T(8,128)(2,1)S(1)}, bf16[1024,128]{1,0:T(8,128)(2,1)S(1)}) custom-call(bf16[256,512]{1,0:T(8,128)(2,1)S(1)} %copy-done.5, bf16[256,512]{1,0:T(8,128)(2,1)S(1)} %copy-done.7, bf16[256,512]{1,0:T(8,128)(2,1)S(1)} %copy-done.6, bf16[3,256,128]{2,1,0:T(8,128)(2,1)S(1)} %collective-permute-done.6.refs_7_.refs_3_, ...), custom_call_target="tpu_custom_call" | custom-call | flops 1 | bytes 1 | tf_op jit(solution)/shard_map/attend/pallas_call | solution.py:33
  55.2 0.3 collective-permute-start.11
  55.5 0.5 collective-permute-start.22
  56.1 1.8 %collective-permute-start.14 = (bf16[1024,128]{1,0:T(8,128)(2,1)S(1)}, bf16[1024,128]{1,0:T(8,128)(2,1)S(1)}, u32[]{:S(2)}, u32[]{:S(2)}) collective-permute-start(bf16[1024,128]{1,0:T(8,128)(2,1)S(1)} %add.63.refs_4_), channel_id=1, source_target_pairs={{0,4},{4,8},{8,12},{12,0},{1,5},{5,9},{9,13},{13,1},{2,6},{6,10},{... | collective-permute-start | bytes 786440 | tf_op jit(solution)/shard_map/ppermute | solution.py:61
  57.9 0.2 collective-permute-start.10
  58.1 5.2 %collective-permute-done.11.refs_3_ = bf16[1024,128]{1,0:T(8,128)(2,1)S(1)} collective-permute-done((bf16[1024,128]{1,0:T(8,128)(2,1)S(1)}, bf16[1024,128]{1,0:T(8,128)(2,1)S(1)}, u32[]{:S(2)}, u32[]{:S(2)}) %collective-permute-start.11) | collective-permute-done | bytes 262176 | tf_op jit(solution)/shard_map/ppermute | solution.py:61
  63.3 3.3 %collective-permute-start.12 = (bf16[1024,128]{1,0:T(8,128)(2,1)S(1)}, bf16[1024,128]{1,0:T(8,128)(2,1)S(1)}, u32[]{:S(2)}, u32[]{:S(2)}) collective-permute-start(bf16[1024,128]{1,0:T(8,128)(2,1)S(1)} %collective-permute-done.11.refs_3_), channel_id=1, source_target_pairs={{0,12},{4,0},{8,4},{12,8},{1,13},{5,1},{9,5},{13,9},{2,14},{6,2},{... | collective-permute-start | bytes 786440 | tf_op jit(solution)/shard_map/ppermute | solution.py:61
  66.6 3.5 %collective-permute-done.14.refs_1_ = bf16[1024,128]{1,0:T(8,128)(2,1)S(1)} collective-permute-done((bf16[1024,128]{1,0:T(8,128)(2,1)S(1)}, bf16[1024,128]{1,0:T(8,128)(2,1)S(1)}, u32[]{:S(2)}, u32[]{:S(2)}) %collective-permute-start.14) | collective-permute-done | bytes 262176 | tf_op jit(solution)/shard_map/ppermute | solution.py:61
  70.2 1.5 attend_tan.1
  71.6 1.5 collective-permute-start.16
  73.2 2.5 %collective-permute-done.10.refs_2_.refs_1_ = bf16[1024,128]{1,0:T(8,128)(2,1)S(1)} collective-permute-done((bf16[1024,128]{1,0:T(8,128)(2,1)S(1)}, bf16[1024,128]{1,0:T(8,128)(2,1)S(1)}, u32[]{:S(2)}, u32[]{:S(2)}) %collective-permute-start.10) | collective-permute-done | bytes 262176 | tf_op jit(solution)/shard_map/ppermute | solution.py:61
  75.7 5.3 %collective-permute-done.16.refs_1_ = bf16[512,128]{1,0:T(8,128)(2,1)S(1)} collective-permute-done((bf16[512,128]{1,0:T(8,128)(2,1)S(1)}, bf16[512,128]{1,0:T(8,128)(2,1)S(1)}, u32[]{:S(2)}, u32[]{:S(2)}) %collective-permute-start.16) | collective-permute-done | bytes 131104 | tf_op jit(solution)/shard_map/ppermute | solution.py:65
  81.1 0.2 cut_rows.1.refs_7_
  81.2 1.6 collective-permute-start.17
  82.8 1.5 collective-permute-start.23
  84.3 3.5 %collective-permute-start.20 = (bf16[512,256]{1,0:T(8,128)(2,1)S(1)}, bf16[512,256]{1,0:T(8,128)(2,1)S(1)}, u32[]{:S(2)}, u32[]{:S(2)}) collective-permute-start(bf16[512,256]{1,0:T(8,128)(2,1)S(1)} %join.1.refs_4_.refs_1_), channel_id=1, source_target_pairs={{0,12},{4,0},{8,4},{12,8},{1,13},{5,1},{9,5},{13,9},{2,14},{6,2},{... | collective-permute-start | bytes 786440 | tf_op jit(solution)/shard_map/ppermute | solution.py:61
  87.8 6.8 %collective-permute-done.20.refs_4_ = bf16[512,256]{1,0:T(8,128)(2,1)S(1)} collective-permute-done((bf16[512,256]{1,0:T(8,128)(2,1)S(1)}, bf16[512,256]{1,0:T(8,128)(2,1)S(1)}, u32[]{:S(2)}, u32[]{:S(2)}) %collective-permute-start.20) | collective-permute-done | bytes 262176 | tf_op jit(solution)/shard_map/ppermute | solution.py:61
  94.5 4.3 %collective-permute-start.21 = (bf16[512,256]{1,0:T(8,128)(2,1)S(1)}, bf16[512,256]{1,0:T(8,128)(2,1)S(1)}, u32[]{:S(2)}, u32[]{:S(2)}) collective-permute-start(bf16[512,256]{1,0:T(8,128)(2,1)S(1)} %collective-permute-done.20.refs_4_), channel_id=1, source_target_pairs={{0,12},{4,0},{8,4},{12,8},{1,13},{5,1},{9,5},{13,9},{2,14},{6,2},{... | collective-permute-start | bytes 786440 | tf_op jit(solution)/shard_map/ppermute | solution.py:61
  98.9 1.3 out_term.1.refs_0_.refs_8_
  100.2 0.8 collective-permute-done.19.refs_2_
  101.0 1.7 %collective-permute-done.21.refs_3_ = bf16[512,256]{1,0:T(8,128)(2,1)S(1)} collective-permute-done((bf16[512,256]{1,0:T(8,128)(2,1)S(1)}, bf16[512,256]{1,0:T(8,128)(2,1)S(1)}, u32[]{:S(2)}, u32[]{:S(2)}) %collective-permute-start.21) | collective-permute-done | bytes 262176 | tf_op jit(solution)/shard_map/ppermute | solution.py:61
  102.7 1.3 out_sum.1.refs_0_.refs_5_
  104.1 0.1 collective-permute-start.24
  104.2 2.6 %collective-permute-done.24.refs_1_ = bf16[512,1024]{1,0:T(8,128)(2,1)S(1)} collective-permute-done((bf16[512,1024]{1,0:T(8,128)(2,1)S(1)}, bf16[512,1024]{1,0:T(8,128)(2,1)S(1)}, u32[]{:S(2)}, u32[]{:S(2)}) %collective-permute-start.24) | collective-permute-done | bytes 1048608 | tf_op jit(solution)/shard_map/ppermute | solution.py:65
  106.8 1.7 %grad_term.1 = (bf16[512,1024]{1,0:T(8,128)(2,1)S(1)}, bf16[256,1024]{1,0:T(8,128)(2,1)S(1)}, bf16[512,256]{1,0:T(8,128)(2,1)S(1)}, bf16[512,256]{1,0:T(8,128)(2...) custom-call(bf16[512,1024]{1,0:T(8,128)(2,1)S(1)} %out_sum.1.refs_0_.refs_5_, ...), custom_call_target="tpu_custom_call" | custom-call | flops 1 | bytes 1 | tf_op jit(solution)/shard_map/grad_term/pallas_call | solution.py:33
  108.5 0.5 collective-permute-start.27
  109.0 0.5 collective-permute-start.25
  109.5 3.9 %collective-permute-start.29 = (bf16[512,256]{1,0:T(8,128)(2,1)S(1)}, bf16[512,256]{1,0:T(8,128)(2,1)S(1)}, u32[]{:S(2)}, u32[]{:S(2)}) collective-permute-start(bf16[512,256]{1,0:T(8,128)(2,1)S(1)} %get-tuple-element.47), channel_id=1, source_target_pairs={{0,12},{4,0},{8,4},{12,8},{1,13},{5,1},{9,5},{13,9},{2,14},{6,2},{... | collective-permute-start | bytes 786440 | tf_op jit(solution)/shard_map/ppermute | solution.py:61
  113.4 6.5 %collective-permute-done.27.refs_0_ = bf16[512,256]{1,0:T(8,128)(2,1)S(1)} collective-permute-done((bf16[512,256]{1,0:T(8,128)(2,1)S(1)}, bf16[512,256]{1,0:T(8,128)(2,1)S(1)}, u32[]{:S(2)}, u32[]{:S(2)}) %collective-permute-start.27) | collective-permute-done | bytes 262176 | tf_op jit(solution)/shard_map/ppermute | solution.py:61
  120.0 2.1 %collective-permute-start.28 = (bf16[512,256]{1,0:T(8,128)(2,1)S(1)}, bf16[512,256]{1,0:T(8,128)(2,1)S(1)}, u32[]{:S(2)}, u32[]{:S(2)}) collective-permute-start(bf16[512,256]{1,0:T(8,128)(2,1)S(1)} %add.64.refs_3_), channel_id=1, source_target_pairs={{0,4},{4,8},{8,12},{12,0},{1,5},{5,9},{9,13},{13,1},{2,6},{6,10},{... | collective-permute-start | bytes 786440 | tf_op jit(solution)/shard_map/ppermute | solution.py:61
  122.1 0.9 collective-permute-done.29.refs_2_
  123.0 10.0 %collective-permute-done.28.refs_1_ = bf16[512,256]{1,0:T(8,128)(2,1)S(1)} collective-permute-done((bf16[512,256]{1,0:T(8,128)(2,1)S(1)}, bf16[512,256]{1,0:T(8,128)(2,1)S(1)}, u32[]{:S(2)}, u32[]{:S(2)}) %collective-permute-start.28) | collective-permute-done | bytes 262176 | tf_op jit(solution)/shard_map/ppermute | solution.py:61
  133.0 0.1 add_grad.1
  133.1 0.6 collective-permute-start.30
  133.7 4.4 %collective-permute-done.30.refs_1_ = bf16[512,128]{1,0:T(8,128)(2,1)S(1)} collective-permute-done((bf16[512,128]{1,0:T(8,128)(2,1)S(1)}, bf16[512,128]{1,0:T(8,128)(2,1)S(1)}, u32[]{:S(2)}, u32[]{:S(2)}) %collective-permute-start.30) | collective-permute-done | bytes 131104 | tf_op jit(solution)/shard_map/ppermute | solution.py:65
  138.1 2.1 %key_grad.1.refs_7_.refs_1_ = bf16[1024,128]{1,0:T(8,128)(2,1)S(1)} custom-call(bf16[512,128]{1,0:T(8,128)(2,1)S(1)} %get-tuple-element.48.refs_0_.refs_3_, bf16[512,128]{1,0:T(8,128)(2,1)S(1)} %collective-permute-done.30.refs_1_, bf16[2,1024,1024]{2,1,0:T(8,128)(2,1)S(1)} %get-tuple-element.35.refs_2_.refs_3_, ...), custom_call_target="tpu_custom_call" | custom-call | flops 1 | bytes 1 | tf_op jit(solution)/shard_map/key_grad/pallas_call | solution.py:33
  140.2 1.8 %collective-permute-start.32 = (bf16[1024,128]{1,0:T(8,128)(2,1)S(1)}, bf16[1024,128]{1,0:T(8,128)(2,1)S(1)}, u32[]{:S(2)}, u32[]{:S(2)}) collective-permute-start(bf16[1024,128]{1,0:T(8,128)(2,1)S(1)} %key_grad.1.refs_7_.refs_1_), channel_id=1, source_target_pairs={{0,12},{4,0},{8,4},{12,8},{1,13},{5,1},{9,5},{13,9},{2,14},{6,2},{... | collective-permute-start | bytes 786440 | tf_op jit(solution)/shard_map/ppermute | solution.py:61
  142.0 0.3 collective-permute-start.31
  142.3 10.5 %collective-permute-done.32.refs_4_ = bf16[1024,128]{1,0:T(8,128)(2,1)S(1)} collective-permute-done((bf16[1024,128]{1,0:T(8,128)(2,1)S(1)}, bf16[1024,128]{1,0:T(8,128)(2,1)S(1)}, u32[]{:S(2)}, u32[]{:S(2)}) %collective-permute-start.32) | collective-permute-done | bytes 262176 | tf_op jit(solution)/shard_map/ppermute | solution.py:61
  152.8 0.4 collective-permute-start.33
  153.2 2.5 %out_product.1.refs_1_ = bf16[512,1024]{1,0:T(8,128)(2,1)} custom-call(bf16[1024,128]{1,0:T(8,128)(2,1)S(1)} %get-tuple-element.31.refs_0_, bf16[1024,128]{1,0:T(8,128)(2,1)S(1)} %collective-permute-done.10.refs_2_.refs_1_, bf16[1024,128]{1,0:T(8,128)(2,1)S(1)} %collective-permute-done.12.refs_2_, bf16[1024,128]{1,0:T(8,128)(2,1)S(1)} %collective-permute-done.11.refs_3_, ...), custom_call_target="tpu_custom_call" | custom-call | flops 1 | bytes 1 | tf_op jit(solution)/shard_map/out_product/pallas_call | solution.py:33
  155.7 1.2 copy-done.1
  156.9 0.6 flip.1.refs_0_.refs_5_
  157.6 1.6 collective-permute-done.33.refs_3_
  159.2 2.3 %value_product.1 = bf16[1024,512]{1,0:T(8,128)(2,1)} custom-call(bf16[1024,1024]{1,0:T(8,128)(2,1)S(1)} %flip.1.refs_0_.refs_5_, bf16[1024,128]{1,0:T(8,128)(2,1)S(1)} %key_grad.1.refs_7_.refs_1_, bf16[1024,128]{1,0:T(8,128)(2,1)S(1)} %collective-permute-done.31.refs_2_, bf16[1024,128]{1,0:T(8,128)(2,1)S(1)} %collective-permute-done.33.refs_3_, ...), custom_call_target="tpu_custom_call" | custom-call | flops 1 | bytes 1 | tf_op jit(solution)/shard_map/value_product/pallas_call | solution.py:33
  (42 shorter events, 0.5 us)
Async XLA Ops:
  0.6 32.1 %copy-start = (bf16[512,1024]{1,0:T(8,128)(2,1)S(1)}, bf16[512,1024]{1,0:T(8,128)(2,1)}, u32[]{:S(2)}) copy-start(bf16[512,1024]{1,0:T(8,128)(2,1)} %refs_2_.3) | copy-start | bytes 3145732
  1.8 9.4 %collective-permute-start.1 = (bf16[64,1024]{1,0:T(8,128)(2,1)S(1)}, bf16[64,1024]{1,0:T(8,128)(2,1)S(1)}, u32[]{:S(2)}, u32[]{:S(2)}) collective-permute-start(bf16[64,1024]{1,0:T(8,128)(2,1)S(1)} %get-tuple-element.51), channel_id=1, source_target_pairs={{0,4},{4,8},{8,12},{12,0},{1,5},{5,9},{9,13},{13,1},{2,6},{6,10},{... | collective-permute-start | bytes 393224 | tf_op jit(solution)/shard_map/ppermute | solution.py:61
  4.9 16.0 %collective-permute-start = (bf16[64,1024]{1,0:T(8,128)(2,1)S(1)}, bf16[64,1024]{1,0:T(8,128)(2,1)S(1)}, u32[]{:S(2)}, u32[]{:S(2)}) collective-permute-start(bf16[64,1024]{1,0:T(8,128)(2,1)S(1)} %get-tuple-element.52), channel_id=1, source_target_pairs={{0,12},{4,0},{8,4},{12,8},{1,13},{5,1},{9,5},{13,9},{2,14},{6,2},{... | collective-permute-start | bytes 393224 | tf_op jit(solution)/shard_map/ppermute | solution.py:61
  7.0 20.4 %collective-permute-start.2 = (bf16[64,1024]{1,0:T(8,128)(2,1)S(1)}, bf16[64,1024]{1,0:T(8,128)(2,1)S(1)}, u32[]{:S(2)}, u32[]{:S(2)}) collective-permute-start(bf16[64,1024]{1,0:T(8,128)(2,1)S(1)} %get-tuple-element.50), channel_id=1, source_target_pairs={{0,8},{4,12},{8,0},{12,4},{1,9},{5,13},{9,1},{13,5},{2,10},{6,14},... | collective-permute-start | bytes 393224 | tf_op jit(solution)/shard_map/ppermute | solution.py:61
  8.9 31.5 %copy-start.2 = (bf16[256,4096]{1,0:T(8,128)(2,1)S(1)}, bf16[256,4096]{1,0:T(8,128)(2,1)}, u32[]{:S(2)}) copy-start(bf16[256,4096]{1,0:T(8,128)(2,1)} %refs_0_.2) | copy-start | bytes 6291460
  8.9 31.5 %copy-start.3 = (bf16[1024,512]{1,0:T(8,128)(2,1)S(1)}, bf16[1024,512]{1,0:T(8,128)(2,1)}, u32[]{:S(2)}) copy-start(bf16[1024,512]{1,0:T(8,128)(2,1)} %refs_3_.1) | copy-start | bytes 3145732
  11.3 21.4 %collective-permute-start.7 = (bf16[3,256,128]{2,1,0:T(8,128)(2,1)S(1)}, bf16[3,256,128]{2,1,0:T(8,128)(2,1)S(1)}, u32[]{:S(2)}, u32[]{:S(2)}) collective-permute-start(bf16[3,256,128]{2,1,0:T(8,128)(2,1)S(1)} %pad_maximum_fusion.1), channel_id=1, source_target_pairs={{0,8},{4,12},{8,0},{12,4},{1,9},{5,13},{9,1},{13,5},{2,10},{6,14},... | collective-permute-start | bytes 589832 | tf_op jit(solution)/shard_map/ppermute | solution.py:61
  19.4 13.3 %collective-permute-start.6 = (bf16[3,256,128]{2,1,0:T(8,128)(2,1)S(1)}, bf16[3,256,128]{2,1,0:T(8,128)(2,1)S(1)}, u32[]{:S(2)}, u32[]{:S(2)}) collective-permute-start(bf16[3,256,128]{2,1,0:T(8,128)(2,1)S(1)} %pad_maximum_fusion), channel_id=1, source_target_pairs={{0,4},{4,8},{8,12},{12,0},{1,5},{5,9},{9,13},{13,1},{2,6},{6,10},{... | collective-permute-start | bytes 589832 | tf_op jit(solution)/shard_map/ppermute | solution.py:61
  19.4 9.5 %collective-permute-start.4 = (bf16[64,1024]{1,0:T(8,128)(2,1)S(1)}, bf16[64,1024]{1,0:T(8,128)(2,1)S(1)}, u32[]{:S(2)}, u32[]{:S(2)}) collective-permute-start(bf16[64,1024]{1,0:T(8,128)(2,1)S(1)} %collective-permute-done.1.refs_1_), channel_id=1, source_target_pairs={{0,2},{2,0},{1,3},{3,1},{4,6},{6,4},{5,7},{7,5},{8,10},{10,8},{9,1... | collective-permute-start | bytes 393224 | tf_op jit(solution)/shard_map/ppermute | solution.py:65
  20.9 8.0 %collective-permute-start.3 = (bf16[64,1024]{1,0:T(8,128)(2,1)S(1)}, bf16[64,1024]{1,0:T(8,128)(2,1)S(1)}, u32[]{:S(2)}, u32[]{:S(2)}) collective-permute-start(bf16[64,1024]{1,0:T(8,128)(2,1)S(1)} %collective-permute-done.refs_0_), channel_id=1, source_target_pairs={{0,2},{2,0},{1,3},{3,1},{4,6},{6,4},{5,7},{7,5},{8,10},{10,8},{9,1... | collective-permute-start | bytes 393224 | tf_op jit(solution)/shard_map/ppermute | solution.py:65
  27.4 5.3 %collective-permute-start.5 = (bf16[64,1024]{1,0:T(8,128)(2,1)S(1)}, bf16[64,1024]{1,0:T(8,128)(2,1)S(1)}, u32[]{:S(2)}, u32[]{:S(2)}) collective-permute-start(bf16[64,1024]{1,0:T(8,128)(2,1)S(1)} %collective-permute-done.2.refs_2_), channel_id=1, source_target_pairs={{0,2},{2,0},{1,3},{3,1},{4,6},{6,4},{5,7},{7,5},{8,10},{10,8},{9,1... | collective-permute-start | bytes 393224 | tf_op jit(solution)/shard_map/ppermute | solution.py:65
  32.8 7.5 %collective-permute-start.8 = (bf16[6,64,1024]{2,1,0:T(8,128)(2,1)S(1)}, bf16[6,64,1024]{2,1,0:T(8,128)(2,1)S(1)}, u32[]{:S(2)}, u32[]{:S(2)}) collective-permute-start(bf16[6,64,1024]{2,1,0:T(8,128)(2,1)S(1)} %get-tuple-element.28.refs_1_.refs_5_), channel_id=1, source_target_pairs={{0,1},{1,0},{2,3},{3,2},{4,5},{5,4},{6,7},{7,6},{8,9},{9,8},{10,11... | collective-permute-start | bytes 2359304 | tf_op jit(solution)/shard_map/ppermute | solution.py:65
  32.9 9.2 %copy-start.4 = (bf16[512,1024]{1,0:T(8,128)(2,1)S(1)}, bf16[512,1024]{1,0:T(8,128)(2,1)}, u32[]{:S(2)}) copy-start(bf16[512,1024]{1,0:T(8,128)(2,1)} %refs_5_.2) | copy-start | bytes 3145732
  32.9 14.5 %copy-start.5 = (bf16[256,512]{1,0:T(8,128)(2,1)S(1)}, bf16[256,512]{1,0:T(8,128)(2,1)}, u32[]{:S(2)}) copy-start(bf16[256,512]{1,0:T(8,128)(2,1)} %refs_0_.3) | copy-start | bytes 786436
  33.0 14.5 %copy-start.6 = (bf16[256,512]{1,0:T(8,128)(2,1)S(1)}, bf16[256,512]{1,0:T(8,128)(2,1)}, u32[]{:S(2)}) copy-start(bf16[256,512]{1,0:T(8,128)(2,1)} %refs_2_.2) | copy-start | bytes 786436
  33.0 14.5 %copy-start.7 = (bf16[256,512]{1,0:T(8,128)(2,1)S(1)}, bf16[256,512]{1,0:T(8,128)(2,1)}, u32[]{:S(2)}) copy-start(bf16[256,512]{1,0:T(8,128)(2,1)} %refs_1_.1) | copy-start | bytes 786436
  33.0 7.3 %collective-permute-start.9 = (bf16[3,256,128]{2,1,0:T(8,128)(2,1)S(1)}, bf16[3,256,128]{2,1,0:T(8,128)(2,1)S(1)}, u32[]{:S(2)}, u32[]{:S(2)}) collective-permute-start(bf16[3,256,128]{2,1,0:T(8,128)(2,1)S(1)} %pad_maximum_fusion.2), channel_id=1, source_target_pairs={{0,12},{4,0},{8,4},{12,8},{1,13},{5,1},{9,5},{13,9},{2,14},{6,2},{... | collective-permute-start | bytes 589832 | tf_op jit(solution)/shard_map/ppermute | solution.py:61
  42.0 14.0 %collective-permute-start.13 = (bf16[1024,128]{1,0:T(8,128)(2,1)S(1)}, bf16[1024,128]{1,0:T(8,128)(2,1)S(1)}, u32[]{:S(2)}, u32[]{:S(2)}) collective-permute-start(bf16[1024,128]{1,0:T(8,128)(2,1)S(1)} %get-tuple-element.33), channel_id=1, source_target_pairs={{0,4},{4,8},{8,12},{12,0},{1,5},{5,9},{9,13},{13,1},{2,6},{6,10},{... | collective-permute-start | bytes 786440 | tf_op jit(solution)/shard_map/ppermute | solution.py:61
  42.1 56.7 %collective-permute-start.18 = (bf16[512,1024]{1,0:T(8,128)(2,1)S(1)}, bf16[512,1024]{1,0:T(8,128)(2,1)S(1)}, u32[]{:S(2)}, u32[]{:S(2)}) collective-permute-start(bf16[512,1024]{1,0:T(8,128)(2,1)S(1)} %copy-done.4), channel_id=1, source_target_pairs={{0,2},{2,0},{1,3},{3,1},{4,6},{6,4},{5,7},{7,5},{8,10},{10,8},{9,1... | collective-permute-start | bytes 3145736 | tf_op jit(solution)/shard_map/ppermute | solution.py:65
  43.7 14.3 %collective-permute-start.15 = (bf16[1024,128]{1,0:T(8,128)(2,1)S(1)}, bf16[1024,128]{1,0:T(8,128)(2,1)S(1)}, u32[]{:S(2)}, u32[]{:S(2)}) collective-permute-start(bf16[1024,128]{1,0:T(8,128)(2,1)S(1)} %get-tuple-element.36), channel_id=1, source_target_pairs={{0,12},{4,0},{8,4},{12,8},{1,13},{5,1},{9,5},{13,9},{2,14},{6,2},{... | collective-permute-start | bytes 786440 | tf_op jit(solution)/shard_map/ppermute | solution.py:61
  55.2 8.1 %collective-permute-start.11 = (bf16[1024,128]{1,0:T(8,128)(2,1)S(1)}, bf16[1024,128]{1,0:T(8,128)(2,1)S(1)}, u32[]{:S(2)}, u32[]{:S(2)}) collective-permute-start(bf16[1024,128]{1,0:T(8,128)(2,1)S(1)} %get-tuple-element.31.refs_0_), channel_id=1, source_target_pairs={{0,12},{4,0},{8,4},{12,8},{1,13},{5,1},{9,5},{13,9},{2,14},{6,2},{... | collective-permute-start | bytes 786440 | tf_op jit(solution)/shard_map/ppermute | solution.py:61
  55.5 27.2 %collective-permute-start.22 = (bf16[256,1024]{1,0:T(8,128)(2,1)S(1)}, bf16[256,1024]{1,0:T(8,128)(2,1)S(1)}, u32[]{:S(2)}, u32[]{:S(2)}) collective-permute-start(bf16[256,1024]{1,0:T(8,128)(2,1)S(1)} %get-tuple-element.41), channel_id=1, source_target_pairs={{0,2},{2,0},{1,3},{3,1},{4,6},{6,4},{5,7},{7,5},{8,10},{10,8},{9,1... | collective-permute-start | bytes 1572872 | tf_op jit(solution)/shard_map/ppermute | solution.py:65
  56.1 14.0 %collective-permute-start.14 = (bf16[1024,128]{1,0:T(8,128)(2,1)S(1)}, bf16[1024,128]{1,0:T(8,128)(2,1)S(1)}, u32[]{:S(2)}, u32[]{:S(2)}) collective-permute-start(bf16[1024,128]{1,0:T(8,128)(2,1)S(1)} %add.63.refs_4_), channel_id=1, source_target_pairs={{0,4},{4,8},{8,12},{12,0},{1,5},{5,9},{9,13},{13,1},{2,6},{6,10},{... | collective-permute-start | bytes 786440 | tf_op jit(solution)/shard_map/ppermute | solution.py:61
  57.9 17.7 %collective-permute-start.10 = (bf16[1024,128]{1,0:T(8,128)(2,1)S(1)}, bf16[1024,128]{1,0:T(8,128)(2,1)S(1)}, u32[]{:S(2)}, u32[]{:S(2)}) collective-permute-start(bf16[1024,128]{1,0:T(8,128)(2,1)S(1)} %get-tuple-element.31.refs_0_), channel_id=1, source_target_pairs={{0,4},{4,8},{8,12},{12,0},{1,5},{5,9},{9,13},{13,1},{2,6},{6,10},{... | collective-permute-start | bytes 786440 | tf_op jit(solution)/shard_map/ppermute | solution.py:61
  63.3 17.8 %collective-permute-start.12 = (bf16[1024,128]{1,0:T(8,128)(2,1)S(1)}, bf16[1024,128]{1,0:T(8,128)(2,1)S(1)}, u32[]{:S(2)}, u32[]{:S(2)}) collective-permute-start(bf16[1024,128]{1,0:T(8,128)(2,1)S(1)} %collective-permute-done.11.refs_3_), channel_id=1, source_target_pairs={{0,12},{4,0},{8,4},{12,8},{1,13},{5,1},{9,5},{13,9},{2,14},{6,2},{... | collective-permute-start | bytes 786440 | tf_op jit(solution)/shard_map/ppermute | solution.py:61
  71.6 9.4 %collective-permute-start.16 = (bf16[512,128]{1,0:T(8,128)(2,1)S(1)}, bf16[512,128]{1,0:T(8,128)(2,1)S(1)}, u32[]{:S(2)}, u32[]{:S(2)}) collective-permute-start(bf16[512,128]{1,0:T(8,128)(2,1)S(1)} %get-tuple-element.38), channel_id=1, source_target_pairs={{0,2},{2,0},{1,3},{3,1},{4,6},{6,4},{5,7},{7,5},{8,10},{10,8},{9,1... | collective-permute-start | bytes 393224 | tf_op jit(solution)/shard_map/ppermute | solution.py:65
  81.2 17.6 %collective-permute-start.17 = (bf16[512,512]{1,0:T(8,128)(2,1)S(1)}, bf16[512,512]{1,0:T(8,128)(2,1)S(1)}, u32[]{:S(2)}, u32[]{:S(2)}) collective-permute-start(bf16[512,512]{1,0:T(8,128)(2,1)S(1)} %cut_rows.1.refs_7_), channel_id=1, source_target_pairs={{0,2},{2,0},{1,3},{3,1},{4,6},{6,4},{5,7},{7,5},{8,10},{10,8},{9,1... | collective-permute-start | bytes 1572872 | tf_op jit(solution)/shard_map/ppermute | solution.py:65
  82.8 18.2 %collective-permute-start.23 = (bf16[256,1024]{1,0:T(8,128)(2,1)S(1)}, bf16[256,1024]{1,0:T(8,128)(2,1)S(1)}, u32[]{:S(2)}, u32[]{:S(2)}) collective-permute-start(bf16[256,1024]{1,0:T(8,128)(2,1)S(1)} %collective-permute-done.22.refs_6_.refs_3_), channel_id=1, source_target_pairs={{0,16},{16,0},{1,17},{17,1},{2,18},{18,2},{3,19},{19,3},{4,20},{20... | collective-permute-start | bytes 1572872 | tf_op jit(solution)/shard_map/ppermute | solution.py:65
  84.3 10.2 %collective-permute-start.20 = (bf16[512,256]{1,0:T(8,128)(2,1)S(1)}, bf16[512,256]{1,0:T(8,128)(2,1)S(1)}, u32[]{:S(2)}, u32[]{:S(2)}) collective-permute-start(bf16[512,256]{1,0:T(8,128)(2,1)S(1)} %join.1.refs_4_.refs_1_), channel_id=1, source_target_pairs={{0,12},{4,0},{8,4},{12,8},{1,13},{5,1},{9,5},{13,9},{2,14},{6,2},{... | collective-permute-start | bytes 786440 | tf_op jit(solution)/shard_map/ppermute | solution.py:61
  87.8 13.2 %collective-permute-start.19 = (bf16[512,256]{1,0:T(8,128)(2,1)S(1)}, bf16[512,256]{1,0:T(8,128)(2,1)S(1)}, u32[]{:S(2)}, u32[]{:S(2)}) collective-permute-start(bf16[512,256]{1,0:T(8,128)(2,1)S(1)} %join.1.refs_4_.refs_1_), channel_id=1, source_target_pairs={{0,4},{4,8},{8,12},{12,0},{1,5},{5,9},{9,13},{13,1},{2,6},{6,10},{... | collective-permute-start | bytes 786440 | tf_op jit(solution)/shard_map/ppermute | solution.py:61
  94.5 8.2 %collective-permute-start.21 = (bf16[512,256]{1,0:T(8,128)(2,1)S(1)}, bf16[512,256]{1,0:T(8,128)(2,1)S(1)}, u32[]{:S(2)}, u32[]{:S(2)}) collective-permute-start(bf16[512,256]{1,0:T(8,128)(2,1)S(1)} %collective-permute-done.20.refs_4_), channel_id=1, source_target_pairs={{0,12},{4,0},{8,4},{12,8},{1,13},{5,1},{9,5},{13,9},{2,14},{6,2},{... | collective-permute-start | bytes 786440 | tf_op jit(solution)/shard_map/ppermute | solution.py:61
  104.1 2.7 %collective-permute-start.24 = (bf16[512,1024]{1,0:T(8,128)(2,1)S(1)}, bf16[512,1024]{1,0:T(8,128)(2,1)S(1)}, u32[]{:S(2)}, u32[]{:S(2)}) collective-permute-start(bf16[512,1024]{1,0:T(8,128)(2,1)S(1)} %out_sum.1.refs_0_.refs_5_), channel_id=1, source_target_pairs={{0,1},{1,0},{2,3},{3,2},{4,5},{5,4},{6,7},{7,6},{8,9},{9,8},{10,11... | collective-permute-start | bytes 3145736 | tf_op jit(solution)/shard_map/ppermute | solution.py:65
  108.5 11.5 %collective-permute-start.27 = (bf16[512,256]{1,0:T(8,128)(2,1)S(1)}, bf16[512,256]{1,0:T(8,128)(2,1)S(1)}, u32[]{:S(2)}, u32[]{:S(2)}) collective-permute-start(bf16[512,256]{1,0:T(8,128)(2,1)S(1)} %get-tuple-element.45), channel_id=1, source_target_pairs={{0,4},{4,8},{8,12},{12,0},{1,5},{5,9},{9,13},{13,1},{2,6},{6,10},{... | collective-permute-start | bytes 786440 | tf_op jit(solution)/shard_map/ppermute | solution.py:61
  109.0 24.7 %collective-permute-start.25 = (bf16[256,1024]{1,0:T(8,128)(2,1)S(1)}, bf16[256,1024]{1,0:T(8,128)(2,1)S(1)}, u32[]{:S(2)}, u32[]{:S(2)}) collective-permute-start(bf16[256,1024]{1,0:T(8,128)(2,1)S(1)} %get-tuple-element.43), channel_id=1, source_target_pairs={{0,2},{2,0},{1,3},{3,1},{4,6},{6,4},{5,7},{7,5},{8,10},{10,8},{9,1... | collective-permute-start | bytes 1572872 | tf_op jit(solution)/shard_map/ppermute | solution.py:65
  109.5 13.5 %collective-permute-start.29 = (bf16[512,256]{1,0:T(8,128)(2,1)S(1)}, bf16[512,256]{1,0:T(8,128)(2,1)S(1)}, u32[]{:S(2)}, u32[]{:S(2)}) collective-permute-start(bf16[512,256]{1,0:T(8,128)(2,1)S(1)} %get-tuple-element.47), channel_id=1, source_target_pairs={{0,12},{4,0},{8,4},{12,8},{1,13},{5,1},{9,5},{13,9},{2,14},{6,2},{... | collective-permute-start | bytes 786440 | tf_op jit(solution)/shard_map/ppermute | solution.py:61
  120.0 13.0 %collective-permute-start.28 = (bf16[512,256]{1,0:T(8,128)(2,1)S(1)}, bf16[512,256]{1,0:T(8,128)(2,1)S(1)}, u32[]{:S(2)}, u32[]{:S(2)}) collective-permute-start(bf16[512,256]{1,0:T(8,128)(2,1)S(1)} %add.64.refs_3_), channel_id=1, source_target_pairs={{0,4},{4,8},{8,12},{12,0},{1,5},{5,9},{9,13},{13,1},{2,6},{6,10},{... | collective-permute-start | bytes 786440 | tf_op jit(solution)/shard_map/ppermute | solution.py:61
  133.1 5.0 %collective-permute-start.30 = (bf16[512,128]{1,0:T(8,128)(2,1)S(1)}, bf16[512,128]{1,0:T(8,128)(2,1)S(1)}, u32[]{:S(2)}, u32[]{:S(2)}) collective-permute-start(bf16[512,128]{1,0:T(8,128)(2,1)S(1)} %get-tuple-element.49), channel_id=1, source_target_pairs={{0,2},{2,0},{1,3},{3,1},{4,6},{6,4},{5,7},{7,5},{8,10},{10,8},{9,1... | collective-permute-start | bytes 393224 | tf_op jit(solution)/shard_map/ppermute | solution.py:65
  133.7 19.5 %collective-permute-start.26 = (bf16[256,1024]{1,0:T(8,128)(2,1)S(1)}, bf16[256,1024]{1,0:T(8,128)(2,1)S(1)}, u32[]{:S(2)}, u32[]{:S(2)}) collective-permute-start(bf16[256,1024]{1,0:T(8,128)(2,1)S(1)} %collective-permute-done.25.refs_5_), channel_id=1, source_target_pairs={{0,1},{1,0},{2,3},{3,2},{4,5},{5,4},{6,7},{7,6},{8,9},{9,8},{10,11... | collective-permute-start | bytes 1572872 | tf_op jit(solution)/shard_map/ppermute | solution.py:65
  140.2 12.6 %collective-permute-start.32 = (bf16[1024,128]{1,0:T(8,128)(2,1)S(1)}, bf16[1024,128]{1,0:T(8,128)(2,1)S(1)}, u32[]{:S(2)}, u32[]{:S(2)}) collective-permute-start(bf16[1024,128]{1,0:T(8,128)(2,1)S(1)} %key_grad.1.refs_7_.refs_1_), channel_id=1, source_target_pairs={{0,12},{4,0},{8,4},{12,8},{1,13},{5,1},{9,5},{13,9},{2,14},{6,2},{... | collective-permute-start | bytes 786440 | tf_op jit(solution)/shard_map/ppermute | solution.py:61
  142.0 15.6 %collective-permute-start.31 = (bf16[1024,128]{1,0:T(8,128)(2,1)S(1)}, bf16[1024,128]{1,0:T(8,128)(2,1)S(1)}, u32[]{:S(2)}, u32[]{:S(2)}) collective-permute-start(bf16[1024,128]{1,0:T(8,128)(2,1)S(1)} %key_grad.1.refs_7_.refs_1_), channel_id=1, source_target_pairs={{0,4},{4,8},{8,12},{12,0},{1,5},{5,9},{9,13},{13,1},{2,6},{6,10},{... | collective-permute-start | bytes 786440 | tf_op jit(solution)/shard_map/ppermute | solution.py:61
  152.8 6.4 %collective-permute-start.33 = (bf16[1024,128]{1,0:T(8,128)(2,1)S(1)}, bf16[1024,128]{1,0:T(8,128)(2,1)S(1)}, u32[]{:S(2)}, u32[]{:S(2)}) collective-permute-start(bf16[1024,128]{1,0:T(8,128)(2,1)S(1)} %collective-permute-done.32.refs_4_), channel_id=1, source_target_pairs={{0,12},{4,0},{8,4},{12,8},{1,13},{5,1},{9,5},{13,9},{2,14},{6,2},{... | collective-permute-start | bytes 786440 | tf_op jit(solution)/shard_map/ppermute | solution.py:61
  155.7 1.2 copy-start.1

commit v4 on v3

--- a/solution.py
+++ b/solution.py
@@ -322,7 +322,7 @@
     feats, *terms = call(
         part(tangent_term, n), [bf(tokens, slab)] + [bf(tokens, cols)] * n,
         [normed, packed, swap(packed, "rep"), value_probe], scratch=[held(tokens, block), dma(())],
-        in_specs=[ANY] + [VMEM] * 3, first=qkv[2:])
+        in_specs=[ANY] + [VMEM] * 3)
     other_probe = swap(after(out_probe, packed), "head")
     weights = [swap(after(share, feats), "head")]
     probs, attended = call(

time: 162 us -> 157 us (0.969)
  waiting for transfers between devices: 80.7 us -> 77.7 us
    ppermute x21, waiting for transfers between devices: 64.4 us -> 58.8 us  [ahead(): return lax.ppermute(x, 'seq', [(i, (i + k) % n) for i in range(n)])]
    ppermute x13, waiting for transfers between devices: 16.3 us -> 18.9 us  [swap(): return lax.ppermute(x, axis, [(0, 1), (1, 0)])]
    ppermute x21, starting transfers between devices: 40.5 us -> 38.1 us  [ahead(): return lax.ppermute(x, 'seq', [(i, (i + k) % n) for i in range(n)])]
  transfers between devices with their start and end apart: 34 -> 34, of which waited for: 18 -> 18; matrix products, arithmetic and copies ran while one was open for 1% -> 1% of each run, Pallas kernels for 10% -> 11%
where the time goes in v4:
time: 157 us
  waiting for transfers between devices  77.7 us (49%)
  starting transfers between devices  50.7 us (32%)
  Pallas kernels  23.3 us (15%)
  local copies, waits for them, and re-layouts  4.53 us (3%)
    ppermute x21, waiting for transfers between devices, ahead(): return lax.ppermute(x, 'seq', [(i, (i + k) % n) for i in range(n)])  58.8 us
    ppermute x21, starting transfers between devices, ahead(): return lax.ppermute(x, 'seq', [(i, (i + k) % n) for i in range(n)])  38.1 us
    pallas_call x16, Pallas kernels, __call__(): pl.pallas_call(body, out_shape=outs, in_specs=specs, out_specs=out_specs,...  23.3 us
    ppermute x13, waiting for transfers between devices, swap(): return lax.ppermute(x, axis, [(0, 1), (1, 0)])  18.9 us
    ppermute x13, starting transfers between devices, swap(): return lax.ppermute(x, axis, [(0, 1), (1, 0)])  12.6 us
  transfers between devices with their start and end apart: 34, of which 18 were waited for; matrix products, arithmetic and copies ran while one was open for 1% of the time, Pallas kernels for 11%

profile of v4, /device:TPU:0, one launch (start us, length us, event | category | flops | bytes accessed | tf_op | source)
XLA Modules:
  0.0 157.2 jit_solution(15585262712751087472)
XLA Ops:
  0.7 1.1 fusion
  1.8 3.1 %collective-permute-start.1 = (bf16[64,1024]{1,0:T(8,128)(2,1)S(1)}, bf16[64,1024]{1,0:T(8,128)(2,1)S(1)}, u32[]{:S(2)}, u32[]{:S(2)}) collective-permute-start(bf16[64,1024]{1,0:T(8,128)(2,1)S(1)} %get-tuple-element.51), channel_id=1, source_target_pairs={{0,4},{4,8},{8,12},{12,0},{1,5},{5,9},{9,13},{13,1},{2,6},{6,10},{... | collective-permute-start | bytes 393224 | tf_op jit(solution)/shard_map/ppermute | solution.py:61
  4.9 2.1 %collective-permute-start = (bf16[64,1024]{1,0:T(8,128)(2,1)S(1)}, bf16[64,1024]{1,0:T(8,128)(2,1)S(1)}, u32[]{:S(2)}, u32[]{:S(2)}) collective-permute-start(bf16[64,1024]{1,0:T(8,128)(2,1)S(1)} %get-tuple-element.52), channel_id=1, source_target_pairs={{0,12},{4,0},{8,4},{12,8},{1,13},{5,1},{9,5},{13,9},{2,14},{6,2},{... | collective-permute-start | bytes 393224 | tf_op jit(solution)/shard_map/ppermute | solution.py:61
  7.0 0.9 collective-permute-start.2
  7.9 0.9 dynamic-slice_bitcast_fusion.2
  8.9 1.2 dynamic-slice_bitcast_fusion
  10.1 1.1 collective-permute-done.1.refs_1_
  11.3 8.2 %collective-permute-start.7 = (bf16[3,256,128]{2,1,0:T(8,128)(2,1)S(1)}, bf16[3,256,128]{2,1,0:T(8,128)(2,1)S(1)}, u32[]{:S(2)}, u32[]{:S(2)}) collective-permute-start(bf16[3,256,128]{2,1,0:T(8,128)(2,1)S(1)} %pad_maximum_fusion.1), channel_id=1, source_target_pairs={{0,8},{4,12},{8,0},{12,4},{1,9},{5,13},{9,1},{13,5},{2,10},{6,14},... | collective-permute-start | bytes 589832 | tf_op jit(solution)/shard_map/ppermute | solution.py:61
  19.4 1.5 collective-permute-start.4
  20.9 0.5 collective-permute-start.3
  21.4 5.9 %collective-permute-done.2.refs_2_ = bf16[64,1024]{1,0:T(8,128)(2,1)S(1)} collective-permute-done((bf16[64,1024]{1,0:T(8,128)(2,1)S(1)}, bf16[64,1024]{1,0:T(8,128)(2,1)S(1)}, u32[]{:S(2)}, u32[]{:S(2)}) %collective-permute-start.2) | collective-permute-done | bytes 131104 | tf_op jit(solution)/shard_map/ppermute | solution.py:61
  27.4 1.5 collective-permute-start.5
  28.9 3.8 %collective-permute-done.5.refs_5_ = bf16[64,1024]{1,0:T(8,128)(2,1)S(1)} collective-permute-done((bf16[64,1024]{1,0:T(8,128)(2,1)S(1)}, bf16[64,1024]{1,0:T(8,128)(2,1)S(1)}, u32[]{:S(2)}, u32[]{:S(2)}) %collective-permute-start.5) | collective-permute-done | bytes 131104 | tf_op jit(solution)/shard_map/ppermute | solution.py:65
  32.7 0.1 pack.1
  32.8 0.1 collective-permute-start.8
  33.0 2.1 %collective-permute-done.8.refs_2_ = bf16[6,64,1024]{2,1,0:T(8,128)(2,1)S(1)} collective-permute-done((bf16[6,64,1024]{2,1,0:T(8,128)(2,1)S(1)}, bf16[6,64,1024]{2,1,0:T(8,128)(2,1)S(1)}, u32[]{:S(2)}, u32[]{:S(2)}) %collective-permute-start.8) | collective-permute-done | bytes 786464 | tf_op jit(solution)/shard_map/ppermute | solution.py:65
  35.2 1.7 %tangent_term.1 = (bf16[1024,1024]{1,0:T(8,128)(2,1)S(1)}, bf16[1024,128]{1,0:T(8,128)(2,1)S(1)}, bf16[1024,128]{1,0:T(8,128)(2,1)S(1)}, bf16[1024,128]{1,0:T(8,128)(2,1)S(1)}, bf16[1024,128]{1,0:T(8,128)(2,1)S(1)}) custom-call(bf16[256,4096]{1,0:T(8,128)(2,1)S(1)} %copy-done.2, bf16[6,64,1024]{2,1,0:T(8,128)(2,1)S(1)} %get-tuple-element.28.refs_1_.refs_4_, ...), custom_call_target="tpu_custom_call" | custom-call | flops 1 | bytes 1 | tf_op jit(solution)/shard_map/tangent_term/pallas_call | solution.py:33
  36.9 1.6 collective-permute-start.18
  38.5 3.7 %collective-permute-start.15 = (bf16[1024,128]{1,0:T(8,128)(2,1)S(1)}, bf16[1024,128]{1,0:T(8,128)(2,1)S(1)}, u32[]{:S(2)}, u32[]{:S(2)}) collective-permute-start(bf16[1024,128]{1,0:T(8,128)(2,1)S(1)} %get-tuple-element.36), channel_id=1, source_target_pairs={{0,12},{4,0},{8,4},{12,8},{1,13},{5,1},{9,5},{13,9},{2,14},{6,2},{... | collective-permute-start | bytes 786440 | tf_op jit(solution)/shard_map/ppermute | solution.py:61
  42.3 7.8 %attend.1 = (bf16[2,1024,1024]{2,1,0:T(8,128)(2,1)S(1)}, bf16[1024,128]{1,0:T(8,128)(2,1)S(1)}) custom-call(bf16[256,512]{1,0:T(8,128)(2,1)S(1)} %copy-done.5, bf16[256,512]{1,0:T(8,128)(2,1)S(1)} %copy-done.7, bf16[256,512]{1,0:T(8,128)(2,1)S(1)} %copy-done.6, bf16[3,256,128]{2,1,0:T(8,128)(2,1)S(1)} %collective-permute-done.6.refs_7_.refs_3_, ...), custom_call_target="tpu_custom_call" | custom-call | flops 1 | bytes 1 | tf_op jit(solution)/shard_map/attend/pallas_call | solution.py:33
  50.0 0.5 collective-permute-start.11
  50.5 1.5 collective-permute-start.22
  52.0 0.1 add.63.refs_4_
  52.1 0.7 collective-permute-start.14
  52.8 0.5 collective-permute-start.10
  53.3 4.8 %collective-permute-done.11.refs_3_ = bf16[1024,128]{1,0:T(8,128)(2,1)S(1)} collective-permute-done((bf16[1024,128]{1,0:T(8,128)(2,1)S(1)}, bf16[1024,128]{1,0:T(8,128)(2,1)S(1)}, u32[]{:S(2)}, u32[]{:S(2)}) %collective-permute-start.11) | collective-permute-done | bytes 262176 | tf_op jit(solution)/shard_map/ppermute | solution.py:61
  58.1 3.5 %collective-permute-start.12 = (bf16[1024,128]{1,0:T(8,128)(2,1)S(1)}, bf16[1024,128]{1,0:T(8,128)(2,1)S(1)}, u32[]{:S(2)}, u32[]{:S(2)}) collective-permute-start(bf16[1024,128]{1,0:T(8,128)(2,1)S(1)} %collective-permute-done.11.refs_3_), channel_id=1, source_target_pairs={{0,12},{4,0},{8,4},{12,8},{1,13},{5,1},{9,5},{13,9},{2,14},{6,2},{... | collective-permute-start | bytes 786440 | tf_op jit(solution)/shard_map/ppermute | solution.py:61
  61.6 3.3 %collective-permute-done.14.refs_1_ = bf16[1024,128]{1,0:T(8,128)(2,1)S(1)} collective-permute-done((bf16[1024,128]{1,0:T(8,128)(2,1)S(1)}, bf16[1024,128]{1,0:T(8,128)(2,1)S(1)}, u32[]{:S(2)}, u32[]{:S(2)}) %collective-permute-start.14) | collective-permute-done | bytes 262176 | tf_op jit(solution)/shard_map/ppermute | solution.py:61
  64.9 1.5 attend_tan.1
  66.4 1.6 collective-permute-start.16
  68.0 2.5 %collective-permute-done.10.refs_2_.refs_1_ = bf16[1024,128]{1,0:T(8,128)(2,1)S(1)} collective-permute-done((bf16[1024,128]{1,0:T(8,128)(2,1)S(1)}, bf16[1024,128]{1,0:T(8,128)(2,1)S(1)}, u32[]{:S(2)}, u32[]{:S(2)}) %collective-permute-start.10) | collective-permute-done | bytes 262176 | tf_op jit(solution)/shard_map/ppermute | solution.py:61
  70.4 5.8 %collective-permute-done.16.refs_1_ = bf16[512,128]{1,0:T(8,128)(2,1)S(1)} collective-permute-done((bf16[512,128]{1,0:T(8,128)(2,1)S(1)}, bf16[512,128]{1,0:T(8,128)(2,1)S(1)}, u32[]{:S(2)}, u32[]{:S(2)}) %collective-permute-start.16) | collective-permute-done | bytes 131104 | tf_op jit(solution)/shard_map/ppermute | solution.py:65
  76.3 0.2 cut_rows.1.refs_7_
  76.5 1.6 collective-permute-start.17
  78.0 1.5 collective-permute-start.23
  79.6 3.5 %collective-permute-start.20 = (bf16[512,256]{1,0:T(8,128)(2,1)S(1)}, bf16[512,256]{1,0:T(8,128)(2,1)S(1)}, u32[]{:S(2)}, u32[]{:S(2)}) collective-permute-start(bf16[512,256]{1,0:T(8,128)(2,1)S(1)} %join.1.refs_4_.refs_1_), channel_id=1, source_target_pairs={{0,12},{4,0},{8,4},{12,8},{1,13},{5,1},{9,5},{13,9},{2,14},{6,2},{... | collective-permute-start | bytes 786440 | tf_op jit(solution)/shard_map/ppermute | solution.py:61
  83.0 6.8 %collective-permute-done.20.refs_4_ = bf16[512,256]{1,0:T(8,128)(2,1)S(1)} collective-permute-done((bf16[512,256]{1,0:T(8,128)(2,1)S(1)}, bf16[512,256]{1,0:T(8,128)(2,1)S(1)}, u32[]{:S(2)}, u32[]{:S(2)}) %collective-permute-start.20) | collective-permute-done | bytes 262176 | tf_op jit(solution)/shard_map/ppermute | solution.py:61
  89.8 4.3 %collective-permute-start.21 = (bf16[512,256]{1,0:T(8,128)(2,1)S(1)}, bf16[512,256]{1,0:T(8,128)(2,1)S(1)}, u32[]{:S(2)}, u32[]{:S(2)}) collective-permute-start(bf16[512,256]{1,0:T(8,128)(2,1)S(1)} %collective-permute-done.20.refs_4_), channel_id=1, source_target_pairs={{0,12},{4,0},{8,4},{12,8},{1,13},{5,1},{9,5},{13,9},{2,14},{6,2},{... | collective-permute-start | bytes 786440 | tf_op jit(solution)/shard_map/ppermute | solution.py:61
  94.1 1.3 out_term.1.refs_0_.refs_8_
  95.4 0.5 collective-permute-done.19.refs_2_
  95.9 2.6 %collective-permute-done.21.refs_3_ = bf16[512,256]{1,0:T(8,128)(2,1)S(1)} collective-permute-done((bf16[512,256]{1,0:T(8,128)(2,1)S(1)}, bf16[512,256]{1,0:T(8,128)(2,1)S(1)}, u32[]{:S(2)}, u32[]{:S(2)}) %collective-permute-start.21) | collective-permute-done | bytes 262176 | tf_op jit(solution)/shard_map/ppermute | solution.py:61
  98.4 1.3 out_sum.1.refs_0_.refs_5_
  99.8 0.1 collective-permute-start.24
  99.9 2.6 %collective-permute-done.24.refs_1_ = bf16[512,1024]{1,0:T(8,128)(2,1)S(1)} collective-permute-done((bf16[512,1024]{1,0:T(8,128)(2,1)S(1)}, bf16[512,1024]{1,0:T(8,128)(2,1)S(1)}, u32[]{:S(2)}, u32[]{:S(2)}) %collective-permute-start.24) | collective-permute-done | bytes 1048608 | tf_op jit(solution)/shard_map/ppermute | solution.py:65
  102.5 1.7 %grad_term.1 = (bf16[512,1024]{1,0:T(8,128)(2,1)S(1)}, bf16[256,1024]{1,0:T(8,128)(2,1)S(1)}, bf16[512,256]{1,0:T(8,128)(2,1)S(1)}, bf16[512,256]{1,0:T(8,128)(2...) custom-call(bf16[512,1024]{1,0:T(8,128)(2,1)S(1)} %out_sum.1.refs_0_.refs_5_, ...), custom_call_target="tpu_custom_call" | custom-call | flops 1 | bytes 1 | tf_op jit(solution)/shard_map/grad_term/pallas_call | solution.py:33
  104.2 0.6 collective-permute-start.25
  104.8 4.3 %collective-permute-start.29 = (bf16[512,256]{1,0:T(8,128)(2,1)S(1)}, bf16[512,256]{1,0:T(8,128)(2,1)S(1)}, u32[]{:S(2)}, u32[]{:S(2)}) collective-permute-start(bf16[512,256]{1,0:T(8,128)(2,1)S(1)} %get-tuple-element.47), channel_id=1, source_target_pairs={{0,12},{4,0},{8,4},{12,8},{1,13},{5,1},{9,5},{13,9},{2,14},{6,2},{... | collective-permute-start | bytes 786440 | tf_op jit(solution)/shard_map/ppermute | solution.py:61
  109.1 6.5 %collective-permute-done.27.refs_0_ = bf16[512,256]{1,0:T(8,128)(2,1)S(1)} collective-permute-done((bf16[512,256]{1,0:T(8,128)(2,1)S(1)}, bf16[512,256]{1,0:T(8,128)(2,1)S(1)}, u32[]{:S(2)}, u32[]{:S(2)}) %collective-permute-start.27) | collective-permute-done | bytes 262176 | tf_op jit(solution)/shard_map/ppermute | solution.py:61
  115.7 0.2 collective-permute-start.28
  116.0 2.6 %collective-permute-done.29.refs_2_ = bf16[512,256]{1,0:T(8,128)(2,1)S(1)} collective-permute-done((bf16[512,256]{1,0:T(8,128)(2,1)S(1)}, bf16[512,256]{1,0:T(8,128)(2,1)S(1)}, u32[]{:S(2)}, u32[]{:S(2)}) %collective-permute-start.29) | collective-permute-done | bytes 262176 | tf_op jit(solution)/shard_map/ppermute | solution.py:61
  118.6 10.1 %collective-permute-done.28.refs_1_ = bf16[512,256]{1,0:T(8,128)(2,1)S(1)} collective-permute-done((bf16[512,256]{1,0:T(8,128)(2,1)S(1)}, bf16[512,256]{1,0:T(8,128)(2,1)S(1)}, u32[]{:S(2)}, u32[]{:S(2)}) %collective-permute-start.28) | collective-permute-done | bytes 262176 | tf_op jit(solution)/shard_map/ppermute | solution.py:61
  128.7 0.1 add_grad.1
  128.8 0.6 collective-permute-start.30
  129.4 4.4 %collective-permute-done.30.refs_1_ = bf16[512,128]{1,0:T(8,128)(2,1)S(1)} collective-permute-done((bf16[512,128]{1,0:T(8,128)(2,1)S(1)}, bf16[512,128]{1,0:T(8,128)(2,1)S(1)}, u32[]{:S(2)}, u32[]{:S(2)}) %collective-permute-start.30) | collective-permute-done | bytes 131104 | tf_op jit(solution)/shard_map/ppermute | solution.py:65
  133.8 2.1 %key_grad.1.refs_7_.refs_1_ = bf16[1024,128]{1,0:T(8,128)(2,1)S(1)} custom-call(bf16[512,128]{1,0:T(8,128)(2,1)S(1)} %get-tuple-element.48.refs_0_.refs_3_, bf16[512,128]{1,0:T(8,128)(2,1)S(1)} %collective-permute-done.30.refs_1_, bf16[2,1024,1024]{2,1,0:T(8,128)(2,1)S(1)} %get-tuple-element.35.refs_2_.refs_3_, ...), custom_call_target="tpu_custom_call" | custom-call | flops 1 | bytes 1 | tf_op jit(solution)/shard_map/key_grad/pallas_call | solution.py:33
  135.9 1.8 %collective-permute-start.32 = (bf16[1024,128]{1,0:T(8,128)(2,1)S(1)}, bf16[1024,128]{1,0:T(8,128)(2,1)S(1)}, u32[]{:S(2)}, u32[]{:S(2)}) collective-permute-start(bf16[1024,128]{1,0:T(8,128)(2,1)S(1)} %key_grad.1.refs_7_.refs_1_), channel_id=1, source_target_pairs={{0,12},{4,0},{8,4},{12,8},{1,13},{5,1},{9,5},{13,9},{2,14},{6,2},{... | collective-permute-start | bytes 786440 | tf_op jit(solution)/shard_map/ppermute | solution.py:61
  137.7 0.3 collective-permute-start.31
  138.0 10.5 %collective-permute-done.32.refs_4_ = bf16[1024,128]{1,0:T(8,128)(2,1)S(1)} collective-permute-done((bf16[1024,128]{1,0:T(8,128)(2,1)S(1)}, bf16[1024,128]{1,0:T(8,128)(2,1)S(1)}, u32[]{:S(2)}, u32[]{:S(2)}) %collective-permute-start.32) | collective-permute-done | bytes 262176 | tf_op jit(solution)/shard_map/ppermute | solution.py:61
  148.5 0.4 collective-permute-start.33
  148.9 2.5 %out_product.1.refs_1_ = bf16[512,1024]{1,0:T(8,128)(2,1)} custom-call(bf16[1024,128]{1,0:T(8,128)(2,1)S(1)} %get-tuple-element.31.refs_0_, bf16[1024,128]{1,0:T(8,128)(2,1)S(1)} %collective-permute-done.10.refs_2_.refs_1_, bf16[1024,128]{1,0:T(8,128)(2,1)S(1)} %collective-permute-done.12.refs_2_, bf16[1024,128]{1,0:T(8,128)(2,1)S(1)} %collective-permute-done.11.refs_3_, ...), custom_call_target="tpu_custom_call" | custom-call | flops 1 | bytes 1 | tf_op jit(solution)/shard_map/out_product/pallas_call | solution.py:33
  151.4 1.2 copy-done.1
  152.6 0.6 flip.1.refs_0_.refs_5_
  153.3 1.6 %collective-permute-done.33.refs_3_ = bf16[1024,128]{1,0:T(8,128)(2,1)S(1)} collective-permute-done((bf16[1024,128]{1,0:T(8,128)(2,1)S(1)}, bf16[1024,128]{1,0:T(8,128)(2,1)S(1)}, u32[]{:S(2)}, u32[]{:S(2)}) %collective-permute-start.33) | collective-permute-done | bytes 262176 | tf_op jit(solution)/shard_map/ppermute | solution.py:61
  154.9 2.3 %value_product.1 = bf16[1024,512]{1,0:T(8,128)(2,1)} custom-call(bf16[1024,1024]{1,0:T(8,128)(2,1)S(1)} %flip.1.refs_0_.refs_5_, bf16[1024,128]{1,0:T(8,128)(2,1)S(1)} %key_grad.1.refs_7_.refs_1_, bf16[1024,128]{1,0:T(8,128)(2,1)S(1)} %collective-permute-done.31.refs_2_, bf16[1024,128]{1,0:T(8,128)(2,1)S(1)} %collective-permute-done.33.refs_3_, ...), custom_call_target="tpu_custom_call" | custom-call | flops 1 | bytes 1 | tf_op jit(solution)/shard_map/value_product/pallas_call | solution.py:33
  (42 shorter events, 0.5 us)
Async XLA Ops:
  0.6 32.1 %copy-start = (bf16[512,1024]{1,0:T(8,128)(2,1)S(1)}, bf16[512,1024]{1,0:T(8,128)(2,1)}, u32[]{:S(2)}) copy-start(bf16[512,1024]{1,0:T(8,128)(2,1)} %refs_2_.3) | copy-start | bytes 3145732
  1.8 9.4 %collective-permute-start.1 = (bf16[64,1024]{1,0:T(8,128)(2,1)S(1)}, bf16[64,1024]{1,0:T(8,128)(2,1)S(1)}, u32[]{:S(2)}, u32[]{:S(2)}) collective-permute-start(bf16[64,1024]{1,0:T(8,128)(2,1)S(1)} %get-tuple-element.51), channel_id=1, source_target_pairs={{0,4},{4,8},{8,12},{12,0},{1,5},{5,9},{9,13},{13,1},{2,6},{6,10},{... | collective-permute-start | bytes 393224 | tf_op jit(solution)/shard_map/ppermute | solution.py:61
  4.9 16.0 %collective-permute-start = (bf16[64,1024]{1,0:T(8,128)(2,1)S(1)}, bf16[64,1024]{1,0:T(8,128)(2,1)S(1)}, u32[]{:S(2)}, u32[]{:S(2)}) collective-permute-start(bf16[64,1024]{1,0:T(8,128)(2,1)S(1)} %get-tuple-element.52), channel_id=1, source_target_pairs={{0,12},{4,0},{8,4},{12,8},{1,13},{5,1},{9,5},{13,9},{2,14},{6,2},{... | collective-permute-start | bytes 393224 | tf_op jit(solution)/shard_map/ppermute | solution.py:61
  7.0 20.4 %collective-permute-start.2 = (bf16[64,1024]{1,0:T(8,128)(2,1)S(1)}, bf16[64,1024]{1,0:T(8,128)(2,1)S(1)}, u32[]{:S(2)}, u32[]{:S(2)}) collective-permute-start(bf16[64,1024]{1,0:T(8,128)(2,1)S(1)} %get-tuple-element.50), channel_id=1, source_target_pairs={{0,8},{4,12},{8,0},{12,4},{1,9},{5,13},{9,1},{13,5},{2,10},{6,14},... | collective-permute-start | bytes 393224 | tf_op jit(solution)/shard_map/ppermute | solution.py:61
  8.9 26.3 %copy-start.2 = (bf16[256,4096]{1,0:T(8,128)(2,1)S(1)}, bf16[256,4096]{1,0:T(8,128)(2,1)}, u32[]{:S(2)}) copy-start(bf16[256,4096]{1,0:T(8,128)(2,1)} %refs_0_.2) | copy-start | bytes 6291460
  8.9 26.3 %copy-start.3 = (bf16[1024,512]{1,0:T(8,128)(2,1)S(1)}, bf16[1024,512]{1,0:T(8,128)(2,1)}, u32[]{:S(2)}) copy-start(bf16[1024,512]{1,0:T(8,128)(2,1)} %refs_3_.1) | copy-start | bytes 3145732
  11.3 21.4 %collective-permute-start.7 = (bf16[3,256,128]{2,1,0:T(8,128)(2,1)S(1)}, bf16[3,256,128]{2,1,0:T(8,128)(2,1)S(1)}, u32[]{:S(2)}, u32[]{:S(2)}) collective-permute-start(bf16[3,256,128]{2,1,0:T(8,128)(2,1)S(1)} %pad_maximum_fusion.1), channel_id=1, source_target_pairs={{0,8},{4,12},{8,0},{12,4},{1,9},{5,13},{9,1},{13,5},{2,10},{6,14},... | collective-permute-start | bytes 589832 | tf_op jit(solution)/shard_map/ppermute | solution.py:61
  19.4 13.3 %collective-permute-start.6 = (bf16[3,256,128]{2,1,0:T(8,128)(2,1)S(1)}, bf16[3,256,128]{2,1,0:T(8,128)(2,1)S(1)}, u32[]{:S(2)}, u32[]{:S(2)}) collective-permute-start(bf16[3,256,128]{2,1,0:T(8,128)(2,1)S(1)} %pad_maximum_fusion), channel_id=1, source_target_pairs={{0,4},{4,8},{8,12},{12,0},{1,5},{5,9},{9,13},{13,1},{2,6},{6,10},{... | collective-permute-start | bytes 589832 | tf_op jit(solution)/shard_map/ppermute | solution.py:61
  19.4 9.5 %collective-permute-start.4 = (bf16[64,1024]{1,0:T(8,128)(2,1)S(1)}, bf16[64,1024]{1,0:T(8,128)(2,1)S(1)}, u32[]{:S(2)}, u32[]{:S(2)}) collective-permute-start(bf16[64,1024]{1,0:T(8,128)(2,1)S(1)} %collective-permute-done.1.refs_1_), channel_id=1, source_target_pairs={{0,2},{2,0},{1,3},{3,1},{4,6},{6,4},{5,7},{7,5},{8,10},{10,8},{9,1... | collective-permute-start | bytes 393224 | tf_op jit(solution)/shard_map/ppermute | solution.py:65
  20.9 8.0 %collective-permute-start.3 = (bf16[64,1024]{1,0:T(8,128)(2,1)S(1)}, bf16[64,1024]{1,0:T(8,128)(2,1)S(1)}, u32[]{:S(2)}, u32[]{:S(2)}) collective-permute-start(bf16[64,1024]{1,0:T(8,128)(2,1)S(1)} %collective-permute-done.refs_0_), channel_id=1, source_target_pairs={{0,2},{2,0},{1,3},{3,1},{4,6},{6,4},{5,7},{7,5},{8,10},{10,8},{9,1... | collective-permute-start | bytes 393224 | tf_op jit(solution)/shard_map/ppermute | solution.py:65
  27.4 5.3 %collective-permute-start.5 = (bf16[64,1024]{1,0:T(8,128)(2,1)S(1)}, bf16[64,1024]{1,0:T(8,128)(2,1)S(1)}, u32[]{:S(2)}, u32[]{:S(2)}) collective-permute-start(bf16[64,1024]{1,0:T(8,128)(2,1)S(1)} %collective-permute-done.2.refs_2_), channel_id=1, source_target_pairs={{0,2},{2,0},{1,3},{3,1},{4,6},{6,4},{5,7},{7,5},{8,10},{10,8},{9,1... | collective-permute-start | bytes 393224 | tf_op jit(solution)/shard_map/ppermute | solution.py:65
  32.8 2.4 %collective-permute-start.8 = (bf16[6,64,1024]{2,1,0:T(8,128)(2,1)S(1)}, bf16[6,64,1024]{2,1,0:T(8,128)(2,1)S(1)}, u32[]{:S(2)}, u32[]{:S(2)}) collective-permute-start(bf16[6,64,1024]{2,1,0:T(8,128)(2,1)S(1)} %get-tuple-element.28.refs_1_.refs_4_), channel_id=1, source_target_pairs={{0,1},{1,0},{2,3},{3,2},{4,5},{5,4},{6,7},{7,6},{8,9},{9,8},{10,11... | collective-permute-start | bytes 2359304 | tf_op jit(solution)/shard_map/ppermute | solution.py:65
  32.9 4.0 %copy-start.4 = (bf16[512,1024]{1,0:T(8,128)(2,1)S(1)}, bf16[512,1024]{1,0:T(8,128)(2,1)}, u32[]{:S(2)}) copy-start(bf16[512,1024]{1,0:T(8,128)(2,1)} %refs_5_.2) | copy-start | bytes 3145732
  32.9 9.3 %copy-start.5 = (bf16[256,512]{1,0:T(8,128)(2,1)S(1)}, bf16[256,512]{1,0:T(8,128)(2,1)}, u32[]{:S(2)}) copy-start(bf16[256,512]{1,0:T(8,128)(2,1)} %refs_0_.3) | copy-start | bytes 786436
  33.0 9.3 %copy-start.6 = (bf16[256,512]{1,0:T(8,128)(2,1)S(1)}, bf16[256,512]{1,0:T(8,128)(2,1)}, u32[]{:S(2)}) copy-start(bf16[256,512]{1,0:T(8,128)(2,1)} %refs_2_.2) | copy-start | bytes 786436
  33.0 9.3 %copy-start.7 = (bf16[256,512]{1,0:T(8,128)(2,1)S(1)}, bf16[256,512]{1,0:T(8,128)(2,1)}, u32[]{:S(2)}) copy-start(bf16[256,512]{1,0:T(8,128)(2,1)} %refs_1_.1) | copy-start | bytes 786436
  33.0 9.3 %collective-permute-start.9 = (bf16[3,256,128]{2,1,0:T(8,128)(2,1)S(1)}, bf16[3,256,128]{2,1,0:T(8,128)(2,1)S(1)}, u32[]{:S(2)}, u32[]{:S(2)}) collective-permute-start(bf16[3,256,128]{2,1,0:T(8,128)(2,1)S(1)} %pad_maximum_fusion.2), channel_id=1, source_target_pairs={{0,12},{4,0},{8,4},{12,8},{1,13},{5,1},{9,5},{13,9},{2,14},{6,2},{... | collective-permute-start | bytes 589832 | tf_op jit(solution)/shard_map/ppermute | solution.py:61
  36.9 15.1 %collective-permute-start.13 = (bf16[1024,128]{1,0:T(8,128)(2,1)S(1)}, bf16[1024,128]{1,0:T(8,128)(2,1)S(1)}, u32[]{:S(2)}, u32[]{:S(2)}) collective-permute-start(bf16[1024,128]{1,0:T(8,128)(2,1)S(1)} %get-tuple-element.33), channel_id=1, source_target_pairs={{0,4},{4,8},{8,12},{12,0},{1,5},{5,9},{9,13},{13,1},{2,6},{6,10},{... | collective-permute-start | bytes 786440 | tf_op jit(solution)/shard_map/ppermute | solution.py:61
  36.9 57.1 %collective-permute-start.18 = (bf16[512,1024]{1,0:T(8,128)(2,1)S(1)}, bf16[512,1024]{1,0:T(8,128)(2,1)S(1)}, u32[]{:S(2)}, u32[]{:S(2)}) collective-permute-start(bf16[512,1024]{1,0:T(8,128)(2,1)S(1)} %copy-done.4), channel_id=1, source_target_pairs={{0,2},{2,0},{1,3},{3,1},{4,6},{6,4},{5,7},{7,5},{8,10},{10,8},{9,1... | collective-permute-start | bytes 3145736 | tf_op jit(solution)/shard_map/ppermute | solution.py:65
  38.5 14.3 %collective-permute-start.15 = (bf16[1024,128]{1,0:T(8,128)(2,1)S(1)}, bf16[1024,128]{1,0:T(8,128)(2,1)S(1)}, u32[]{:S(2)}, u32[]{:S(2)}) collective-permute-start(bf16[1024,128]{1,0:T(8,128)(2,1)S(1)} %get-tuple-element.36), channel_id=1, source_target_pairs={{0,12},{4,0},{8,4},{12,8},{1,13},{5,1},{9,5},{13,9},{2,14},{6,2},{... | collective-permute-start | bytes 786440 | tf_op jit(solution)/shard_map/ppermute | solution.py:61
  50.0 8.0 %collective-permute-start.11 = (bf16[1024,128]{1,0:T(8,128)(2,1)S(1)}, bf16[1024,128]{1,0:T(8,128)(2,1)S(1)}, u32[]{:S(2)}, u32[]{:S(2)}) collective-permute-start(bf16[1024,128]{1,0:T(8,128)(2,1)S(1)} %get-tuple-element.31.refs_0_), channel_id=1, source_target_pairs={{0,12},{4,0},{8,4},{12,8},{1,13},{5,1},{9,5},{13,9},{2,14},{6,2},{... | collective-permute-start | bytes 786440 | tf_op jit(solution)/shard_map/ppermute | solution.py:61
  50.5 27.5 %collective-permute-start.22 = (bf16[256,1024]{1,0:T(8,128)(2,1)S(1)}, bf16[256,1024]{1,0:T(8,128)(2,1)S(1)}, u32[]{:S(2)}, u32[]{:S(2)}) collective-permute-start(bf16[256,1024]{1,0:T(8,128)(2,1)S(1)} %get-tuple-element.41), channel_id=1, source_target_pairs={{0,2},{2,0},{1,3},{3,1},{4,6},{6,4},{5,7},{7,5},{8,10},{10,8},{9,1... | collective-permute-start | bytes 1572872 | tf_op jit(solution)/shard_map/ppermute | solution.py:65
  52.1 12.8 %collective-permute-start.14 = (bf16[1024,128]{1,0:T(8,128)(2,1)S(1)}, bf16[1024,128]{1,0:T(8,128)(2,1)S(1)}, u32[]{:S(2)}, u32[]{:S(2)}) collective-permute-start(bf16[1024,128]{1,0:T(8,128)(2,1)S(1)} %add.63.refs_4_), channel_id=1, source_target_pairs={{0,4},{4,8},{8,12},{12,0},{1,5},{5,9},{9,13},{13,1},{2,6},{6,10},{... | collective-permute-start | bytes 786440 | tf_op jit(solution)/shard_map/ppermute | solution.py:61
  52.8 17.7 %collective-permute-start.10 = (bf16[1024,128]{1,0:T(8,128)(2,1)S(1)}, bf16[1024,128]{1,0:T(8,128)(2,1)S(1)}, u32[]{:S(2)}, u32[]{:S(2)}) collective-permute-start(bf16[1024,128]{1,0:T(8,128)(2,1)S(1)} %get-tuple-element.31.refs_0_), channel_id=1, source_target_pairs={{0,4},{4,8},{8,12},{12,0},{1,5},{5,9},{9,13},{13,1},{2,6},{6,10},{... | collective-permute-start | bytes 786440 | tf_op jit(solution)/shard_map/ppermute | solution.py:61
  58.1 18.2 %collective-permute-start.12 = (bf16[1024,128]{1,0:T(8,128)(2,1)S(1)}, bf16[1024,128]{1,0:T(8,128)(2,1)S(1)}, u32[]{:S(2)}, u32[]{:S(2)}) collective-permute-start(bf16[1024,128]{1,0:T(8,128)(2,1)S(1)} %collective-permute-done.11.refs_3_), channel_id=1, source_target_pairs={{0,12},{4,0},{8,4},{12,8},{1,13},{5,1},{9,5},{13,9},{2,14},{6,2},{... | collective-permute-start | bytes 786440 | tf_op jit(solution)/shard_map/ppermute | solution.py:61
  66.4 9.9 %collective-permute-start.16 = (bf16[512,128]{1,0:T(8,128)(2,1)S(1)}, bf16[512,128]{1,0:T(8,128)(2,1)S(1)}, u32[]{:S(2)}, u32[]{:S(2)}) collective-permute-start(bf16[512,128]{1,0:T(8,128)(2,1)S(1)} %get-tuple-element.38), channel_id=1, source_target_pairs={{0,2},{2,0},{1,3},{3,1},{4,6},{6,4},{5,7},{7,5},{8,10},{10,8},{9,1... | collective-permute-start | bytes 393224 | tf_op jit(solution)/shard_map/ppermute | solution.py:65
  76.5 17.6 %collective-permute-start.17 = (bf16[512,512]{1,0:T(8,128)(2,1)S(1)}, bf16[512,512]{1,0:T(8,128)(2,1)S(1)}, u32[]{:S(2)}, u32[]{:S(2)}) collective-permute-start(bf16[512,512]{1,0:T(8,128)(2,1)S(1)} %cut_rows.1.refs_7_), channel_id=1, source_target_pairs={{0,2},{2,0},{1,3},{3,1},{4,6},{6,4},{5,7},{7,5},{8,10},{10,8},{9,1... | collective-permute-start | bytes 1572872 | tf_op jit(solution)/shard_map/ppermute | solution.py:65
  78.0 17.9 %collective-permute-start.23 = (bf16[256,1024]{1,0:T(8,128)(2,1)S(1)}, bf16[256,1024]{1,0:T(8,128)(2,1)S(1)}, u32[]{:S(2)}, u32[]{:S(2)}) collective-permute-start(bf16[256,1024]{1,0:T(8,128)(2,1)S(1)} %collective-permute-done.22.refs_6_.refs_3_), channel_id=1, source_target_pairs={{0,16},{16,0},{1,17},{17,1},{2,18},{18,2},{3,19},{19,3},{4,20},{20... | collective-permute-start | bytes 1572872 | tf_op jit(solution)/shard_map/ppermute | solution.py:65
  79.6 10.2 %collective-permute-start.20 = (bf16[512,256]{1,0:T(8,128)(2,1)S(1)}, bf16[512,256]{1,0:T(8,128)(2,1)S(1)}, u32[]{:S(2)}, u32[]{:S(2)}) collective-permute-start(bf16[512,256]{1,0:T(8,128)(2,1)S(1)} %join.1.refs_4_.refs_1_), channel_id=1, source_target_pairs={{0,12},{4,0},{8,4},{12,8},{1,13},{5,1},{9,5},{13,9},{2,14},{6,2},{... | collective-permute-start | bytes 786440 | tf_op jit(solution)/shard_map/ppermute | solution.py:61
  83.0 12.9 %collective-permute-start.19 = (bf16[512,256]{1,0:T(8,128)(2,1)S(1)}, bf16[512,256]{1,0:T(8,128)(2,1)S(1)}, u32[]{:S(2)}, u32[]{:S(2)}) collective-permute-start(bf16[512,256]{1,0:T(8,128)(2,1)S(1)} %join.1.refs_4_.refs_1_), channel_id=1, source_target_pairs={{0,4},{4,8},{8,12},{12,0},{1,5},{5,9},{9,13},{13,1},{2,6},{6,10},{... | collective-permute-start | bytes 786440 | tf_op jit(solution)/shard_map/ppermute | solution.py:61
  89.8 8.7 %collective-permute-start.21 = (bf16[512,256]{1,0:T(8,128)(2,1)S(1)}, bf16[512,256]{1,0:T(8,128)(2,1)S(1)}, u32[]{:S(2)}, u32[]{:S(2)}) collective-permute-start(bf16[512,256]{1,0:T(8,128)(2,1)S(1)} %collective-permute-done.20.refs_4_), channel_id=1, source_target_pairs={{0,12},{4,0},{8,4},{12,8},{1,13},{5,1},{9,5},{13,9},{2,14},{6,2},{... | collective-permute-start | bytes 786440 | tf_op jit(solution)/shard_map/ppermute | solution.py:61
  99.8 2.7 %collective-permute-start.24 = (bf16[512,1024]{1,0:T(8,128)(2,1)S(1)}, bf16[512,1024]{1,0:T(8,128)(2,1)S(1)}, u32[]{:S(2)}, u32[]{:S(2)}) collective-permute-start(bf16[512,1024]{1,0:T(8,128)(2,1)S(1)} %out_sum.1.refs_0_.refs_5_), channel_id=1, source_target_pairs={{0,1},{1,0},{2,3},{3,2},{4,5},{5,4},{6,7},{7,6},{8,9},{9,8},{10,11... | collective-permute-start | bytes 3145736 | tf_op jit(solution)/shard_map/ppermute | solution.py:65
  104.2 11.5 %collective-permute-start.27 = (bf16[512,256]{1,0:T(8,128)(2,1)S(1)}, bf16[512,256]{1,0:T(8,128)(2,1)S(1)}, u32[]{:S(2)}, u32[]{:S(2)}) collective-permute-start(bf16[512,256]{1,0:T(8,128)(2,1)S(1)} %get-tuple-element.45), channel_id=1, source_target_pairs={{0,4},{4,8},{8,12},{12,0},{1,5},{5,9},{9,13},{13,1},{2,6},{6,10},{... | collective-permute-start | bytes 786440 | tf_op jit(solution)/shard_map/ppermute | solution.py:61
  104.2 25.2 %collective-permute-start.25 = (bf16[256,1024]{1,0:T(8,128)(2,1)S(1)}, bf16[256,1024]{1,0:T(8,128)(2,1)S(1)}, u32[]{:S(2)}, u32[]{:S(2)}) collective-permute-start(bf16[256,1024]{1,0:T(8,128)(2,1)S(1)} %get-tuple-element.43), channel_id=1, source_target_pairs={{0,2},{2,0},{1,3},{3,1},{4,6},{6,4},{5,7},{7,5},{8,10},{10,8},{9,1... | collective-permute-start | bytes 1572872 | tf_op jit(solution)/shard_map/ppermute | solution.py:65
  104.8 13.7 %collective-permute-start.29 = (bf16[512,256]{1,0:T(8,128)(2,1)S(1)}, bf16[512,256]{1,0:T(8,128)(2,1)S(1)}, u32[]{:S(2)}, u32[]{:S(2)}) collective-permute-start(bf16[512,256]{1,0:T(8,128)(2,1)S(1)} %get-tuple-element.47), channel_id=1, source_target_pairs={{0,12},{4,0},{8,4},{12,8},{1,13},{5,1},{9,5},{13,9},{2,14},{6,2},{... | collective-permute-start | bytes 786440 | tf_op jit(solution)/shard_map/ppermute | solution.py:61
  115.7 13.0 %collective-permute-start.28 = (bf16[512,256]{1,0:T(8,128)(2,1)S(1)}, bf16[512,256]{1,0:T(8,128)(2,1)S(1)}, u32[]{:S(2)}, u32[]{:S(2)}) collective-permute-start(bf16[512,256]{1,0:T(8,128)(2,1)S(1)} %add.64.refs_3_), channel_id=1, source_target_pairs={{0,4},{4,8},{8,12},{12,0},{1,5},{5,9},{9,13},{13,1},{2,6},{6,10},{... | collective-permute-start | bytes 786440 | tf_op jit(solution)/shard_map/ppermute | solution.py:61
  128.8 5.0 %collective-permute-start.30 = (bf16[512,128]{1,0:T(8,128)(2,1)S(1)}, bf16[512,128]{1,0:T(8,128)(2,1)S(1)}, u32[]{:S(2)}, u32[]{:S(2)}) collective-permute-start(bf16[512,128]{1,0:T(8,128)(2,1)S(1)} %get-tuple-element.49), channel_id=1, source_target_pairs={{0,2},{2,0},{1,3},{3,1},{4,6},{6,4},{5,7},{7,5},{8,10},{10,8},{9,1... | collective-permute-start | bytes 393224 | tf_op jit(solution)/shard_map/ppermute | solution.py:65
  129.4 19.5 %collective-permute-start.26 = (bf16[256,1024]{1,0:T(8,128)(2,1)S(1)}, bf16[256,1024]{1,0:T(8,128)(2,1)S(1)}, u32[]{:S(2)}, u32[]{:S(2)}) collective-permute-start(bf16[256,1024]{1,0:T(8,128)(2,1)S(1)} %collective-permute-done.25.refs_5_), channel_id=1, source_target_pairs={{0,1},{1,0},{2,3},{3,2},{4,5},{5,4},{6,7},{7,6},{8,9},{9,8},{10,11... | collective-permute-start | bytes 1572872 | tf_op jit(solution)/shard_map/ppermute | solution.py:65
  135.9 12.6 %collective-permute-start.32 = (bf16[1024,128]{1,0:T(8,128)(2,1)S(1)}, bf16[1024,128]{1,0:T(8,128)(2,1)S(1)}, u32[]{:S(2)}, u32[]{:S(2)}) collective-permute-start(bf16[1024,128]{1,0:T(8,128)(2,1)S(1)} %key_grad.1.refs_7_.refs_1_), channel_id=1, source_target_pairs={{0,12},{4,0},{8,4},{12,8},{1,13},{5,1},{9,5},{13,9},{2,14},{6,2},{... | collective-permute-start | bytes 786440 | tf_op jit(solution)/shard_map/ppermute | solution.py:61
  137.7 15.6 %collective-permute-start.31 = (bf16[1024,128]{1,0:T(8,128)(2,1)S(1)}, bf16[1024,128]{1,0:T(8,128)(2,1)S(1)}, u32[]{:S(2)}, u32[]{:S(2)}) collective-permute-start(bf16[1024,128]{1,0:T(8,128)(2,1)S(1)} %key_grad.1.refs_7_.refs_1_), channel_id=1, source_target_pairs={{0,4},{4,8},{8,12},{12,0},{1,5},{5,9},{9,13},{13,1},{2,6},{6,10},{... | collective-permute-start | bytes 786440 | tf_op jit(solution)/shard_map/ppermute | solution.py:61
  148.5 6.4 %collective-permute-start.33 = (bf16[1024,128]{1,0:T(8,128)(2,1)S(1)}, bf16[1024,128]{1,0:T(8,128)(2,1)S(1)}, u32[]{:S(2)}, u32[]{:S(2)}) collective-permute-start(bf16[1024,128]{1,0:T(8,128)(2,1)S(1)} %collective-permute-done.32.refs_4_), channel_id=1, source_target_pairs={{0,12},{4,0},{8,4},{12,8},{1,13},{5,1},{9,5},{13,9},{2,14},{6,2},{... | collective-permute-start | bytes 786440 | tf_op jit(solution)/shard_map/ppermute | solution.py:61
  151.4 1.2 copy-start.1

commit v5 on v4

--- a/solution.py
+++ b/solution.py
@@ -204,20 +204,37 @@
     out[...] = (total + dot(lhs[1, :, at(1 - group, rows)], two[...])).astype(jnp.bfloat16)
 
 
-def grad_term(n, mine, other_core, weight, one, two, tangent_out, share, *refs):
-    outs, grad = refs[:n], refs[n]
-    me = lax.axis_index("seq")
-    cols = outs[0].shape[1] // 2
+def grad_far(n, mine, other_core, weight, one, two, tangent_out, share, out):
+    me, group = lax.axis_index("seq"), lax.axis_index("groups")
+    cols = out.shape[1] // 2
     tangent_out[...] = (mine[...].astype(jnp.float32) + other_core[...].astype(jnp.float32)).astype(jnp.bfloat16)
     share[...] = tangent_out[at(lax.axis_index("rep"), share.shape[0]), :]
-    group = lax.axis_index("groups")
+    where = lax.rem(me + n // 2, n)
+    out[:, :cols] = dot(tangent_out[...], weight[at(where, cols), :], 1, 1).astype(jnp.bfloat16)
+    near = where // (n // 2) == group
+
+    @pl.when(near)
+    def _():
+        rows = one[at(lax.rem(where, n // 2), cols), :]
+        out[:, cols:] = dot(tangent_out[...], rows, 1, 1).astype(jnp.bfloat16)
+
+    @pl.when(jnp.logical_not(near))
+    def _():
+        rows = two[at(lax.rem(where, n // 2), cols), :]
+        out[:, cols:] = dot(tangent_out[...], rows, 1, 1).astype(jnp.bfloat16)
+
+
+def grad_term(n, tangent_out, weight, one, two, *refs):
+    outs, grad = refs[: n - 1], refs[n - 1]
+    me, group = lax.axis_index("seq"), lax.axis_index("groups")
+    cols = outs[0].shape[1] // 2
     rows = one.shape[0]
     grad[0] = dot(tangent_out[...], weight[...], 1, 1).astype(jnp.bfloat16)
     grad[1, :, at(group, rows)] = dot(tangent_out[...], one[...], 1, 1).astype(jnp.bfloat16)
     grad[1, :, at(1 - group, rows)] = dot(tangent_out[...], two[...], 1, 1).astype(jnp.bfloat16)
     for d in range(2):
-        for k in range(n):
-            outs[k][:, d * cols : (d + 1) * cols] = grad[d, :, at(lax.rem(me + k, n), cols)]
+        for j, k in enumerate(k for k in range(n) if k != n // 2):
+            outs[j][:, d * cols : (d + 1) * cols] = grad[d, :, at(lax.rem(me + k, n), cols)]
 
 
 def add_grad(n, *refs):
@@ -342,10 +359,13 @@
         [*att, swap(away, "head"), out_probe, other_probe], scratch=[held(half, block)])
     (mine,) = call(
         part(out_sum, n), [bf(half, slab)], [base, *tan, out_weight, *weights], scratch=[held(2, half, block)])
-    tangent_out, share, *grads = call(
-        part(grad_term, n), [bf(half, slab), bf(half // 2, slab)] + [bf(half, 2 * cols)] * n,
-        [mine, swap(mine, "rep"), out_weight, *weights],
+    tangent_out, share, far = call(
+        part(grad_far, n), [bf(half, slab), bf(half // 2, slab), bf(half, 2 * cols)],
+        [mine, swap(mine, "rep"), out_weight, *weights])
+    grads = call(
+        part(grad_term, n), [bf(half, 2 * cols)] * (n - 1), [tangent_out, out_weight, *weights],
         scratch=[held(2, half, block)])
+    grads = [*grads[: n // 2], far, *grads[n // 2 :]]
     home, away = call(part(add_grad, 3), [bf(half, cols)] * 2, summed(grads))
     (value_grad,) = call(
         key_grad, [bf(tokens, cols)], [home, swap(away, "head"), probs],
@@ -364,7 +384,7 @@
 def body(*args):
     tok, cols = args[1].shape
     n = lax.axis_size("seq")
-    even = cols % (n * 128) == 0 and tok % 64 == 0 and tok * n % 64 == 0
+    even = n % 2 == 0 and cols % (n * 128) == 0 and tok % 64 == 0 and tok * n % 64 == 0
     if even and all(lax.axis_size(axis) == 2 for axis in ("groups", "head", "rep")):
         return by_heads(*args)
     return by_tokens(*args)

time: 157 us -> 157 us (level)
    ppermute x21, waiting for transfers between devices: 58.8 us -> 57 us  [ahead(): return lax.ppermute(x, 'seq', [(i, (i + k) % n) for i in range(n)])]
    pallas_call x16 -> x17, Pallas kernels: 23.3 us -> 24.1 us  [__call__(): pl.pallas_call(body, out_shape=outs, in_specs=specs, out_specs=out_specs,...]
  transfers between devices with their start and end apart: 34 -> 34, of which waited for: 18 -> 18; matrix products, arithmetic and copies ran while one was open for 1% -> 1% of each run, Pallas kernels for 11% -> 12%
where the time goes in v5:
time: 157 us; the launch traced here: 156 us
  waiting for transfers between devices  76.3 us (49%)
  starting transfers between devices  50.3 us (32%)
  Pallas kernels  24.1 us (15%)
  local copies, waits for them, and re-layouts  4.53 us (3%)
    ppermute x21, waiting for transfers between devices, ahead(): return lax.ppermute(x, 'seq', [(i, (i + k) % n) for i in range(n)])  57 us
    ppermute x21, starting transfers between devices, ahead(): return lax.ppermute(x, 'seq', [(i, (i + k) % n) for i in range(n)])  38.2 us
    pallas_call x17, Pallas kernels, __call__(): pl.pallas_call(body, out_shape=outs, in_specs=specs, out_specs=out_specs,...  24.1 us
    ppermute x13, waiting for transfers between devices, swap(): return lax.ppermute(x, axis, [(0, 1), (1, 0)])  19.3 us
    ppermute x13, starting transfers between devices, swap(): return lax.ppermute(x, axis, [(0, 1), (1, 0)])  12.1 us
  transfers between devices with their start and end apart: 34, of which 18 were waited for; matrix products, arithmetic and copies ran while one was open for 1% of the time, Pallas kernels for 12%

profile of v5, /device:TPU:0, one launch (start us, length us, event | category | flops | bytes accessed | tf_op | source)
XLA Modules:
  0.0 156.4 jit_solution(4822842216956845658)
XLA Ops:
  0.7 1.1 fusion
  1.8 3.1 %collective-permute-start.1 = (bf16[64,1024]{1,0:T(8,128)(2,1)S(1)}, bf16[64,1024]{1,0:T(8,128)(2,1)S(1)}, u32[]{:S(2)}, u32[]{:S(2)}) collective-permute-start(bf16[64,1024]{1,0:T(8,128)(2,1)S(1)} %get-tuple-element.51), channel_id=1, source_target_pairs={{0,4},{4,8},{8,12},{12,0},{1,5},{5,9},{9,13},{13,1},{2,6},{6,10},{... | collective-permute-start | bytes 393224 | tf_op jit(solution)/shard_map/ppermute | solution.py:61
  4.9 2.1 %collective-permute-start = (bf16[64,1024]{1,0:T(8,128)(2,1)S(1)}, bf16[64,1024]{1,0:T(8,128)(2,1)S(1)}, u32[]{:S(2)}, u32[]{:S(2)}) collective-permute-start(bf16[64,1024]{1,0:T(8,128)(2,1)S(1)} %get-tuple-element.52), channel_id=1, source_target_pairs={{0,12},{4,0},{8,4},{12,8},{1,13},{5,1},{9,5},{13,9},{2,14},{6,2},{... | collective-permute-start | bytes 393224 | tf_op jit(solution)/shard_map/ppermute | solution.py:61
  7.0 0.9 collective-permute-start.2
  7.9 0.9 dynamic-slice_bitcast_fusion.2
  8.9 1.2 dynamic-slice_bitcast_fusion
  10.1 1.1 collective-permute-done.1.refs_1_
  11.3 8.2 %collective-permute-start.7 = (bf16[3,256,128]{2,1,0:T(8,128)(2,1)S(1)}, bf16[3,256,128]{2,1,0:T(8,128)(2,1)S(1)}, u32[]{:S(2)}, u32[]{:S(2)}) collective-permute-start(bf16[3,256,128]{2,1,0:T(8,128)(2,1)S(1)} %pad_maximum_fusion.1), channel_id=1, source_target_pairs={{0,8},{4,12},{8,0},{12,4},{1,9},{5,13},{9,1},{13,5},{2,10},{6,14},... | collective-permute-start | bytes 589832 | tf_op jit(solution)/shard_map/ppermute | solution.py:61
  19.4 1.5 collective-permute-start.4
  20.9 0.5 collective-permute-start.3
  21.4 5.9 %collective-permute-done.2.refs_2_ = bf16[64,1024]{1,0:T(8,128)(2,1)S(1)} collective-permute-done((bf16[64,1024]{1,0:T(8,128)(2,1)S(1)}, bf16[64,1024]{1,0:T(8,128)(2,1)S(1)}, u32[]{:S(2)}, u32[]{:S(2)}) %collective-permute-start.2) | collective-permute-done | bytes 131104 | tf_op jit(solution)/shard_map/ppermute | solution.py:61
  27.4 1.5 collective-permute-start.5
  28.9 3.8 %collective-permute-done.5.refs_5_ = bf16[64,1024]{1,0:T(8,128)(2,1)S(1)} collective-permute-done((bf16[64,1024]{1,0:T(8,128)(2,1)S(1)}, bf16[64,1024]{1,0:T(8,128)(2,1)S(1)}, u32[]{:S(2)}, u32[]{:S(2)}) %collective-permute-start.5) | collective-permute-done | bytes 131104 | tf_op jit(solution)/shard_map/ppermute | solution.py:65
  32.7 0.1 pack.1
  32.8 0.1 collective-permute-start.8
  33.0 2.1 %collective-permute-done.8.refs_2_ = bf16[6,64,1024]{2,1,0:T(8,128)(2,1)S(1)} collective-permute-done((bf16[6,64,1024]{2,1,0:T(8,128)(2,1)S(1)}, bf16[6,64,1024]{2,1,0:T(8,128)(2,1)S(1)}, u32[]{:S(2)}, u32[]{:S(2)}) %collective-permute-start.8) | collective-permute-done | bytes 786464 | tf_op jit(solution)/shard_map/ppermute | solution.py:65
  35.2 1.7 %tangent_term.1 = (bf16[1024,1024]{1,0:T(8,128)(2,1)S(1)}, bf16[1024,128]{1,0:T(8,128)(2,1)S(1)}, bf16[1024,128]{1,0:T(8,128)(2,1)S(1)}, bf16[1024,128]{1,0:T(8,128)(2,1)S(1)}, bf16[1024,128]{1,0:T(8,128)(2,1)S(1)}) custom-call(bf16[256,4096]{1,0:T(8,128)(2,1)S(1)} %copy-done.2, bf16[6,64,1024]{2,1,0:T(8,128)(2,1)S(1)} %get-tuple-element.28.refs_1_.refs_4_, ...), custom_call_target="tpu_custom_call" | custom-call | flops 1 | bytes 1 | tf_op jit(solution)/shard_map/tangent_term/pallas_call | solution.py:33
  36.9 1.6 collective-permute-start.18
  38.5 3.7 %collective-permute-start.15 = (bf16[1024,128]{1,0:T(8,128)(2,1)S(1)}, bf16[1024,128]{1,0:T(8,128)(2,1)S(1)}, u32[]{:S(2)}, u32[]{:S(2)}) collective-permute-start(bf16[1024,128]{1,0:T(8,128)(2,1)S(1)} %get-tuple-element.36), channel_id=1, source_target_pairs={{0,12},{4,0},{8,4},{12,8},{1,13},{5,1},{9,5},{13,9},{2,14},{6,2},{... | collective-permute-start | bytes 786440 | tf_op jit(solution)/shard_map/ppermute | solution.py:61
  42.3 7.8 %attend.1 = (bf16[2,1024,1024]{2,1,0:T(8,128)(2,1)S(1)}, bf16[1024,128]{1,0:T(8,128)(2,1)S(1)}) custom-call(bf16[256,512]{1,0:T(8,128)(2,1)S(1)} %copy-done.5, bf16[256,512]{1,0:T(8,128)(2,1)S(1)} %copy-done.7, bf16[256,512]{1,0:T(8,128)(2,1)S(1)} %copy-done.6, bf16[3,256,128]{2,1,0:T(8,128)(2,1)S(1)} %collective-permute-done.6.refs_7_.refs_3_, ...), custom_call_target="tpu_custom_call" | custom-call | flops 1 | bytes 1 | tf_op jit(solution)/shard_map/attend/pallas_call | solution.py:33
  50.0 0.5 collective-permute-start.11
  50.5 1.5 collective-permute-start.22
  52.1 0.7 collective-permute-start.14
  52.8 0.5 collective-permute-start.10
  53.3 4.8 %collective-permute-done.11.refs_3_ = bf16[1024,128]{1,0:T(8,128)(2,1)S(1)} collective-permute-done((bf16[1024,128]{1,0:T(8,128)(2,1)S(1)}, bf16[1024,128]{1,0:T(8,128)(2,1)S(1)}, u32[]{:S(2)}, u32[]{:S(2)}) %collective-permute-start.11) | collective-permute-done | bytes 262176 | tf_op jit(solution)/shard_map/ppermute | solution.py:61
  58.1 3.5 %collective-permute-start.12 = (bf16[1024,128]{1,0:T(8,128)(2,1)S(1)}, bf16[1024,128]{1,0:T(8,128)(2,1)S(1)}, u32[]{:S(2)}, u32[]{:S(2)}) collective-permute-start(bf16[1024,128]{1,0:T(8,128)(2,1)S(1)} %collective-permute-done.11.refs_3_), channel_id=1, source_target_pairs={{0,12},{4,0},{8,4},{12,8},{1,13},{5,1},{9,5},{13,9},{2,14},{6,2},{... | collective-permute-start | bytes 786440 | tf_op jit(solution)/shard_map/ppermute | solution.py:61
  61.6 3.3 %collective-permute-done.14.refs_1_ = bf16[1024,128]{1,0:T(8,128)(2,1)S(1)} collective-permute-done((bf16[1024,128]{1,0:T(8,128)(2,1)S(1)}, bf16[1024,128]{1,0:T(8,128)(2,1)S(1)}, u32[]{:S(2)}, u32[]{:S(2)}) %collective-permute-start.14) | collective-permute-done | bytes 262176 | tf_op jit(solution)/shard_map/ppermute | solution.py:61
  64.9 1.5 attend_tan.1
  66.4 1.6 %collective-permute-start.16 = (bf16[512,128]{1,0:T(8,128)(2,1)S(1)}, bf16[512,128]{1,0:T(8,128)(2,1)S(1)}, u32[]{:S(2)}, u32[]{:S(2)}) collective-permute-start(bf16[512,128]{1,0:T(8,128)(2,1)S(1)} %get-tuple-element.38), channel_id=1, source_target_pairs={{0,2},{2,0},{1,3},{3,1},{4,6},{6,4},{5,7},{7,5},{8,10},{10,8},{9,1... | collective-permute-start | bytes 393224 | tf_op jit(solution)/shard_map/ppermute | solution.py:65
  68.0 2.5 %collective-permute-done.10.refs_2_.refs_1_ = bf16[1024,128]{1,0:T(8,128)(2,1)S(1)} collective-permute-done((bf16[1024,128]{1,0:T(8,128)(2,1)S(1)}, bf16[1024,128]{1,0:T(8,128)(2,1)S(1)}, u32[]{:S(2)}, u32[]{:S(2)}) %collective-permute-start.10) | collective-permute-done | bytes 262176 | tf_op jit(solution)/shard_map/ppermute | solution.py:61
  70.4 5.8 %collective-permute-done.16.refs_1_ = bf16[512,128]{1,0:T(8,128)(2,1)S(1)} collective-permute-done((bf16[512,128]{1,0:T(8,128)(2,1)S(1)}, bf16[512,128]{1,0:T(8,128)(2,1)S(1)}, u32[]{:S(2)}, u32[]{:S(2)}) %collective-permute-start.16) | collective-permute-done | bytes 131104 | tf_op jit(solution)/shard_map/ppermute | solution.py:65
  76.3 0.2 cut_rows.1.refs_7_
  76.5 1.6 collective-permute-start.17
  78.0 1.5 collective-permute-start.23
  79.6 3.5 %collective-permute-start.20 = (bf16[512,256]{1,0:T(8,128)(2,1)S(1)}, bf16[512,256]{1,0:T(8,128)(2,1)S(1)}, u32[]{:S(2)}, u32[]{:S(2)}) collective-permute-start(bf16[512,256]{1,0:T(8,128)(2,1)S(1)} %join.1.refs_4_.refs_1_), channel_id=1, source_target_pairs={{0,12},{4,0},{8,4},{12,8},{1,13},{5,1},{9,5},{13,9},{2,14},{6,2},{... | collective-permute-start | bytes 786440 | tf_op jit(solution)/shard_map/ppermute | solution.py:61
  83.0 6.8 %collective-permute-done.20.refs_4_ = bf16[512,256]{1,0:T(8,128)(2,1)S(1)} collective-permute-done((bf16[512,256]{1,0:T(8,128)(2,1)S(1)}, bf16[512,256]{1,0:T(8,128)(2,1)S(1)}, u32[]{:S(2)}, u32[]{:S(2)}) %collective-permute-start.20) | collective-permute-done | bytes 262176 | tf_op jit(solution)/shard_map/ppermute | solution.py:61
  89.8 4.3 %collective-permute-start.21 = (bf16[512,256]{1,0:T(8,128)(2,1)S(1)}, bf16[512,256]{1,0:T(8,128)(2,1)S(1)}, u32[]{:S(2)}, u32[]{:S(2)}) collective-permute-start(bf16[512,256]{1,0:T(8,128)(2,1)S(1)} %collective-permute-done.20.refs_4_), channel_id=1, source_target_pairs={{0,12},{4,0},{8,4},{12,8},{1,13},{5,1},{9,5},{13,9},{2,14},{6,2},{... | collective-permute-start | bytes 786440 | tf_op jit(solution)/shard_map/ppermute | solution.py:61
  94.1 1.3 out_term.1.refs_0_.refs_8_
  95.4 0.5 collective-permute-done.19.refs_2_
  95.9 2.6 %collective-permute-done.21.refs_3_ = bf16[512,256]{1,0:T(8,128)(2,1)S(1)} collective-permute-done((bf16[512,256]{1,0:T(8,128)(2,1)S(1)}, bf16[512,256]{1,0:T(8,128)(2,1)S(1)}, u32[]{:S(2)}, u32[]{:S(2)}) %collective-permute-start.21) | collective-permute-done | bytes 262176 | tf_op jit(solution)/shard_map/ppermute | solution.py:61
  98.4 1.3 out_sum.1.refs_0_.refs_5_
  99.8 0.1 collective-permute-start.24
  99.9 2.6 %collective-permute-done.24.refs_1_ = bf16[512,1024]{1,0:T(8,128)(2,1)S(1)} collective-permute-done((bf16[512,1024]{1,0:T(8,128)(2,1)S(1)}, bf16[512,1024]{1,0:T(8,128)(2,1)S(1)}, u32[]{:S(2)}, u32[]{:S(2)}) %collective-permute-start.24) | collective-permute-done | bytes 1048608 | tf_op jit(solution)/shard_map/ppermute | solution.py:65
  102.5 1.0 grad_far.1
  103.6 0.6 collective-permute-start.25
  104.2 1.5 grad_term.1
  105.7 4.3 %collective-permute-start.29 = (bf16[512,256]{1,0:T(8,128)(2,1)S(1)}, bf16[512,256]{1,0:T(8,128)(2,1)S(1)}, u32[]{:S(2)}, u32[]{:S(2)}) collective-permute-start(bf16[512,256]{1,0:T(8,128)(2,1)S(1)} %get-tuple-element.47), channel_id=1, source_target_pairs={{0,12},{4,0},{8,4},{12,8},{1,13},{5,1},{9,5},{13,9},{2,14},{6,2},{... | collective-permute-start | bytes 786440 | tf_op jit(solution)/shard_map/ppermute | solution.py:61
  110.1 5.0 %collective-permute-done.27.refs_0_ = bf16[512,256]{1,0:T(8,128)(2,1)S(1)} collective-permute-done((bf16[512,256]{1,0:T(8,128)(2,1)S(1)}, bf16[512,256]{1,0:T(8,128)(2,1)S(1)}, u32[]{:S(2)}, u32[]{:S(2)}) %collective-permute-start.27) | collective-permute-done | bytes 262176 | tf_op jit(solution)/shard_map/ppermute | solution.py:61
  115.1 0.2 collective-permute-start.28
  115.4 4.1 %collective-permute-done.29.refs_2_ = bf16[512,256]{1,0:T(8,128)(2,1)S(1)} collective-permute-done((bf16[512,256]{1,0:T(8,128)(2,1)S(1)}, bf16[512,256]{1,0:T(8,128)(2,1)S(1)}, u32[]{:S(2)}, u32[]{:S(2)}) %collective-permute-start.29) | collective-permute-done | bytes 262176 | tf_op jit(solution)/shard_map/ppermute | solution.py:61
  119.4 8.5 %collective-permute-done.28.refs_1_ = bf16[512,256]{1,0:T(8,128)(2,1)S(1)} collective-permute-done((bf16[512,256]{1,0:T(8,128)(2,1)S(1)}, bf16[512,256]{1,0:T(8,128)(2,1)S(1)}, u32[]{:S(2)}, u32[]{:S(2)}) %collective-permute-start.28) | collective-permute-done | bytes 262176 | tf_op jit(solution)/shard_map/ppermute | solution.py:61
  127.9 0.1 add_grad.1
  128.0 0.1 collective-permute-start.30
  128.2 4.9 %collective-permute-done.30.refs_1_ = bf16[512,128]{1,0:T(8,128)(2,1)S(1)} collective-permute-done((bf16[512,128]{1,0:T(8,128)(2,1)S(1)}, bf16[512,128]{1,0:T(8,128)(2,1)S(1)}, u32[]{:S(2)}, u32[]{:S(2)}) %collective-permute-start.30) | collective-permute-done | bytes 131104 | tf_op jit(solution)/shard_map/ppermute | solution.py:65
  133.0 2.1 %key_grad.1.refs_7_.refs_1_ = bf16[1024,128]{1,0:T(8,128)(2,1)S(1)} custom-call(bf16[512,128]{1,0:T(8,128)(2,1)S(1)} %get-tuple-element.48.refs_0_.refs_3_, bf16[512,128]{1,0:T(8,128)(2,1)S(1)} %collective-permute-done.30.refs_1_, bf16[2,1024,1024]{2,1,0:T(8,128)(2,1)S(1)} %get-tuple-element.35.refs_2_.refs_3_, ...), custom_call_target="tpu_custom_call" | custom-call | flops 1 | bytes 1 | tf_op jit(solution)/shard_map/key_grad/pallas_call | solution.py:33
  135.1 1.8 %collective-permute-start.32 = (bf16[1024,128]{1,0:T(8,128)(2,1)S(1)}, bf16[1024,128]{1,0:T(8,128)(2,1)S(1)}, u32[]{:S(2)}, u32[]{:S(2)}) collective-permute-start(bf16[1024,128]{1,0:T(8,128)(2,1)S(1)} %key_grad.1.refs_7_.refs_1_), channel_id=1, source_target_pairs={{0,12},{4,0},{8,4},{12,8},{1,13},{5,1},{9,5},{13,9},{2,14},{6,2},{... | collective-permute-start | bytes 786440 | tf_op jit(solution)/shard_map/ppermute | solution.py:61
  136.9 0.3 collective-permute-start.31
  137.2 10.5 %collective-permute-done.32.refs_4_ = bf16[1024,128]{1,0:T(8,128)(2,1)S(1)} collective-permute-done((bf16[1024,128]{1,0:T(8,128)(2,1)S(1)}, bf16[1024,128]{1,0:T(8,128)(2,1)S(1)}, u32[]{:S(2)}, u32[]{:S(2)}) %collective-permute-start.32) | collective-permute-done | bytes 262176 | tf_op jit(solution)/shard_map/ppermute | solution.py:61
  147.7 0.4 collective-permute-start.33
  148.1 2.5 %out_product.1.refs_1_ = bf16[512,1024]{1,0:T(8,128)(2,1)} custom-call(bf16[1024,128]{1,0:T(8,128)(2,1)S(1)} %get-tuple-element.31.refs_0_, bf16[1024,128]{1,0:T(8,128)(2,1)S(1)} %collective-permute-done.10.refs_2_.refs_1_, bf16[1024,128]{1,0:T(8,128)(2,1)S(1)} %collective-permute-done.12.refs_2_, bf16[1024,128]{1,0:T(8,128)(2,1)S(1)} %collective-permute-done.11.refs_3_, ...), custom_call_target="tpu_custom_call" | custom-call | flops 1 | bytes 1 | tf_op jit(solution)/shard_map/out_product/pallas_call | solution.py:33
  150.6 1.2 copy-done.1
  151.8 0.6 flip.1.refs_0_.refs_5_
  152.5 1.5 collective-permute-done.33.refs_3_
  154.0 2.3 %value_product.1 = bf16[1024,512]{1,0:T(8,128)(2,1)} custom-call(bf16[1024,1024]{1,0:T(8,128)(2,1)S(1)} %flip.1.refs_0_.refs_5_, bf16[1024,128]{1,0:T(8,128)(2,1)S(1)} %key_grad.1.refs_7_.refs_1_, bf16[1024,128]{1,0:T(8,128)(2,1)S(1)} %collective-permute-done.31.refs_2_, bf16[1024,128]{1,0:T(8,128)(2,1)S(1)} %collective-permute-done.33.refs_3_, ...), custom_call_target="tpu_custom_call" | custom-call | flops 1 | bytes 1 | tf_op jit(solution)/shard_map/value_product/pallas_call | solution.py:33
  (43 shorter events, 0.6 us)
Async XLA Ops:
  0.6 32.1 %copy-start = (bf16[512,1024]{1,0:T(8,128)(2,1)S(1)}, bf16[512,1024]{1,0:T(8,128)(2,1)}, u32[]{:S(2)}) copy-start(bf16[512,1024]{1,0:T(8,128)(2,1)} %refs_1_.3) | copy-start | bytes 3145732
  1.8 9.4 %collective-permute-start.1 = (bf16[64,1024]{1,0:T(8,128)(2,1)S(1)}, bf16[64,1024]{1,0:T(8,128)(2,1)S(1)}, u32[]{:S(2)}, u32[]{:S(2)}) collective-permute-start(bf16[64,1024]{1,0:T(8,128)(2,1)S(1)} %get-tuple-element.51), channel_id=1, source_target_pairs={{0,4},{4,8},{8,12},{12,0},{1,5},{5,9},{9,13},{13,1},{2,6},{6,10},{... | collective-permute-start | bytes 393224 | tf_op jit(solution)/shard_map/ppermute | solution.py:61
  4.9 16.0 %collective-permute-start = (bf16[64,1024]{1,0:T(8,128)(2,1)S(1)}, bf16[64,1024]{1,0:T(8,128)(2,1)S(1)}, u32[]{:S(2)}, u32[]{:S(2)}) collective-permute-start(bf16[64,1024]{1,0:T(8,128)(2,1)S(1)} %get-tuple-element.52), channel_id=1, source_target_pairs={{0,12},{4,0},{8,4},{12,8},{1,13},{5,1},{9,5},{13,9},{2,14},{6,2},{... | collective-permute-start | bytes 393224 | tf_op jit(solution)/shard_map/ppermute | solution.py:61
  7.0 20.4 %collective-permute-start.2 = (bf16[64,1024]{1,0:T(8,128)(2,1)S(1)}, bf16[64,1024]{1,0:T(8,128)(2,1)S(1)}, u32[]{:S(2)}, u32[]{:S(2)}) collective-permute-start(bf16[64,1024]{1,0:T(8,128)(2,1)S(1)} %get-tuple-element.50), channel_id=1, source_target_pairs={{0,8},{4,12},{8,0},{12,4},{1,9},{5,13},{9,1},{13,5},{2,10},{6,14},... | collective-permute-start | bytes 393224 | tf_op jit(solution)/shard_map/ppermute | solution.py:61
  8.9 26.3 %copy-start.2 = (bf16[256,4096]{1,0:T(8,128)(2,1)S(1)}, bf16[256,4096]{1,0:T(8,128)(2,1)}, u32[]{:S(2)}) copy-start(bf16[256,4096]{1,0:T(8,128)(2,1)} %refs_0_.2) | copy-start | bytes 6291460
  8.9 26.3 %copy-start.3 = (bf16[1024,512]{1,0:T(8,128)(2,1)S(1)}, bf16[1024,512]{1,0:T(8,128)(2,1)}, u32[]{:S(2)}) copy-start(bf16[1024,512]{1,0:T(8,128)(2,1)} %refs_3_.1) | copy-start | bytes 3145732
  11.3 21.4 %collective-permute-start.7 = (bf16[3,256,128]{2,1,0:T(8,128)(2,1)S(1)}, bf16[3,256,128]{2,1,0:T(8,128)(2,1)S(1)}, u32[]{:S(2)}, u32[]{:S(2)}) collective-permute-start(bf16[3,256,128]{2,1,0:T(8,128)(2,1)S(1)} %pad_maximum_fusion.1), channel_id=1, source_target_pairs={{0,8},{4,12},{8,0},{12,4},{1,9},{5,13},{9,1},{13,5},{2,10},{6,14},... | collective-permute-start | bytes 589832 | tf_op jit(solution)/shard_map/ppermute | solution.py:61
  19.4 13.3 %collective-permute-start.6 = (bf16[3,256,128]{2,1,0:T(8,128)(2,1)S(1)}, bf16[3,256,128]{2,1,0:T(8,128)(2,1)S(1)}, u32[]{:S(2)}, u32[]{:S(2)}) collective-permute-start(bf16[3,256,128]{2,1,0:T(8,128)(2,1)S(1)} %pad_maximum_fusion), channel_id=1, source_target_pairs={{0,4},{4,8},{8,12},{12,0},{1,5},{5,9},{9,13},{13,1},{2,6},{6,10},{... | collective-permute-start | bytes 589832 | tf_op jit(solution)/shard_map/ppermute | solution.py:61
  19.4 9.5 %collective-permute-start.4 = (bf16[64,1024]{1,0:T(8,128)(2,1)S(1)}, bf16[64,1024]{1,0:T(8,128)(2,1)S(1)}, u32[]{:S(2)}, u32[]{:S(2)}) collective-permute-start(bf16[64,1024]{1,0:T(8,128)(2,1)S(1)} %collective-permute-done.1.refs_1_), channel_id=1, source_target_pairs={{0,2},{2,0},{1,3},{3,1},{4,6},{6,4},{5,7},{7,5},{8,10},{10,8},{9,1... | collective-permute-start | bytes 393224 | tf_op jit(solution)/shard_map/ppermute | solution.py:65
  20.9 8.0 %collective-permute-start.3 = (bf16[64,1024]{1,0:T(8,128)(2,1)S(1)}, bf16[64,1024]{1,0:T(8,128)(2,1)S(1)}, u32[]{:S(2)}, u32[]{:S(2)}) collective-permute-start(bf16[64,1024]{1,0:T(8,128)(2,1)S(1)} %collective-permute-done.refs_0_), channel_id=1, source_target_pairs={{0,2},{2,0},{1,3},{3,1},{4,6},{6,4},{5,7},{7,5},{8,10},{10,8},{9,1... | collective-permute-start | bytes 393224 | tf_op jit(solution)/shard_map/ppermute | solution.py:65
  27.4 5.3 %collective-permute-start.5 = (bf16[64,1024]{1,0:T(8,128)(2,1)S(1)}, bf16[64,1024]{1,0:T(8,128)(2,1)S(1)}, u32[]{:S(2)}, u32[]{:S(2)}) collective-permute-start(bf16[64,1024]{1,0:T(8,128)(2,1)S(1)} %collective-permute-done.2.refs_2_), channel_id=1, source_target_pairs={{0,2},{2,0},{1,3},{3,1},{4,6},{6,4},{5,7},{7,5},{8,10},{10,8},{9,1... | collective-permute-start | bytes 393224 | tf_op jit(solution)/shard_map/ppermute | solution.py:65
  32.8 2.4 %collective-permute-start.8 = (bf16[6,64,1024]{2,1,0:T(8,128)(2,1)S(1)}, bf16[6,64,1024]{2,1,0:T(8,128)(2,1)S(1)}, u32[]{:S(2)}, u32[]{:S(2)}) collective-permute-start(bf16[6,64,1024]{2,1,0:T(8,128)(2,1)S(1)} %get-tuple-element.28.refs_1_.refs_4_), channel_id=1, source_target_pairs={{0,1},{1,0},{2,3},{3,2},{4,5},{5,4},{6,7},{7,6},{8,9},{9,8},{10,11... | collective-permute-start | bytes 2359304 | tf_op jit(solution)/shard_map/ppermute | solution.py:65
  32.9 4.0 %copy-start.4 = (bf16[512,1024]{1,0:T(8,128)(2,1)S(1)}, bf16[512,1024]{1,0:T(8,128)(2,1)}, u32[]{:S(2)}) copy-start(bf16[512,1024]{1,0:T(8,128)(2,1)} %refs_5_.2) | copy-start | bytes 3145732
  32.9 9.3 %copy-start.5 = (bf16[256,512]{1,0:T(8,128)(2,1)S(1)}, bf16[256,512]{1,0:T(8,128)(2,1)}, u32[]{:S(2)}) copy-start(bf16[256,512]{1,0:T(8,128)(2,1)} %refs_0_.3) | copy-start | bytes 786436
  33.0 9.3 %copy-start.6 = (bf16[256,512]{1,0:T(8,128)(2,1)S(1)}, bf16[256,512]{1,0:T(8,128)(2,1)}, u32[]{:S(2)}) copy-start(bf16[256,512]{1,0:T(8,128)(2,1)} %refs_2_.2) | copy-start | bytes 786436
  33.0 9.3 %copy-start.7 = (bf16[256,512]{1,0:T(8,128)(2,1)S(1)}, bf16[256,512]{1,0:T(8,128)(2,1)}, u32[]{:S(2)}) copy-start(bf16[256,512]{1,0:T(8,128)(2,1)} %refs_1_.2) | copy-start | bytes 786436
  33.0 9.3 %collective-permute-start.9 = (bf16[3,256,128]{2,1,0:T(8,128)(2,1)S(1)}, bf16[3,256,128]{2,1,0:T(8,128)(2,1)S(1)}, u32[]{:S(2)}, u32[]{:S(2)}) collective-permute-start(bf16[3,256,128]{2,1,0:T(8,128)(2,1)S(1)} %pad_maximum_fusion.2), channel_id=1, source_target_pairs={{0,12},{4,0},{8,4},{12,8},{1,13},{5,1},{9,5},{13,9},{2,14},{6,2},{... | collective-permute-start | bytes 589832 | tf_op jit(solution)/shard_map/ppermute | solution.py:61
  36.9 15.1 %collective-permute-start.13 = (bf16[1024,128]{1,0:T(8,128)(2,1)S(1)}, bf16[1024,128]{1,0:T(8,128)(2,1)S(1)}, u32[]{:S(2)}, u32[]{:S(2)}) collective-permute-start(bf16[1024,128]{1,0:T(8,128)(2,1)S(1)} %get-tuple-element.33), channel_id=1, source_target_pairs={{0,4},{4,8},{8,12},{12,0},{1,5},{5,9},{9,13},{13,1},{2,6},{6,10},{... | collective-permute-start | bytes 786440 | tf_op jit(solution)/shard_map/ppermute | solution.py:61
  36.9 57.1 %collective-permute-start.18 = (bf16[512,1024]{1,0:T(8,128)(2,1)S(1)}, bf16[512,1024]{1,0:T(8,128)(2,1)S(1)}, u32[]{:S(2)}, u32[]{:S(2)}) collective-permute-start(bf16[512,1024]{1,0:T(8,128)(2,1)S(1)} %copy-done.4), channel_id=1, source_target_pairs={{0,2},{2,0},{1,3},{3,1},{4,6},{6,4},{5,7},{7,5},{8,10},{10,8},{9,1... | collective-permute-start | bytes 3145736 | tf_op jit(solution)/shard_map/ppermute | solution.py:65
  38.5 14.3 %collective-permute-start.15 = (bf16[1024,128]{1,0:T(8,128)(2,1)S(1)}, bf16[1024,128]{1,0:T(8,128)(2,1)S(1)}, u32[]{:S(2)}, u32[]{:S(2)}) collective-permute-start(bf16[1024,128]{1,0:T(8,128)(2,1)S(1)} %get-tuple-element.36), channel_id=1, source_target_pairs={{0,12},{4,0},{8,4},{12,8},{1,13},{5,1},{9,5},{13,9},{2,14},{6,2},{... | collective-permute-start | bytes 786440 | tf_op jit(solution)/shard_map/ppermute | solution.py:61
  50.0 8.0 %collective-permute-start.11 = (bf16[1024,128]{1,0:T(8,128)(2,1)S(1)}, bf16[1024,128]{1,0:T(8,128)(2,1)S(1)}, u32[]{:S(2)}, u32[]{:S(2)}) collective-permute-start(bf16[1024,128]{1,0:T(8,128)(2,1)S(1)} %get-tuple-element.31.refs_0_), channel_id=1, source_target_pairs={{0,12},{4,0},{8,4},{12,8},{1,13},{5,1},{9,5},{13,9},{2,14},{6,2},{... | collective-permute-start | bytes 786440 | tf_op jit(solution)/shard_map/ppermute | solution.py:61
  50.5 27.5 %collective-permute-start.22 = (bf16[256,1024]{1,0:T(8,128)(2,1)S(1)}, bf16[256,1024]{1,0:T(8,128)(2,1)S(1)}, u32[]{:S(2)}, u32[]{:S(2)}) collective-permute-start(bf16[256,1024]{1,0:T(8,128)(2,1)S(1)} %get-tuple-element.41), channel_id=1, source_target_pairs={{0,2},{2,0},{1,3},{3,1},{4,6},{6,4},{5,7},{7,5},{8,10},{10,8},{9,1... | collective-permute-start | bytes 1572872 | tf_op jit(solution)/shard_map/ppermute | solution.py:65
  52.1 12.8 %collective-permute-start.14 = (bf16[1024,128]{1,0:T(8,128)(2,1)S(1)}, bf16[1024,128]{1,0:T(8,128)(2,1)S(1)}, u32[]{:S(2)}, u32[]{:S(2)}) collective-permute-start(bf16[1024,128]{1,0:T(8,128)(2,1)S(1)} %add.63.refs_4_), channel_id=1, source_target_pairs={{0,4},{4,8},{8,12},{12,0},{1,5},{5,9},{9,13},{13,1},{2,6},{6,10},{... | collective-permute-start | bytes 786440 | tf_op jit(solution)/shard_map/ppermute | solution.py:61
  52.8 17.7 %collective-permute-start.10 = (bf16[1024,128]{1,0:T(8,128)(2,1)S(1)}, bf16[1024,128]{1,0:T(8,128)(2,1)S(1)}, u32[]{:S(2)}, u32[]{:S(2)}) collective-permute-start(bf16[1024,128]{1,0:T(8,128)(2,1)S(1)} %get-tuple-element.31.refs_0_), channel_id=1, source_target_pairs={{0,4},{4,8},{8,12},{12,0},{1,5},{5,9},{9,13},{13,1},{2,6},{6,10},{... | collective-permute-start | bytes 786440 | tf_op jit(solution)/shard_map/ppermute | solution.py:61
  58.1 18.2 %collective-permute-start.12 = (bf16[1024,128]{1,0:T(8,128)(2,1)S(1)}, bf16[1024,128]{1,0:T(8,128)(2,1)S(1)}, u32[]{:S(2)}, u32[]{:S(2)}) collective-permute-start(bf16[1024,128]{1,0:T(8,128)(2,1)S(1)} %collective-permute-done.11.refs_3_), channel_id=1, source_target_pairs={{0,12},{4,0},{8,4},{12,8},{1,13},{5,1},{9,5},{13,9},{2,14},{6,2},{... | collective-permute-start | bytes 786440 | tf_op jit(solution)/shard_map/ppermute | solution.py:61
  66.4 9.9 %collective-permute-start.16 = (bf16[512,128]{1,0:T(8,128)(2,1)S(1)}, bf16[512,128]{1,0:T(8,128)(2,1)S(1)}, u32[]{:S(2)}, u32[]{:S(2)}) collective-permute-start(bf16[512,128]{1,0:T(8,128)(2,1)S(1)} %get-tuple-element.38), channel_id=1, source_target_pairs={{0,2},{2,0},{1,3},{3,1},{4,6},{6,4},{5,7},{7,5},{8,10},{10,8},{9,1... | collective-permute-start | bytes 393224 | tf_op jit(solution)/shard_map/ppermute | solution.py:65
  76.5 17.6 %collective-permute-start.17 = (bf16[512,512]{1,0:T(8,128)(2,1)S(1)}, bf16[512,512]{1,0:T(8,128)(2,1)S(1)}, u32[]{:S(2)}, u32[]{:S(2)}) collective-permute-start(bf16[512,512]{1,0:T(8,128)(2,1)S(1)} %cut_rows.1.refs_7_), channel_id=1, source_target_pairs={{0,2},{2,0},{1,3},{3,1},{4,6},{6,4},{5,7},{7,5},{8,10},{10,8},{9,1... | collective-permute-start | bytes 1572872 | tf_op jit(solution)/shard_map/ppermute | solution.py:65
  78.0 17.9 %collective-permute-start.23 = (bf16[256,1024]{1,0:T(8,128)(2,1)S(1)}, bf16[256,1024]{1,0:T(8,128)(2,1)S(1)}, u32[]{:S(2)}, u32[]{:S(2)}) collective-permute-start(bf16[256,1024]{1,0:T(8,128)(2,1)S(1)} %collective-permute-done.22.refs_6_.refs_3_.refs_2_), channel_id=1, source_target_pairs={{0,16},{16,0},{1,17},{17,1},{2,18},{18,2},{3,19},{19,3},{4,20},{20... | collective-permute-start | bytes 1572872 | tf_op jit(solution)/shard_map/ppermute | solution.py:65
  79.6 10.2 %collective-permute-start.20 = (bf16[512,256]{1,0:T(8,128)(2,1)S(1)}, bf16[512,256]{1,0:T(8,128)(2,1)S(1)}, u32[]{:S(2)}, u32[]{:S(2)}) collective-permute-start(bf16[512,256]{1,0:T(8,128)(2,1)S(1)} %join.1.refs_4_.refs_1_), channel_id=1, source_target_pairs={{0,12},{4,0},{8,4},{12,8},{1,13},{5,1},{9,5},{13,9},{2,14},{6,2},{... | collective-permute-start | bytes 786440 | tf_op jit(solution)/shard_map/ppermute | solution.py:61
  83.0 12.9 %collective-permute-start.19 = (bf16[512,256]{1,0:T(8,128)(2,1)S(1)}, bf16[512,256]{1,0:T(8,128)(2,1)S(1)}, u32[]{:S(2)}, u32[]{:S(2)}) collective-permute-start(bf16[512,256]{1,0:T(8,128)(2,1)S(1)} %join.1.refs_4_.refs_1_), channel_id=1, source_target_pairs={{0,4},{4,8},{8,12},{12,0},{1,5},{5,9},{9,13},{13,1},{2,6},{6,10},{... | collective-permute-start | bytes 786440 | tf_op jit(solution)/shard_map/ppermute | solution.py:61
  89.8 8.7 %collective-permute-start.21 = (bf16[512,256]{1,0:T(8,128)(2,1)S(1)}, bf16[512,256]{1,0:T(8,128)(2,1)S(1)}, u32[]{:S(2)}, u32[]{:S(2)}) collective-permute-start(bf16[512,256]{1,0:T(8,128)(2,1)S(1)} %collective-permute-done.20.refs_4_), channel_id=1, source_target_pairs={{0,12},{4,0},{8,4},{12,8},{1,13},{5,1},{9,5},{13,9},{2,14},{6,2},{... | collective-permute-start | bytes 786440 | tf_op jit(solution)/shard_map/ppermute | solution.py:61
  99.8 2.7 %collective-permute-start.24 = (bf16[512,1024]{1,0:T(8,128)(2,1)S(1)}, bf16[512,1024]{1,0:T(8,128)(2,1)S(1)}, u32[]{:S(2)}, u32[]{:S(2)}) collective-permute-start(bf16[512,1024]{1,0:T(8,128)(2,1)S(1)} %out_sum.1.refs_0_.refs_5_), channel_id=1, source_target_pairs={{0,1},{1,0},{2,3},{3,2},{4,5},{5,4},{6,7},{7,6},{8,9},{9,8},{10,11... | collective-permute-start | bytes 3145736 | tf_op jit(solution)/shard_map/ppermute | solution.py:65
  103.5 11.5 %collective-permute-start.27 = (bf16[512,256]{1,0:T(8,128)(2,1)S(1)}, bf16[512,256]{1,0:T(8,128)(2,1)S(1)}, u32[]{:S(2)}, u32[]{:S(2)}) collective-permute-start(bf16[512,256]{1,0:T(8,128)(2,1)S(1)} %get-tuple-element.45), channel_id=1, source_target_pairs={{0,4},{4,8},{8,12},{12,0},{1,5},{5,9},{9,13},{13,1},{2,6},{6,10},{... | collective-permute-start | bytes 786440 | tf_op jit(solution)/shard_map/ppermute | solution.py:61
  103.6 24.5 %collective-permute-start.25 = (bf16[256,1024]{1,0:T(8,128)(2,1)S(1)}, bf16[256,1024]{1,0:T(8,128)(2,1)S(1)}, u32[]{:S(2)}, u32[]{:S(2)}) collective-permute-start(bf16[256,1024]{1,0:T(8,128)(2,1)S(1)} %get-tuple-element.43), channel_id=1, source_target_pairs={{0,2},{2,0},{1,3},{3,1},{4,6},{6,4},{5,7},{7,5},{8,10},{10,8},{9,1... | collective-permute-start | bytes 1572872 | tf_op jit(solution)/shard_map/ppermute | solution.py:65
  105.7 13.7 %collective-permute-start.29 = (bf16[512,256]{1,0:T(8,128)(2,1)S(1)}, bf16[512,256]{1,0:T(8,128)(2,1)S(1)}, u32[]{:S(2)}, u32[]{:S(2)}) collective-permute-start(bf16[512,256]{1,0:T(8,128)(2,1)S(1)} %get-tuple-element.47), channel_id=1, source_target_pairs={{0,12},{4,0},{8,4},{12,8},{1,13},{5,1},{9,5},{13,9},{2,14},{6,2},{... | collective-permute-start | bytes 786440 | tf_op jit(solution)/shard_map/ppermute | solution.py:61
  115.1 12.8 %collective-permute-start.28 = (bf16[512,256]{1,0:T(8,128)(2,1)S(1)}, bf16[512,256]{1,0:T(8,128)(2,1)S(1)}, u32[]{:S(2)}, u32[]{:S(2)}) collective-permute-start(bf16[512,256]{1,0:T(8,128)(2,1)S(1)} %add.64.refs_3_), channel_id=1, source_target_pairs={{0,4},{4,8},{8,12},{12,0},{1,5},{5,9},{9,13},{13,1},{2,6},{6,10},{... | collective-permute-start | bytes 786440 | tf_op jit(solution)/shard_map/ppermute | solution.py:61
  128.0 5.0 %collective-permute-start.30 = (bf16[512,128]{1,0:T(8,128)(2,1)S(1)}, bf16[512,128]{1,0:T(8,128)(2,1)S(1)}, u32[]{:S(2)}, u32[]{:S(2)}) collective-permute-start(bf16[512,128]{1,0:T(8,128)(2,1)S(1)} %get-tuple-element.49), channel_id=1, source_target_pairs={{0,2},{2,0},{1,3},{3,1},{4,6},{6,4},{5,7},{7,5},{8,10},{10,8},{9,1... | collective-permute-start | bytes 393224 | tf_op jit(solution)/shard_map/ppermute | solution.py:65
  128.1 20.0 %collective-permute-start.26 = (bf16[256,1024]{1,0:T(8,128)(2,1)S(1)}, bf16[256,1024]{1,0:T(8,128)(2,1)S(1)}, u32[]{:S(2)}, u32[]{:S(2)}) collective-permute-start(bf16[256,1024]{1,0:T(8,128)(2,1)S(1)} %collective-permute-done.25.refs_5_), channel_id=1, source_target_pairs={{0,1},{1,0},{2,3},{3,2},{4,5},{5,4},{6,7},{7,6},{8,9},{9,8},{10,11... | collective-permute-start | bytes 1572872 | tf_op jit(solution)/shard_map/ppermute | solution.py:65
  135.1 12.6 %collective-permute-start.32 = (bf16[1024,128]{1,0:T(8,128)(2,1)S(1)}, bf16[1024,128]{1,0:T(8,128)(2,1)S(1)}, u32[]{:S(2)}, u32[]{:S(2)}) collective-permute-start(bf16[1024,128]{1,0:T(8,128)(2,1)S(1)} %key_grad.1.refs_7_.refs_1_), channel_id=1, source_target_pairs={{0,12},{4,0},{8,4},{12,8},{1,13},{5,1},{9,5},{13,9},{2,14},{6,2},{... | collective-permute-start | bytes 786440 | tf_op jit(solution)/shard_map/ppermute | solution.py:61
  136.9 15.6 %collective-permute-start.31 = (bf16[1024,128]{1,0:T(8,128)(2,1)S(1)}, bf16[1024,128]{1,0:T(8,128)(2,1)S(1)}, u32[]{:S(2)}, u32[]{:S(2)}) collective-permute-start(bf16[1024,128]{1,0:T(8,128)(2,1)S(1)} %key_grad.1.refs_7_.refs_1_), channel_id=1, source_target_pairs={{0,4},{4,8},{8,12},{12,0},{1,5},{5,9},{9,13},{13,1},{2,6},{6,10},{... | collective-permute-start | bytes 786440 | tf_op jit(solution)/shard_map/ppermute | solution.py:61
  147.7 6.4 %collective-permute-start.33 = (bf16[1024,128]{1,0:T(8,128)(2,1)S(1)}, bf16[1024,128]{1,0:T(8,128)(2,1)S(1)}, u32[]{:S(2)}, u32[]{:S(2)}) collective-permute-start(bf16[1024,128]{1,0:T(8,128)(2,1)S(1)} %collective-permute-done.32.refs_4_), channel_id=1, source_target_pairs={{0,12},{4,0},{8,4},{12,8},{1,13},{5,1},{9,5},{13,9},{2,14},{6,2},{... | collective-permute-start | bytes 786440 | tf_op jit(solution)/shard_map/ppermute | solution.py:61
  150.6 1.2 copy-start.1

commit v6 on v5

--- a/solution.py
+++ b/solution.py
@@ -19,7 +19,7 @@
     def __init__(self):
         self.last = None
 
-    def __call__(self, kernel, outs, ins, scratch=(), in_specs=None, first=()):
+    def __call__(self, kernel, outs, ins, scratch=(), in_specs=None, first=(), mib=18):
         specs = in_specs or [VMEM] * len(ins)
         out_specs = [HBM] * len(outs) if in_specs and HBM in in_specs and VMEM not in in_specs else [VMEM] * len(outs)
         count = len(ins)
@@ -36,7 +36,7 @@
             in_specs=specs,
             out_specs=out_specs,
             scratch_shapes=list(scratch),
-            compiler_params=pltpu.CompilerParams(vmem_limit_bytes=18 * 2**20),
+            compiler_params=pltpu.CompilerParams(vmem_limit_bytes=mib * 2**20),
             cost_estimate=pl.CostEstimate(flops=1, bytes_accessed=1, transcendentals=0),
             name=getattr(kernel, "func", kernel).__name__,
         )(*ins)
@@ -70,12 +70,19 @@
 
 
 def pack(*refs):
-    *pieces, weight, out, share, sem = refs
-    copy = pltpu.make_async_copy(weight.at[at(lax.axis_index("groups"), share.shape[0])], share, sem)
-    copy.start()
+    *pieces, weight, probe, out, share, upper, lower, sems = refs
+    rows = share.shape[0]
+    copies = [
+        pltpu.make_async_copy(weight.at[at(lax.axis_index("groups"), rows)], share, sems.at[0]),
+        pltpu.make_async_copy(probe.at[pl.ds(0, rows)], upper, sems.at[1]),
+        pltpu.make_async_copy(probe.at[pl.ds(rows, rows)], lower, sems.at[2]),
+    ]
+    for copy in copies:
+        copy.start()
     for j, piece in enumerate(pieces):
         out[j] = piece[...]
-    copy.wait()
+    for copy in copies:
+        copy.wait()
 
 
 def tangent_term(n, normed, packed, peer, probe, feats, *refs):
@@ -119,16 +126,14 @@
             all3[j][at(lax.rem(me - k + n, n), tok), :] = pieces[k - 1][j]
     heads = cols // DH
     v_flip = v_all[...].T
-    lane = lax.broadcasted_iota(jnp.int32, (tok, cols), 1) // DH
-
-    @pl.loop(0, n)
-    def _(c):
-        rows = at(c, tok)
+    step = probs.shape[2] // 2
+    lane = lax.broadcasted_iota(jnp.int32, (step, cols), 1) // DH
+    for c in range(2):
+        rows = slice(c * step, (c + 1) * step)
+        scores = [dot(k_all[...], jnp.where(lane == h, q_all[rows, :], 0), 1, 1) for h in range(heads)]
         parts = []
         for h in range(heads):
-            query = jnp.where(lane == h, q_all[rows, :], 0)
-            scores = dot(k_all[...], query, 1, 1)
-            exps = jnp.exp(scores - jnp.max(scores, axis=0, keepdims=True))
+            exps = jnp.exp(scores[h] - jnp.max(scores[h], axis=0, keepdims=True))
             prob = (exps * (1.0 / jnp.sum(exps, axis=0, keepdims=True))).astype(jnp.bfloat16)
             probs[h, :, rows] = prob
             parts.append(dot(v_flip, prob))
@@ -180,14 +185,16 @@
 
 
 def out_term(n, *refs):
-    pieces, (theirs, probe, other, total, lhs) = refs[:n], refs[n:]
+    pieces, (theirs, probe, upper, lower, total, lhs) = refs[:n], refs[n:]
     me, head = lax.axis_index("seq"), lax.axis_index("head")
     half = theirs.shape[0]
     cols = pieces[0].shape[1]
     for k in range(n):
         lhs[:, at(lax.rem(me - k + n, n), cols)] = pieces[k][at(head, half), :]
     total[...] = dot(lhs[...], probe[...])
-    total[...] += dot(theirs[...], other[...])
+    rows = upper.shape[0]
+    total[...] += dot(theirs[:, :rows], upper[...])
+    total[...] += dot(theirs[:, rows:], lower[...])
 
 
 def out_sum(n, *refs):
@@ -312,12 +319,14 @@
             pieces[n - k] = ahead(pieces[(n - k + 1) % n], n - 1)
         return pieces
 
-    def summed(terms):
+    def summed(terms, together=False):
         sums = [terms[0]]
-        for step, far in ((1, n // 2), (-1, (n - 1) // 2)):
-            total = ahead(terms[step * far], step)
+        ways = ((1, n // 2), (-1, (n - 1) // 2))
+        begun = [ahead(terms[step * far], step) for step, far in ways]
+        for (step, far), total in zip(ways, begun):
             for k in range(far - 1, 0, -1):
-                (total,) = call(add, [bf(*total.shape)], [total, terms[step * k]])
+                first = begun if together else ()
+                (total,) = call(add, [bf(*total.shape)], [total, terms[step * k]], first=first)
                 total = ahead(total, step)
             sums.append(total)
         return sums
@@ -333,30 +342,31 @@
         qkv.append(ahead(after(piece, got[0]), k))
     got = got[-1:] + got[:-1]
     other = [swap(x, "head") for x in got]
-    packed, share = call(
-        pack, [bf(2 * (n - 1), quarter, slab), bf(block // 2, slab)], [*got, *other, out_weight],
-        scratch=[dma(())], in_specs=[VMEM] * (2 * n - 2) + [ANY], first=qkv[:2])
+    packed, share, upper, lower = call(
+        pack, [bf(2 * (n - 1), quarter, slab)] + [bf(block // 2, slab)] * 3, [*got, *other, out_weight, out_probe],
+        scratch=[dma((3,))], in_specs=[VMEM] * (2 * n - 2) + [ANY] * 2, first=qkv[:2])
     feats, *terms = call(
         part(tangent_term, n), [bf(tokens, slab)] + [bf(tokens, cols)] * n,
         [normed, packed, swap(packed, "rep"), value_probe], scratch=[held(tokens, block), dma(())],
         in_specs=[ANY] + [VMEM] * 3)
-    other_probe = swap(after(out_probe, packed), "head")
+    upper = swap(upper, "head")
     weights = [swap(after(share, feats), "head")]
     probs, attended = call(
         part(attend, n), [bf(heads, tokens, tokens), bf(tokens, cols)], [*proj, *qkv],
-        scratch=[held(tokens, cols)] * 3)
+        scratch=[held(tokens, cols)] * 3, mib=32)
     att = gathered(attended)
-    tangent = summed(terms)
+    tangent = summed(terms, together=True)
     tan, tan_away = call(
         part(attend_tan, 3), [bf(half, cols)] * 2, [*tangent, probs],
-        scratch=[held(heads, tokens, tokens), held(tokens, cols), dma((heads,))], in_specs=[VMEM] * 3 + [ANY])
+        scratch=[held(heads, tokens, tokens), held(tokens, cols), dma((heads,))], in_specs=[VMEM] * 3 + [ANY], first=[upper])
     (tan,) = call(join, [bf(half, 2 * cols)], [tan, swap(tan_away, "head")], first=[att[1], att[-1]])
     weights.append(swap(weights[0], "groups"))
     tan = gathered(tan)
     (away,) = call(part(cut_rows, n), [bf(half, block)], att)
+    lower = swap(after(lower, tan[0]), "head")
     (base,) = call(
         part(out_term, n), [jax.ShapeDtypeStruct((half, slab), f32)],
-        [*att, swap(away, "head"), out_probe, other_probe], scratch=[held(half, block)])
+        [*att, swap(away, "head"), out_probe, upper, lower], scratch=[held(half, block)])
     (mine,) = call(
         part(out_sum, n), [bf(half, slab)], [base, *tan, out_weight, *weights], scratch=[held(2, half, block)])
     tangent_out, share, far = call(

time: 157 us -> 154 us (0.981)
  waiting for transfers between devices: 76.3 us -> 81.7 us
  starting transfers between devices: 50.3 us -> 46.1 us
  Pallas kernels: 24.1 us -> 20.2 us
    ppermute x21, waiting for transfers between devices: 57 us -> 64.6 us  [ahead(): return lax.ppermute(x, 'seq', [(i, (i + k) % n) for i in range(n)])]
    ppermute x21, starting transfers between devices: 38.2 us -> 32.1 us  [ahead(): return lax.ppermute(x, 'seq', [(i, (i + k) % n) for i in range(n)])]
    pallas_call x17, Pallas kernels: 24.1 us -> 20.2 us  [__call__(): pl.pallas_call(body, out_shape=outs, in_specs=specs, out_specs=out_specs,...]
    ppermute x13 -> x14, waiting for transfers between devices: 19.3 us -> 17.1 us  [swap(): return lax.ppermute(x, axis, [(0, 1), (1, 0)])]
    ppermute x13 -> x14, starting transfers between devices: 12.1 us -> 14 us  [swap(): return lax.ppermute(x, axis, [(0, 1), (1, 0)])]
  transfers between devices with their start and end apart: 34 -> 35, of which waited for: 18 -> 20; matrix products, arithmetic and copies ran while one was open for 1% -> 1% of each run, Pallas kernels for 12% -> 10%
where the time goes in v6:
time: 154 us; the launch traced here: 153 us
  waiting for transfers between devices  81.7 us (53%)
  starting transfers between devices  46.1 us (30%)
  Pallas kernels  20.2 us (13%)
  local copies, waits for them, and re-layouts  4.44 us (3%)
    ppermute x21, waiting for transfers between devices, ahead(): return lax.ppermute(x, 'seq', [(i, (i + k) % n) for i in range(n)])  64.6 us
    ppermute x21, starting transfers between devices, ahead(): return lax.ppermute(x, 'seq', [(i, (i + k) % n) for i in range(n)])  32.1 us
    pallas_call x17, Pallas kernels, __call__(): pl.pallas_call(body, out_shape=outs, in_specs=specs, out_specs=out_specs,...  20.2 us
    ppermute x14, waiting for transfers between devices, swap(): return lax.ppermute(x, axis, [(0, 1), (1, 0)])  17.1 us
    ppermute x14, starting transfers between devices, swap(): return lax.ppermute(x, axis, [(0, 1), (1, 0)])  14 us
  transfers between devices with their start and end apart: 35, of which 20 were waited for; matrix products, arithmetic and copies ran while one was open for 1% of the time, Pallas kernels for 10%

profile of v6, /device:TPU:0, one launch (start us, length us, event | category | flops | bytes accessed | tf_op | source)
XLA Modules:
  0.0 153.4 jit_solution(11411775142279243606)
XLA Ops:
  0.7 1.2 fusion
  1.9 3.1 %collective-permute-start.1 = (bf16[64,1024]{1,0:T(8,128)(2,1)S(1)}, bf16[64,1024]{1,0:T(8,128)(2,1)S(1)}, u32[]{:S(2)}, u32[]{:S(2)}) collective-permute-start(bf16[64,1024]{1,0:T(8,128)(2,1)S(1)} %get-tuple-element.55), channel_id=1, source_target_pairs={{0,4},{4,8},{8,12},{12,0},{1,5},{5,9},{9,13},{13,1},{2,6},{6,10},{... | collective-permute-start | bytes 393224 | tf_op jit(solution)/shard_map/ppermute | solution.py:61
  5.0 2.1 %collective-permute-start = (bf16[64,1024]{1,0:T(8,128)(2,1)S(1)}, bf16[64,1024]{1,0:T(8,128)(2,1)S(1)}, u32[]{:S(2)}, u32[]{:S(2)}) collective-permute-start(bf16[64,1024]{1,0:T(8,128)(2,1)S(1)} %get-tuple-element.56), channel_id=1, source_target_pairs={{0,12},{4,0},{8,4},{12,8},{1,13},{5,1},{9,5},{13,9},{2,14},{6,2},{... | collective-permute-start | bytes 393224 | tf_op jit(solution)/shard_map/ppermute | solution.py:61
  7.1 0.9 collective-permute-start.2
  8.0 0.9 dynamic-slice_bitcast_fusion.2
  8.9 1.0 dynamic-slice_bitcast_fusion
  10.1 1.3 collective-permute-done.1.refs_1_
  11.3 8.2 %collective-permute-start.7 = (bf16[3,256,128]{2,1,0:T(8,128)(2,1)S(1)}, bf16[3,256,128]{2,1,0:T(8,128)(2,1)S(1)}, u32[]{:S(2)}, u32[]{:S(2)}) collective-permute-start(bf16[3,256,128]{2,1,0:T(8,128)(2,1)S(1)} %pad_maximum_fusion.1), channel_id=1, source_target_pairs={{0,8},{4,12},{8,0},{12,4},{1,9},{5,13},{9,1},{13,5},{2,10},{6,14},... | collective-permute-start | bytes 589832 | tf_op jit(solution)/shard_map/ppermute | solution.py:61
  19.5 1.5 collective-permute-start.4
  21.0 0.5 collective-permute-start.3
  21.5 5.9 %collective-permute-done.2.refs_2_ = bf16[64,1024]{1,0:T(8,128)(2,1)S(1)} collective-permute-done((bf16[64,1024]{1,0:T(8,128)(2,1)S(1)}, bf16[64,1024]{1,0:T(8,128)(2,1)S(1)}, u32[]{:S(2)}, u32[]{:S(2)}) %collective-permute-start.2) | collective-permute-done | bytes 131104 | tf_op jit(solution)/shard_map/ppermute | solution.py:61
  27.4 1.5 collective-permute-start.5
  28.9 3.8 %collective-permute-done.5.refs_5_ = bf16[64,1024]{1,0:T(8,128)(2,1)S(1)} collective-permute-done((bf16[64,1024]{1,0:T(8,128)(2,1)S(1)}, bf16[64,1024]{1,0:T(8,128)(2,1)S(1)}, u32[]{:S(2)}, u32[]{:S(2)}) %collective-permute-start.5) | collective-permute-done | bytes 131104 | tf_op jit(solution)/shard_map/ppermute | solution.py:65
  32.8 0.2 pack.1
  33.2 2.1 %collective-permute-done.8.refs_2_ = bf16[6,64,1024]{2,1,0:T(8,128)(2,1)S(1)} collective-permute-done((bf16[6,64,1024]{2,1,0:T(8,128)(2,1)S(1)}, bf16[6,64,1024]{2,1,0:T(8,128)(2,1)S(1)}, u32[]{:S(2)}, u32[]{:S(2)}) %collective-permute-start.8) | collective-permute-done | bytes 786464 | tf_op jit(solution)/shard_map/ppermute | solution.py:65
  35.4 1.7 %tangent_term.1 = (bf16[1024,1024]{1,0:T(8,128)(2,1)S(1)}, bf16[1024,128]{1,0:T(8,128)(2,1)S(1)}, bf16[1024,128]{1,0:T(8,128)(2,1)S(1)}, bf16[1024,128]{1,0:T(8,128)(2,1)S(1)}, bf16[1024,128]{1,0:T(8,128)(2,1)S(1)}) custom-call(bf16[256,4096]{1,0:T(8,128)(2,1)S(1)} %copy-done.3, bf16[6,64,1024]{2,1,0:T(8,128)(2,1)S(1)} %get-tuple-element.30.refs_1_.refs_4_, ...), custom_call_target="tpu_custom_call" | custom-call | flops 1 | bytes 1 | tf_op jit(solution)/shard_map/tangent_term/pallas_call | solution.py:33
  37.1 3.8 %collective-permute-start.14 = (bf16[1024,128]{1,0:T(8,128)(2,1)S(1)}, bf16[1024,128]{1,0:T(8,128)(2,1)S(1)}, u32[]{:S(2)}, u32[]{:S(2)}) collective-permute-start(bf16[1024,128]{1,0:T(8,128)(2,1)S(1)} %get-tuple-element.37), channel_id=1, source_target_pairs={{0,12},{4,0},{8,4},{12,8},{1,13},{5,1},{9,5},{13,9},{2,14},{6,2},{... | collective-permute-start | bytes 786440 | tf_op jit(solution)/shard_map/ppermute | solution.py:61
  40.9 1.5 collective-permute-start.16
  42.4 3.7 %attend.1 = (bf16[2,1024,1024]{2,1,0:T(8,128)(2,1)S(1)}, bf16[1024,128]{1,0:T(8,128)(2,1)S(1)}) custom-call(bf16[256,512]{1,0:T(8,128)(2,1)S(1)} %copy-done.5, bf16[256,512]{1,0:T(8,128)(2,1)S(1)} %copy-done.7, bf16[256,512]{1,0:T(8,128)(2,1)S(1)} %copy-done.6, bf16[3,256,128]{2,1,0:T(8,128)(2,1)S(1)} %collective-permute-done.6.refs_8_.refs_3_, ...), custom_call_target="tpu_custom_call" | custom-call | flops 1 | bytes 1 | tf_op jit(solution)/shard_map/attend/pallas_call | solution.py:33
  46.2 0.5 collective-permute-start.11
  46.6 1.5 collective-permute-start.23
  48.1 4.0 %collective-permute-done.14.refs_3_.refs_2_ = bf16[1024,128]{1,0:T(8,128)(2,1)S(1)} collective-permute-done((bf16[1024,128]{1,0:T(8,128)(2,1)S(1)}, bf16[1024,128]{1,0:T(8,128)(2,1)S(1)}, u32[]{:S(2)}, u32[]{:S(2)}) %collective-permute-start.14) | collective-permute-done | bytes 262176 | tf_op jit(solution)/shard_map/ppermute | solution.py:61
  52.3 2.7 %collective-permute-start.10 = (bf16[1024,128]{1,0:T(8,128)(2,1)S(1)}, bf16[1024,128]{1,0:T(8,128)(2,1)S(1)}, u32[]{:S(2)}, u32[]{:S(2)}) collective-permute-start(bf16[1024,128]{1,0:T(8,128)(2,1)S(1)} %get-tuple-element.33.refs_0_), channel_id=1, source_target_pairs={{0,4},{4,8},{8,12},{12,0},{1,5},{5,9},{9,13},{13,1},{2,6},{6,10},{... | collective-permute-start | bytes 786440 | tf_op jit(solution)/shard_map/ppermute | solution.py:61
  54.9 2.4 %collective-permute-done.11.refs_3_ = bf16[1024,128]{1,0:T(8,128)(2,1)S(1)} collective-permute-done((bf16[1024,128]{1,0:T(8,128)(2,1)S(1)}, bf16[1024,128]{1,0:T(8,128)(2,1)S(1)}, u32[]{:S(2)}, u32[]{:S(2)}) %collective-permute-start.11) | collective-permute-done | bytes 262176 | tf_op jit(solution)/shard_map/ppermute | solution.py:61
  57.3 2.4 %collective-permute-start.12 = (bf16[1024,128]{1,0:T(8,128)(2,1)S(1)}, bf16[1024,128]{1,0:T(8,128)(2,1)S(1)}, u32[]{:S(2)}, u32[]{:S(2)}) collective-permute-start(bf16[1024,128]{1,0:T(8,128)(2,1)S(1)} %collective-permute-done.11.refs_3_), channel_id=1, source_target_pairs={{0,12},{4,0},{8,4},{12,8},{1,13},{5,1},{9,5},{13,9},{2,14},{6,2},{... | collective-permute-start | bytes 786440 | tf_op jit(solution)/shard_map/ppermute | solution.py:61
  59.7 5.4 %collective-permute-done.15.refs_1_ = bf16[1024,128]{1,0:T(8,128)(2,1)S(1)} collective-permute-done((bf16[1024,128]{1,0:T(8,128)(2,1)S(1)}, bf16[1024,128]{1,0:T(8,128)(2,1)S(1)}, u32[]{:S(2)}, u32[]{:S(2)}) %collective-permute-start.15) | collective-permute-done | bytes 262176 | tf_op jit(solution)/shard_map/ppermute | solution.py:61
  65.1 1.5 attend_tan.1
  66.6 1.6 %collective-permute-start.17 = (bf16[512,128]{1,0:T(8,128)(2,1)S(1)}, bf16[512,128]{1,0:T(8,128)(2,1)S(1)}, u32[]{:S(2)}, u32[]{:S(2)}) collective-permute-start(bf16[512,128]{1,0:T(8,128)(2,1)S(1)} %get-tuple-element.41), channel_id=1, source_target_pairs={{0,2},{2,0},{1,3},{3,1},{4,6},{6,4},{5,7},{7,5},{8,10},{10,8},{9,1... | collective-permute-start | bytes 393224 | tf_op jit(solution)/shard_map/ppermute | solution.py:65
  68.2 2.5 %collective-permute-done.10.refs_2_.refs_1_ = bf16[1024,128]{1,0:T(8,128)(2,1)S(1)} collective-permute-done((bf16[1024,128]{1,0:T(8,128)(2,1)S(1)}, bf16[1024,128]{1,0:T(8,128)(2,1)S(1)}, u32[]{:S(2)}, u32[]{:S(2)}) %collective-permute-start.10) | collective-permute-done | bytes 262176 | tf_op jit(solution)/shard_map/ppermute | solution.py:61
  70.6 1.0 collective-permute-done.17.refs_1_
  71.7 1.6 %collective-permute-start.19 = (bf16[256,1024]{1,0:T(8,128)(2,1)S(1)}, bf16[256,1024]{1,0:T(8,128)(2,1)S(1)}, u32[]{:S(2)}, u32[]{:S(2)}) collective-permute-start(bf16[256,1024]{1,0:T(8,128)(2,1)S(1)} %get-tuple-element.43), channel_id=1, source_target_pairs={{0,2},{2,0},{1,3},{3,1},{4,6},{6,4},{5,7},{7,5},{8,10},{10,8},{9,1... | collective-permute-start | bytes 1572872 | tf_op jit(solution)/shard_map/ppermute | solution.py:65
  73.3 2.2 %collective-permute-done.12.refs_2_ = bf16[1024,128]{1,0:T(8,128)(2,1)S(1)} collective-permute-done((bf16[1024,128]{1,0:T(8,128)(2,1)S(1)}, bf16[1024,128]{1,0:T(8,128)(2,1)S(1)}, u32[]{:S(2)}, u32[]{:S(2)}) %collective-permute-start.12) | collective-permute-done | bytes 262176 | tf_op jit(solution)/shard_map/ppermute | solution.py:61
  75.5 0.1 cut_rows.1.refs_8_
  75.6 1.6 %collective-permute-start.18 = (bf16[512,512]{1,0:T(8,128)(2,1)S(1)}, bf16[512,512]{1,0:T(8,128)(2,1)S(1)}, u32[]{:S(2)}, u32[]{:S(2)}) collective-permute-start(bf16[512,512]{1,0:T(8,128)(2,1)S(1)} %cut_rows.1.refs_8_), channel_id=1, source_target_pairs={{0,2},{2,0},{1,3},{3,1},{4,6},{6,4},{5,7},{7,5},{8,10},{10,8},{9,1... | collective-permute-start | bytes 1572872 | tf_op jit(solution)/shard_map/ppermute | solution.py:65
  77.2 1.5 collective-permute-start.24
  78.7 0.9 collective-permute-start.21
  79.6 1.1 collective-permute-start.20
  80.7 10.7 %collective-permute-done.21.refs_4_ = bf16[512,256]{1,0:T(8,128)(2,1)S(1)} collective-permute-done((bf16[512,256]{1,0:T(8,128)(2,1)S(1)}, bf16[512,256]{1,0:T(8,128)(2,1)S(1)}, u32[]{:S(2)}, u32[]{:S(2)}) %collective-permute-start.21) | collective-permute-done | bytes 262176 | tf_op jit(solution)/shard_map/ppermute | solution.py:61
  91.4 3.0 %collective-permute-done.18.refs_4_ = bf16[512,512]{1,0:T(8,128)(2,1)S(1)} collective-permute-done((bf16[512,512]{1,0:T(8,128)(2,1)S(1)}, bf16[512,512]{1,0:T(8,128)(2,1)S(1)}, u32[]{:S(2)}, u32[]{:S(2)}) %collective-permute-start.18) | collective-permute-done | bytes 524320 | tf_op jit(solution)/shard_map/ppermute | solution.py:65
  94.4 1.3 out_term.1.refs_0_.refs_8_
  95.7 2.0 %collective-permute-done.22.refs_3_ = bf16[512,256]{1,0:T(8,128)(2,1)S(1)} collective-permute-done((bf16[512,256]{1,0:T(8,128)(2,1)S(1)}, bf16[512,256]{1,0:T(8,128)(2,1)S(1)}, u32[]{:S(2)}, u32[]{:S(2)}) %collective-permute-start.22) | collective-permute-done | bytes 262176 | tf_op jit(solution)/shard_map/ppermute | solution.py:61
  97.8 1.3 out_sum.1.refs_0_.refs_5_
  99.1 0.1 collective-permute-start.25
  99.2 2.6 %collective-permute-done.25.refs_1_ = bf16[512,1024]{1,0:T(8,128)(2,1)S(1)} collective-permute-done((bf16[512,1024]{1,0:T(8,128)(2,1)S(1)}, bf16[512,1024]{1,0:T(8,128)(2,1)S(1)}, u32[]{:S(2)}, u32[]{:S(2)}) %collective-permute-start.25) | collective-permute-done | bytes 1048608 | tf_op jit(solution)/shard_map/ppermute | solution.py:65
  101.8 1.0 grad_far.1
  102.9 0.4 collective-permute-start.28
  103.3 0.5 collective-permute-start.26
  103.8 1.5 grad_term.1
  105.3 3.7 %collective-permute-start.30 = (bf16[512,256]{1,0:T(8,128)(2,1)S(1)}, bf16[512,256]{1,0:T(8,128)(2,1)S(1)}, u32[]{:S(2)}, u32[]{:S(2)}) collective-permute-start(bf16[512,256]{1,0:T(8,128)(2,1)S(1)} %get-tuple-element.51), channel_id=1, source_target_pairs={{0,12},{4,0},{8,4},{12,8},{1,13},{5,1},{9,5},{13,9},{2,14},{6,2},{... | collective-permute-start | bytes 786440 | tf_op jit(solution)/shard_map/ppermute | solution.py:61
  109.0 5.1 %collective-permute-done.28.refs_0_ = bf16[512,256]{1,0:T(8,128)(2,1)S(1)} collective-permute-done((bf16[512,256]{1,0:T(8,128)(2,1)S(1)}, bf16[512,256]{1,0:T(8,128)(2,1)S(1)}, u32[]{:S(2)}, u32[]{:S(2)}) %collective-permute-start.28) | collective-permute-done | bytes 262176 | tf_op jit(solution)/shard_map/ppermute | solution.py:61
  114.2 5.4 %collective-permute-done.30.refs_2_ = bf16[512,256]{1,0:T(8,128)(2,1)S(1)} collective-permute-done((bf16[512,256]{1,0:T(8,128)(2,1)S(1)}, bf16[512,256]{1,0:T(8,128)(2,1)S(1)}, u32[]{:S(2)}, u32[]{:S(2)}) %collective-permute-start.30) | collective-permute-done | bytes 262176 | tf_op jit(solution)/shard_map/ppermute | solution.py:61
  119.6 4.9 %collective-permute-done.29.refs_1_ = bf16[512,256]{1,0:T(8,128)(2,1)S(1)} collective-permute-done((bf16[512,256]{1,0:T(8,128)(2,1)S(1)}, bf16[512,256]{1,0:T(8,128)(2,1)S(1)}, u32[]{:S(2)}, u32[]{:S(2)}) %collective-permute-start.29) | collective-permute-done | bytes 262176 | tf_op jit(solution)/shard_map/ppermute | solution.py:61
  124.5 0.1 add_grad.1
  124.6 0.6 collective-permute-start.31
  125.2 4.4 %collective-permute-done.31.refs_1_ = bf16[512,128]{1,0:T(8,128)(2,1)S(1)} collective-permute-done((bf16[512,128]{1,0:T(8,128)(2,1)S(1)}, bf16[512,128]{1,0:T(8,128)(2,1)S(1)}, u32[]{:S(2)}, u32[]{:S(2)}) %collective-permute-start.31) | collective-permute-done | bytes 131104 | tf_op jit(solution)/shard_map/ppermute | solution.py:65
  129.6 2.1 %key_grad.1.refs_7_.refs_1_ = bf16[1024,128]{1,0:T(8,128)(2,1)S(1)} custom-call(bf16[512,128]{1,0:T(8,128)(2,1)S(1)} %get-tuple-element.52.refs_0_.refs_3_, bf16[512,128]{1,0:T(8,128)(2,1)S(1)} %collective-permute-done.31.refs_1_, bf16[2,1024,1024]{2,1,0:T(8,128)(2,1)S(1)} %get-tuple-element.38.refs_4_.refs_3_.refs_2_, ...), custom_call_target="tpu_custom_call" | custom-call | flops 1 | bytes 1 | tf_op jit(solution)/shard_map/key_grad/pallas_call | solution.py:33
  131.7 1.3 collective-permute-start.33
  133.0 0.7 collective-permute-start.32
  133.8 10.9 %collective-permute-done.33.refs_4_ = bf16[1024,128]{1,0:T(8,128)(2,1)S(1)} collective-permute-done((bf16[1024,128]{1,0:T(8,128)(2,1)S(1)}, bf16[1024,128]{1,0:T(8,128)(2,1)S(1)}, u32[]{:S(2)}, u32[]{:S(2)}) %collective-permute-start.33) | collective-permute-done | bytes 262176 | tf_op jit(solution)/shard_map/ppermute | solution.py:61
  144.7 2.5 %out_product.1.refs_1_ = bf16[512,1024]{1,0:T(8,128)(2,1)} custom-call(bf16[1024,128]{1,0:T(8,128)(2,1)S(1)} %get-tuple-element.33.refs_0_, bf16[1024,128]{1,0:T(8,128)(2,1)S(1)} %collective-permute-done.10.refs_2_.refs_1_, bf16[1024,128]{1,0:T(8,128)(2,1)S(1)} %collective-permute-done.12.refs_2_, bf16[1024,128]{1,0:T(8,128)(2,1)S(1)} %collective-permute-done.11.refs_3_, ...), custom_call_target="tpu_custom_call" | custom-call | flops 1 | bytes 1 | tf_op jit(solution)/shard_map/out_product/pallas_call | solution.py:33
  147.3 1.2 copy-done.1
  148.5 0.6 flip.1.refs_0_.refs_5_
  149.1 2.0 %collective-permute-done.34.refs_3_ = bf16[1024,128]{1,0:T(8,128)(2,1)S(1)} collective-permute-done((bf16[1024,128]{1,0:T(8,128)(2,1)S(1)}, bf16[1024,128]{1,0:T(8,128)(2,1)S(1)}, u32[]{:S(2)}, u32[]{:S(2)}) %collective-permute-start.34) | collective-permute-done | bytes 262176 | tf_op jit(solution)/shard_map/ppermute | solution.py:61
  151.1 2.3 %value_product.1 = bf16[1024,512]{1,0:T(8,128)(2,1)} custom-call(bf16[1024,1024]{1,0:T(8,128)(2,1)S(1)} %flip.1.refs_0_.refs_5_, bf16[1024,128]{1,0:T(8,128)(2,1)S(1)} %key_grad.1.refs_7_.refs_1_, bf16[1024,128]{1,0:T(8,128)(2,1)S(1)} %collective-permute-done.32.refs_2_, bf16[1024,128]{1,0:T(8,128)(2,1)S(1)} %collective-permute-done.34.refs_3_, ...), custom_call_target="tpu_custom_call" | custom-call | flops 1 | bytes 1 | tf_op jit(solution)/shard_map/value_product/pallas_call | solution.py:33
  (45 shorter events, 0.6 us)
Async XLA Ops:
  0.6 32.1 %copy-start = (bf16[512,1024]{1,0:T(8,128)(2,1)S(1)}, bf16[512,1024]{1,0:T(8,128)(2,1)}, u32[]{:S(2)}) copy-start(bf16[512,1024]{1,0:T(8,128)(2,1)} %refs_1_.3) | copy-start | bytes 3145732
  0.6 32.1 %copy-start.2 = (bf16[512,1024]{1,0:T(8,128)(2,1)S(1)}, bf16[512,1024]{1,0:T(8,128)(2,1)}, u32[]{:S(2)}) copy-start(bf16[512,1024]{1,0:T(8,128)(2,1)} %refs_5_.2) | copy-start | bytes 3145732
  1.9 9.4 %collective-permute-start.1 = (bf16[64,1024]{1,0:T(8,128)(2,1)S(1)}, bf16[64,1024]{1,0:T(8,128)(2,1)S(1)}, u32[]{:S(2)}, u32[]{:S(2)}) collective-permute-start(bf16[64,1024]{1,0:T(8,128)(2,1)S(1)} %get-tuple-element.55), channel_id=1, source_target_pairs={{0,4},{4,8},{8,12},{12,0},{1,5},{5,9},{9,13},{13,1},{2,6},{6,10},{... | collective-permute-start | bytes 393224 | tf_op jit(solution)/shard_map/ppermute | solution.py:61
  5.0 16.0 %collective-permute-start = (bf16[64,1024]{1,0:T(8,128)(2,1)S(1)}, bf16[64,1024]{1,0:T(8,128)(2,1)S(1)}, u32[]{:S(2)}, u32[]{:S(2)}) collective-permute-start(bf16[64,1024]{1,0:T(8,128)(2,1)S(1)} %get-tuple-element.56), channel_id=1, source_target_pairs={{0,12},{4,0},{8,4},{12,8},{1,13},{5,1},{9,5},{13,9},{2,14},{6,2},{... | collective-permute-start | bytes 393224 | tf_op jit(solution)/shard_map/ppermute | solution.py:61
  7.1 20.4 %collective-permute-start.2 = (bf16[64,1024]{1,0:T(8,128)(2,1)S(1)}, bf16[64,1024]{1,0:T(8,128)(2,1)S(1)}, u32[]{:S(2)}, u32[]{:S(2)}) collective-permute-start(bf16[64,1024]{1,0:T(8,128)(2,1)S(1)} %get-tuple-element.54), channel_id=1, source_target_pairs={{0,8},{4,12},{8,0},{12,4},{1,9},{5,13},{9,1},{13,5},{2,10},{6,14},... | collective-permute-start | bytes 393224 | tf_op jit(solution)/shard_map/ppermute | solution.py:61
  10.0 25.3 %copy-start.3 = (bf16[256,4096]{1,0:T(8,128)(2,1)S(1)}, bf16[256,4096]{1,0:T(8,128)(2,1)}, u32[]{:S(2)}) copy-start(bf16[256,4096]{1,0:T(8,128)(2,1)} %refs_0_.2) | copy-start | bytes 6291460
  10.0 25.3 %copy-start.4 = (bf16[1024,512]{1,0:T(8,128)(2,1)S(1)}, bf16[1024,512]{1,0:T(8,128)(2,1)}, u32[]{:S(2)}) copy-start(bf16[1024,512]{1,0:T(8,128)(2,1)} %refs_3_.1) | copy-start | bytes 3145732
  11.3 21.4 %collective-permute-start.7 = (bf16[3,256,128]{2,1,0:T(8,128)(2,1)S(1)}, bf16[3,256,128]{2,1,0:T(8,128)(2,1)S(1)}, u32[]{:S(2)}, u32[]{:S(2)}) collective-permute-start(bf16[3,256,128]{2,1,0:T(8,128)(2,1)S(1)} %pad_maximum_fusion.1), channel_id=1, source_target_pairs={{0,8},{4,12},{8,0},{12,4},{1,9},{5,13},{9,1},{13,5},{2,10},{6,14},... | collective-permute-start | bytes 589832 | tf_op jit(solution)/shard_map/ppermute | solution.py:61
  19.5 13.3 %collective-permute-start.6 = (bf16[3,256,128]{2,1,0:T(8,128)(2,1)S(1)}, bf16[3,256,128]{2,1,0:T(8,128)(2,1)S(1)}, u32[]{:S(2)}, u32[]{:S(2)}) collective-permute-start(bf16[3,256,128]{2,1,0:T(8,128)(2,1)S(1)} %pad_maximum_fusion), channel_id=1, source_target_pairs={{0,4},{4,8},{8,12},{12,0},{1,5},{5,9},{9,13},{13,1},{2,6},{6,10},{... | collective-permute-start | bytes 589832 | tf_op jit(solution)/shard_map/ppermute | solution.py:61
  19.5 9.5 %collective-permute-start.4 = (bf16[64,1024]{1,0:T(8,128)(2,1)S(1)}, bf16[64,1024]{1,0:T(8,128)(2,1)S(1)}, u32[]{:S(2)}, u32[]{:S(2)}) collective-permute-start(bf16[64,1024]{1,0:T(8,128)(2,1)S(1)} %collective-permute-done.1.refs_1_), channel_id=1, source_target_pairs={{0,2},{2,0},{1,3},{3,1},{4,6},{6,4},{5,7},{7,5},{8,10},{10,8},{9,1... | collective-permute-start | bytes 393224 | tf_op jit(solution)/shard_map/ppermute | solution.py:65
  21.0 8.0 %collective-permute-start.3 = (bf16[64,1024]{1,0:T(8,128)(2,1)S(1)}, bf16[64,1024]{1,0:T(8,128)(2,1)S(1)}, u32[]{:S(2)}, u32[]{:S(2)}) collective-permute-start(bf16[64,1024]{1,0:T(8,128)(2,1)S(1)} %collective-permute-done.refs_0_), channel_id=1, source_target_pairs={{0,2},{2,0},{1,3},{3,1},{4,6},{6,4},{5,7},{7,5},{8,10},{10,8},{9,1... | collective-permute-start | bytes 393224 | tf_op jit(solution)/shard_map/ppermute | solution.py:65
  27.4 5.3 %collective-permute-start.5 = (bf16[64,1024]{1,0:T(8,128)(2,1)S(1)}, bf16[64,1024]{1,0:T(8,128)(2,1)S(1)}, u32[]{:S(2)}, u32[]{:S(2)}) collective-permute-start(bf16[64,1024]{1,0:T(8,128)(2,1)S(1)} %collective-permute-done.2.refs_2_), channel_id=1, source_target_pairs={{0,2},{2,0},{1,3},{3,1},{4,6},{6,4},{5,7},{7,5},{8,10},{10,8},{9,1... | collective-permute-start | bytes 393224 | tf_op jit(solution)/shard_map/ppermute | solution.py:65
  33.0 2.4 %collective-permute-start.8 = (bf16[6,64,1024]{2,1,0:T(8,128)(2,1)S(1)}, bf16[6,64,1024]{2,1,0:T(8,128)(2,1)S(1)}, u32[]{:S(2)}, u32[]{:S(2)}) collective-permute-start(bf16[6,64,1024]{2,1,0:T(8,128)(2,1)S(1)} %get-tuple-element.30.refs_1_.refs_4_), channel_id=1, source_target_pairs={{0,1},{1,0},{2,3},{3,2},{4,5},{5,4},{6,7},{7,6},{8,9},{9,8},{10,11... | collective-permute-start | bytes 2359304 | tf_op jit(solution)/shard_map/ppermute | solution.py:65
  33.1 9.3 %copy-start.5 = (bf16[256,512]{1,0:T(8,128)(2,1)S(1)}, bf16[256,512]{1,0:T(8,128)(2,1)}, u32[]{:S(2)}) copy-start(bf16[256,512]{1,0:T(8,128)(2,1)} %refs_0_.3) | copy-start | bytes 786436
  33.1 9.3 %copy-start.6 = (bf16[256,512]{1,0:T(8,128)(2,1)S(1)}, bf16[256,512]{1,0:T(8,128)(2,1)}, u32[]{:S(2)}) copy-start(bf16[256,512]{1,0:T(8,128)(2,1)} %refs_2_.2) | copy-start | bytes 786436
  33.1 9.3 %copy-start.7 = (bf16[256,512]{1,0:T(8,128)(2,1)S(1)}, bf16[256,512]{1,0:T(8,128)(2,1)}, u32[]{:S(2)}) copy-start(bf16[256,512]{1,0:T(8,128)(2,1)} %refs_1_.2) | copy-start | bytes 786436
  33.1 9.3 %collective-permute-start.9 = (bf16[3,256,128]{2,1,0:T(8,128)(2,1)S(1)}, bf16[3,256,128]{2,1,0:T(8,128)(2,1)S(1)}, u32[]{:S(2)}, u32[]{:S(2)}) collective-permute-start(bf16[3,256,128]{2,1,0:T(8,128)(2,1)S(1)} %pad_maximum_fusion.2), channel_id=1, source_target_pairs={{0,12},{4,0},{8,4},{12,8},{1,13},{5,1},{9,5},{13,9},{2,14},{6,2},{... | collective-permute-start | bytes 589832 | tf_op jit(solution)/shard_map/ppermute | solution.py:61
  37.0 11.1 %collective-permute-start.13 = (bf16[1024,128]{1,0:T(8,128)(2,1)S(1)}, bf16[1024,128]{1,0:T(8,128)(2,1)S(1)}, u32[]{:S(2)}, u32[]{:S(2)}) collective-permute-start(bf16[1024,128]{1,0:T(8,128)(2,1)S(1)} %get-tuple-element.35), channel_id=1, source_target_pairs={{0,4},{4,8},{8,12},{12,0},{1,5},{5,9},{9,13},{13,1},{2,6},{6,10},{... | collective-permute-start | bytes 786440 | tf_op jit(solution)/shard_map/ppermute | solution.py:61
  37.1 15.0 %collective-permute-start.14 = (bf16[1024,128]{1,0:T(8,128)(2,1)S(1)}, bf16[1024,128]{1,0:T(8,128)(2,1)S(1)}, u32[]{:S(2)}, u32[]{:S(2)}) collective-permute-start(bf16[1024,128]{1,0:T(8,128)(2,1)S(1)} %get-tuple-element.37), channel_id=1, source_target_pairs={{0,12},{4,0},{8,4},{12,8},{1,13},{5,1},{9,5},{13,9},{2,14},{6,2},{... | collective-permute-start | bytes 786440 | tf_op jit(solution)/shard_map/ppermute | solution.py:61
  40.9 18.8 %collective-permute-start.16 = (bf16[256,1024]{1,0:T(8,128)(2,1)S(1)}, bf16[256,1024]{1,0:T(8,128)(2,1)S(1)}, u32[]{:S(2)}, u32[]{:S(2)}) collective-permute-start(bf16[256,1024]{1,0:T(8,128)(2,1)S(1)} %get-tuple-element.39), channel_id=1, source_target_pairs={{0,2},{2,0},{1,3},{3,1},{4,6},{6,4},{5,7},{7,5},{8,10},{10,8},{9,1... | collective-permute-start | bytes 1572872 | tf_op jit(solution)/shard_map/ppermute | solution.py:65
  46.2 11.2 %collective-permute-start.11 = (bf16[1024,128]{1,0:T(8,128)(2,1)S(1)}, bf16[1024,128]{1,0:T(8,128)(2,1)S(1)}, u32[]{:S(2)}, u32[]{:S(2)}) collective-permute-start(bf16[1024,128]{1,0:T(8,128)(2,1)S(1)} %get-tuple-element.33.refs_0_), channel_id=1, source_target_pairs={{0,12},{4,0},{8,4},{12,8},{1,13},{5,1},{9,5},{13,9},{2,14},{6,2},{... | collective-permute-start | bytes 786440 | tf_op jit(solution)/shard_map/ppermute | solution.py:61
  46.6 30.6 %collective-permute-start.23 = (bf16[256,1024]{1,0:T(8,128)(2,1)S(1)}, bf16[256,1024]{1,0:T(8,128)(2,1)S(1)}, u32[]{:S(2)}, u32[]{:S(2)}) collective-permute-start(bf16[256,1024]{1,0:T(8,128)(2,1)S(1)} %get-tuple-element.45), channel_id=1, source_target_pairs={{0,2},{2,0},{1,3},{3,1},{4,6},{6,4},{5,7},{7,5},{8,10},{10,8},{9,1... | collective-permute-start | bytes 1572872 | tf_op jit(solution)/shard_map/ppermute | solution.py:65
  52.2 12.9 %collective-permute-start.15 = (bf16[1024,128]{1,0:T(8,128)(2,1)S(1)}, bf16[1024,128]{1,0:T(8,128)(2,1)S(1)}, u32[]{:S(2)}, u32[]{:S(2)}) collective-permute-start(bf16[1024,128]{1,0:T(8,128)(2,1)S(1)} %add.63.refs_5_), channel_id=1, source_target_pairs={{0,4},{4,8},{8,12},{12,0},{1,5},{5,9},{9,13},{13,1},{2,6},{6,10},{... | collective-permute-start | bytes 786440 | tf_op jit(solution)/shard_map/ppermute | solution.py:61
  52.3 18.4 %collective-permute-start.10 = (bf16[1024,128]{1,0:T(8,128)(2,1)S(1)}, bf16[1024,128]{1,0:T(8,128)(2,1)S(1)}, u32[]{:S(2)}, u32[]{:S(2)}) collective-permute-start(bf16[1024,128]{1,0:T(8,128)(2,1)S(1)} %get-tuple-element.33.refs_0_), channel_id=1, source_target_pairs={{0,4},{4,8},{8,12},{12,0},{1,5},{5,9},{9,13},{13,1},{2,6},{6,10},{... | collective-permute-start | bytes 786440 | tf_op jit(solution)/shard_map/ppermute | solution.py:61
  57.3 18.1 %collective-permute-start.12 = (bf16[1024,128]{1,0:T(8,128)(2,1)S(1)}, bf16[1024,128]{1,0:T(8,128)(2,1)S(1)}, u32[]{:S(2)}, u32[]{:S(2)}) collective-permute-start(bf16[1024,128]{1,0:T(8,128)(2,1)S(1)} %collective-permute-done.11.refs_3_), channel_id=1, source_target_pairs={{0,12},{4,0},{8,4},{12,8},{1,13},{5,1},{9,5},{13,9},{2,14},{6,2},{... | collective-permute-start | bytes 786440 | tf_op jit(solution)/shard_map/ppermute | solution.py:61
  66.6 5.0 %collective-permute-start.17 = (bf16[512,128]{1,0:T(8,128)(2,1)S(1)}, bf16[512,128]{1,0:T(8,128)(2,1)S(1)}, u32[]{:S(2)}, u32[]{:S(2)}) collective-permute-start(bf16[512,128]{1,0:T(8,128)(2,1)S(1)} %get-tuple-element.41), channel_id=1, source_target_pairs={{0,2},{2,0},{1,3},{3,1},{4,6},{6,4},{5,7},{7,5},{8,10},{10,8},{9,1... | collective-permute-start | bytes 393224 | tf_op jit(solution)/shard_map/ppermute | solution.py:65
  71.7 19.7 %collective-permute-start.19 = (bf16[256,1024]{1,0:T(8,128)(2,1)S(1)}, bf16[256,1024]{1,0:T(8,128)(2,1)S(1)}, u32[]{:S(2)}, u32[]{:S(2)}) collective-permute-start(bf16[256,1024]{1,0:T(8,128)(2,1)S(1)} %get-tuple-element.43), channel_id=1, source_target_pairs={{0,2},{2,0},{1,3},{3,1},{4,6},{6,4},{5,7},{7,5},{8,10},{10,8},{9,1... | collective-permute-start | bytes 1572872 | tf_op jit(solution)/shard_map/ppermute | solution.py:65
  75.6 18.8 %collective-permute-start.18 = (bf16[512,512]{1,0:T(8,128)(2,1)S(1)}, bf16[512,512]{1,0:T(8,128)(2,1)S(1)}, u32[]{:S(2)}, u32[]{:S(2)}) collective-permute-start(bf16[512,512]{1,0:T(8,128)(2,1)S(1)} %cut_rows.1.refs_8_), channel_id=1, source_target_pairs={{0,2},{2,0},{1,3},{3,1},{4,6},{6,4},{5,7},{7,5},{8,10},{10,8},{9,1... | collective-permute-start | bytes 1572872 | tf_op jit(solution)/shard_map/ppermute | solution.py:65
  77.2 18.5 %collective-permute-start.24 = (bf16[256,1024]{1,0:T(8,128)(2,1)S(1)}, bf16[256,1024]{1,0:T(8,128)(2,1)S(1)}, u32[]{:S(2)}, u32[]{:S(2)}) collective-permute-start(bf16[256,1024]{1,0:T(8,128)(2,1)S(1)} %collective-permute-done.23.refs_6_.refs_3_.refs_2_), channel_id=1, source_target_pairs={{0,16},{16,0},{1,17},{17,1},{2,18},{18,2},{3,19},{19,3},{4,20},{20... | collective-permute-start | bytes 1572872 | tf_op jit(solution)/shard_map/ppermute | solution.py:65
  78.7 12.7 %collective-permute-start.21 = (bf16[512,256]{1,0:T(8,128)(2,1)S(1)}, bf16[512,256]{1,0:T(8,128)(2,1)S(1)}, u32[]{:S(2)}, u32[]{:S(2)}) collective-permute-start(bf16[512,256]{1,0:T(8,128)(2,1)S(1)} %join.1.refs_4_.refs_1_), channel_id=1, source_target_pairs={{0,12},{4,0},{8,4},{12,8},{1,13},{5,1},{9,5},{13,9},{2,14},{6,2},{... | collective-permute-start | bytes 786440 | tf_op jit(solution)/shard_map/ppermute | solution.py:61
  79.6 16.1 %collective-permute-start.20 = (bf16[512,256]{1,0:T(8,128)(2,1)S(1)}, bf16[512,256]{1,0:T(8,128)(2,1)S(1)}, u32[]{:S(2)}, u32[]{:S(2)}) collective-permute-start(bf16[512,256]{1,0:T(8,128)(2,1)S(1)} %join.1.refs_4_.refs_1_), channel_id=1, source_target_pairs={{0,4},{4,8},{8,12},{12,0},{1,5},{5,9},{9,13},{13,1},{2,6},{6,10},{... | collective-permute-start | bytes 786440 | tf_op jit(solution)/shard_map/ppermute | solution.py:61
  91.4 6.4 %collective-permute-start.22 = (bf16[512,256]{1,0:T(8,128)(2,1)S(1)}, bf16[512,256]{1,0:T(8,128)(2,1)S(1)}, u32[]{:S(2)}, u32[]{:S(2)}) collective-permute-start(bf16[512,256]{1,0:T(8,128)(2,1)S(1)} %collective-permute-done.21.refs_4_), channel_id=1, source_target_pairs={{0,12},{4,0},{8,4},{12,8},{1,13},{5,1},{9,5},{13,9},{2,14},{6,2},{... | collective-permute-start | bytes 786440 | tf_op jit(solution)/shard_map/ppermute | solution.py:61
  99.1 2.7 %collective-permute-start.25 = (bf16[512,1024]{1,0:T(8,128)(2,1)S(1)}, bf16[512,1024]{1,0:T(8,128)(2,1)S(1)}, u32[]{:S(2)}, u32[]{:S(2)}) collective-permute-start(bf16[512,1024]{1,0:T(8,128)(2,1)S(1)} %out_sum.1.refs_0_.refs_5_), channel_id=1, source_target_pairs={{0,1},{1,0},{2,3},{3,2},{4,5},{5,4},{6,7},{7,6},{8,9},{9,8},{10,11... | collective-permute-start | bytes 3145736 | tf_op jit(solution)/shard_map/ppermute | solution.py:65
  102.9 11.2 %collective-permute-start.28 = (bf16[512,256]{1,0:T(8,128)(2,1)S(1)}, bf16[512,256]{1,0:T(8,128)(2,1)S(1)}, u32[]{:S(2)}, u32[]{:S(2)}) collective-permute-start(bf16[512,256]{1,0:T(8,128)(2,1)S(1)} %get-tuple-element.49), channel_id=1, source_target_pairs={{0,4},{4,8},{8,12},{12,0},{1,5},{5,9},{9,13},{13,1},{2,6},{6,10},{... | collective-permute-start | bytes 786440 | tf_op jit(solution)/shard_map/ppermute | solution.py:61
  103.3 21.9 %collective-permute-start.26 = (bf16[256,1024]{1,0:T(8,128)(2,1)S(1)}, bf16[256,1024]{1,0:T(8,128)(2,1)S(1)}, u32[]{:S(2)}, u32[]{:S(2)}) collective-permute-start(bf16[256,1024]{1,0:T(8,128)(2,1)S(1)} %get-tuple-element.47), channel_id=1, source_target_pairs={{0,2},{2,0},{1,3},{3,1},{4,6},{6,4},{5,7},{7,5},{8,10},{10,8},{9,1... | collective-permute-start | bytes 1572872 | tf_op jit(solution)/shard_map/ppermute | solution.py:65
  105.3 14.3 %collective-permute-start.30 = (bf16[512,256]{1,0:T(8,128)(2,1)S(1)}, bf16[512,256]{1,0:T(8,128)(2,1)S(1)}, u32[]{:S(2)}, u32[]{:S(2)}) collective-permute-start(bf16[512,256]{1,0:T(8,128)(2,1)S(1)} %get-tuple-element.51), channel_id=1, source_target_pairs={{0,12},{4,0},{8,4},{12,8},{1,13},{5,1},{9,5},{13,9},{2,14},{6,2},{... | collective-permute-start | bytes 786440 | tf_op jit(solution)/shard_map/ppermute | solution.py:61
  114.1 10.4 %collective-permute-start.29 = (bf16[512,256]{1,0:T(8,128)(2,1)S(1)}, bf16[512,256]{1,0:T(8,128)(2,1)S(1)}, u32[]{:S(2)}, u32[]{:S(2)}) collective-permute-start(bf16[512,256]{1,0:T(8,128)(2,1)S(1)} %add.64.refs_3_), channel_id=1, source_target_pairs={{0,4},{4,8},{8,12},{12,0},{1,5},{5,9},{9,13},{13,1},{2,6},{6,10},{... | collective-permute-start | bytes 786440 | tf_op jit(solution)/shard_map/ppermute | solution.py:61
  124.6 5.0 %collective-permute-start.31 = (bf16[512,128]{1,0:T(8,128)(2,1)S(1)}, bf16[512,128]{1,0:T(8,128)(2,1)S(1)}, u32[]{:S(2)}, u32[]{:S(2)}) collective-permute-start(bf16[512,128]{1,0:T(8,128)(2,1)S(1)} %get-tuple-element.53), channel_id=1, source_target_pairs={{0,2},{2,0},{1,3},{3,1},{4,6},{6,4},{5,7},{7,5},{8,10},{10,8},{9,1... | collective-permute-start | bytes 393224 | tf_op jit(solution)/shard_map/ppermute | solution.py:65
  125.2 19.5 %collective-permute-start.27 = (bf16[256,1024]{1,0:T(8,128)(2,1)S(1)}, bf16[256,1024]{1,0:T(8,128)(2,1)S(1)}, u32[]{:S(2)}, u32[]{:S(2)}) collective-permute-start(bf16[256,1024]{1,0:T(8,128)(2,1)S(1)} %collective-permute-done.26.refs_5_), channel_id=1, source_target_pairs={{0,1},{1,0},{2,3},{3,2},{4,5},{5,4},{6,7},{7,6},{8,9},{9,8},{10,11... | collective-permute-start | bytes 1572872 | tf_op jit(solution)/shard_map/ppermute | solution.py:65
  131.7 13.0 %collective-permute-start.33 = (bf16[1024,128]{1,0:T(8,128)(2,1)S(1)}, bf16[1024,128]{1,0:T(8,128)(2,1)S(1)}, u32[]{:S(2)}, u32[]{:S(2)}) collective-permute-start(bf16[1024,128]{1,0:T(8,128)(2,1)S(1)} %key_grad.1.refs_7_.refs_1_), channel_id=1, source_target_pairs={{0,12},{4,0},{8,4},{12,8},{1,13},{5,1},{9,5},{13,9},{2,14},{6,2},{... | collective-permute-start | bytes 786440 | tf_op jit(solution)/shard_map/ppermute | solution.py:61
  133.0 16.1 %collective-permute-start.32 = (bf16[1024,128]{1,0:T(8,128)(2,1)S(1)}, bf16[1024,128]{1,0:T(8,128)(2,1)S(1)}, u32[]{:S(2)}, u32[]{:S(2)}) collective-permute-start(bf16[1024,128]{1,0:T(8,128)(2,1)S(1)} %key_grad.1.refs_7_.refs_1_), channel_id=1, source_target_pairs={{0,4},{4,8},{8,12},{12,0},{1,5},{5,9},{9,13},{13,1},{2,6},{6,10},{... | collective-permute-start | bytes 786440 | tf_op jit(solution)/shard_map/ppermute | solution.py:61
  144.7 6.4 %collective-permute-start.34 = (bf16[1024,128]{1,0:T(8,128)(2,1)S(1)}, bf16[1024,128]{1,0:T(8,128)(2,1)S(1)}, u32[]{:S(2)}, u32[]{:S(2)}) collective-permute-start(bf16[1024,128]{1,0:T(8,128)(2,1)S(1)} %collective-permute-done.33.refs_4_), channel_id=1, source_target_pairs={{0,12},{4,0},{8,4},{12,8},{1,13},{5,1},{9,5},{13,9},{2,14},{6,2},{... | collective-permute-start | bytes 786440 | tf_op jit(solution)/shard_map/ppermute | solution.py:61
  147.3 1.2 copy-start.1

commit v7 on v6

--- a/solution.py
+++ b/solution.py
@@ -254,33 +254,47 @@
     away[...] = total[:, cols:].astype(jnp.bfloat16)
 
 
-def key_grad(mine, theirs, probs, out, grad, held, sems):
+def key_grad(part, *refs):
+    if part:
+        base, *refs = refs
+    piece, probs, out, held, sems = refs
     heads, tokens, _ = probs.shape
-    half, cols = mine.shape
+    half, cols = piece.shape
     parts = held.shape[0]
     rows = tokens // parts
-    copies = [pltpu.make_async_copy(probs.at[:, pl.ds(c * rows, rows)], held.at[c], sems.at[c]) for c in range(parts)]
+    head = lax.axis_index("head")
+    queries = at(1 - head if part else head, half)
+    copies = [
+        pltpu.make_async_copy(probs.at[:, pl.ds(c * rows, rows), queries], held.at[c], sems.at[c])
+        for c in range(parts)]
     for copy in copies:
         copy.start()
-    head = lax.axis_index("head")
-    grad[at(head, half), :] = mine[...]
-    grad[at(1 - head, half), :] = theirs[...]
     lane = lax.broadcasted_iota(jnp.int32, (rows, cols), 1) // DH
     for c in range(parts):
         copies[c].wait()
-        value = dot(held[c, 0], grad[...])
+        value = dot(held[c, 0], piece[...])
         for h in range(1, heads):
-            value = jnp.where(lane == h, dot(held[c, h], grad[...]), value)
-        out[pl.ds(c * rows, rows), :] = value.astype(jnp.bfloat16)
+            value = jnp.where(lane == h, dot(held[c, h], piece[...]), value)
+        if part:
+            value = value + base[c * rows : (c + 1) * rows, :]
+        out[c * rows : (c + 1) * rows, :] = value.astype(out.dtype)
+
+
+def value_part(*refs):
+    count = len(refs) // 2
+    flipped, blocks, outs = refs[0], refs[1 : count + 1], refs[count + 1 :]
+    for block, out in zip(blocks, outs):
+        out[...] = dot(flipped[...], block[...]).astype(jnp.bfloat16)
 
 
 def value_product(n, *refs):
-    flipped, blocks, out, rhs = refs[0], refs[1 : n + 1], refs[n + 1], refs[n + 2]
+    flipped, block, parts, out = refs[0], refs[1], refs[2 : n + 1], refs[n + 1]
     me = lax.axis_index("seq")
-    cols = blocks[0].shape[1]
-    for k in range(n):
-        rhs[:, at(lax.rem(me - k + n, n), cols)] = blocks[k][...]
-    out[...] = dot(flipped[...], rhs[...]).astype(jnp.bfloat16)
+    cols = block.shape[1]
+    for k, part in zip((k for k in range(n) if k != n // 2), parts):
+        out[:, at(lax.rem(me - k + n, n), cols)] = part[...]
+    where = at(lax.rem(me - n // 2 + n, n), cols)
+    out[:, where] = dot(flipped[...], block[...]).astype(jnp.bfloat16)
 
 
 def out_product(n, *refs):
@@ -377,17 +391,21 @@
         scratch=[held(2, half, block)])
     grads = [*grads[: n // 2], far, *grads[n // 2 :]]
     home, away = call(part(add_grad, 3), [bf(half, cols)] * 2, summed(grads))
-    (value_grad,) = call(
-        key_grad, [bf(tokens, cols)], [home, swap(away, "head"), probs],
-        scratch=[held(tokens, cols), held(4, heads, tokens // 4, tokens), dma((4,))], in_specs=[VMEM] * 2 + [ANY])
+    value_grad = None
+    for j, piece in enumerate((home, swap(away, "head"))):
+        (value_grad,) = call(
+            part(key_grad, j), [jax.ShapeDtypeStruct((tokens, cols), jnp.bfloat16 if j else f32)],
+            [value_grad, piece, probs] if j else [piece, probs],
+            scratch=[held(4, heads, tokens // 4, half), dma((4,))], in_specs=[VMEM] * (j + 1) + [ANY])
     value_grad = gathered(value_grad)
     share = swap(share, "head")
     (out_curv,) = call(
         part(out_product, n), [bf(block, slab)], [*att, tangent_out, share, swap(share, "rep")],
         scratch=[held(tokens, slab)])
     (flipped,) = call(flip, [bf(slab, tokens)], [feats])
-    (value_curv,) = call(
-        part(value_product, n), [bf(slab, block)], [flipped, *value_grad], scratch=[held(tokens, block)])
+    far = value_grad.pop(n // 2)
+    parts = call(value_part, [bf(slab, cols)] * (n - 1), [flipped, *value_grad])
+    (value_curv,) = call(part(value_product, n), [bf(slab, block)], [flipped, far, *parts])
     return value_curv, out_curv
 
 

time: 154 us -> 152 us (0.987)
  waiting for transfers between devices: 81.7 us -> 77.1 us
  Pallas kernels: 20.2 us -> 22.2 us
    ppermute x21, waiting for transfers between devices: 64.6 us -> 61.5 us  [ahead(): return lax.ppermute(x, 'seq', [(i, (i + k) % n) for i in range(n)])]
    pallas_call x17 -> x19, Pallas kernels: 20.2 us -> 22.2 us  [__call__(): pl.pallas_call(body, out_shape=outs, in_specs=specs, out_specs=out_specs,...]
  transfers between devices with their start and end apart: 35 -> 35, of which waited for: 20 -> 19; matrix products, arithmetic and copies ran while one was open for 1% -> 1% of each run, Pallas kernels for 10% -> 12%
where the time goes in v7:
time: 152 us
  waiting for transfers between devices  77.1 us (51%)
  starting transfers between devices  46.7 us (31%)
  Pallas kernels  22.2 us (15%)
  local copies, waits for them, and re-layouts  4.44 us (3%)
    ppermute x21, waiting for transfers between devices, ahead(): return lax.ppermute(x, 'seq', [(i, (i + k) % n) for i in range(n)])  61.5 us
    ppermute x21, starting transfers between devices, ahead(): return lax.ppermute(x, 'seq', [(i, (i + k) % n) for i in range(n)])  32.8 us
    pallas_call x19, Pallas kernels, __call__(): pl.pallas_call(body, out_shape=outs, in_specs=specs, out_specs=out_specs,...  22.2 us
    ppermute x14, waiting for transfers between devices, swap(): return lax.ppermute(x, axis, [(0, 1), (1, 0)])  15.6 us
    ppermute x14, starting transfers between devices, swap(): return lax.ppermute(x, axis, [(0, 1), (1, 0)])  14 us
  transfers between devices with their start and end apart: 35, of which 19 were waited for; matrix products, arithmetic and copies ran while one was open for 1% of the time, Pallas kernels for 12%

profile of v7, /device:TPU:0, one launch (start us, length us, event | category | flops | bytes accessed | tf_op | source)
XLA Modules:
  0.0 151.5 jit_solution(1599971486831889884)
XLA Ops:
  0.7 1.2 fusion
  1.9 3.1 %collective-permute-start.1 = (bf16[64,1024]{1,0:T(8,128)(2,1)S(1)}, bf16[64,1024]{1,0:T(8,128)(2,1)S(1)}, u32[]{:S(2)}, u32[]{:S(2)}) collective-permute-start(bf16[64,1024]{1,0:T(8,128)(2,1)S(1)} %get-tuple-element.61), channel_id=1, source_target_pairs={{0,4},{4,8},{8,12},{12,0},{1,5},{5,9},{9,13},{13,1},{2,6},{6,10},{... | collective-permute-start | bytes 393224 | tf_op jit(solution)/shard_map/ppermute | solution.py:61
  5.0 2.1 %collective-permute-start = (bf16[64,1024]{1,0:T(8,128)(2,1)S(1)}, bf16[64,1024]{1,0:T(8,128)(2,1)S(1)}, u32[]{:S(2)}, u32[]{:S(2)}) collective-permute-start(bf16[64,1024]{1,0:T(8,128)(2,1)S(1)} %get-tuple-element.62), channel_id=1, source_target_pairs={{0,12},{4,0},{8,4},{12,8},{1,13},{5,1},{9,5},{13,9},{2,14},{6,2},{... | collective-permute-start | bytes 393224 | tf_op jit(solution)/shard_map/ppermute | solution.py:61
  7.1 0.9 collective-permute-start.2
  8.0 0.9 dynamic-slice_bitcast_fusion.2
  8.9 1.0 dynamic-slice_bitcast_fusion
  10.1 1.3 collective-permute-done.1.refs_1_
  11.3 8.2 %collective-permute-start.7 = (bf16[3,256,128]{2,1,0:T(8,128)(2,1)S(1)}, bf16[3,256,128]{2,1,0:T(8,128)(2,1)S(1)}, u32[]{:S(2)}, u32[]{:S(2)}) collective-permute-start(bf16[3,256,128]{2,1,0:T(8,128)(2,1)S(1)} %pad_maximum_fusion.1), channel_id=1, source_target_pairs={{0,8},{4,12},{8,0},{12,4},{1,9},{5,13},{9,1},{13,5},{2,10},{6,14},... | collective-permute-start | bytes 589832 | tf_op jit(solution)/shard_map/ppermute | solution.py:61
  19.5 1.5 collective-permute-start.4
  21.0 0.5 collective-permute-start.3
  21.5 5.9 %collective-permute-done.2.refs_2_ = bf16[64,1024]{1,0:T(8,128)(2,1)S(1)} collective-permute-done((bf16[64,1024]{1,0:T(8,128)(2,1)S(1)}, bf16[64,1024]{1,0:T(8,128)(2,1)S(1)}, u32[]{:S(2)}, u32[]{:S(2)}) %collective-permute-start.2) | collective-permute-done | bytes 131104 | tf_op jit(solution)/shard_map/ppermute | solution.py:61
  27.4 1.5 collective-permute-start.5
  28.9 3.8 %collective-permute-done.5.refs_5_ = bf16[64,1024]{1,0:T(8,128)(2,1)S(1)} collective-permute-done((bf16[64,1024]{1,0:T(8,128)(2,1)S(1)}, bf16[64,1024]{1,0:T(8,128)(2,1)S(1)}, u32[]{:S(2)}, u32[]{:S(2)}) %collective-permute-start.5) | collective-permute-done | bytes 131104 | tf_op jit(solution)/shard_map/ppermute | solution.py:65
  32.8 0.2 pack.1
  33.2 2.1 %collective-permute-done.8.refs_2_ = bf16[6,64,1024]{2,1,0:T(8,128)(2,1)S(1)} collective-permute-done((bf16[6,64,1024]{2,1,0:T(8,128)(2,1)S(1)}, bf16[6,64,1024]{2,1,0:T(8,128)(2,1)S(1)}, u32[]{:S(2)}, u32[]{:S(2)}) %collective-permute-start.8) | collective-permute-done | bytes 786464 | tf_op jit(solution)/shard_map/ppermute | solution.py:65
  35.4 1.7 %tangent_term.1 = (bf16[1024,1024]{1,0:T(8,128)(2,1)S(1)}, bf16[1024,128]{1,0:T(8,128)(2,1)S(1)}, bf16[1024,128]{1,0:T(8,128)(2,1)S(1)}, bf16[1024,128]{1,0:T(8,128)(2,1)S(1)}, bf16[1024,128]{1,0:T(8,128)(2,1)S(1)}) custom-call(bf16[256,4096]{1,0:T(8,128)(2,1)S(1)} %copy-done.3, bf16[6,64,1024]{2,1,0:T(8,128)(2,1)S(1)} %get-tuple-element.33.refs_1_.refs_4_, ...), custom_call_target="tpu_custom_call" | custom-call | flops 1 | bytes 1 | tf_op jit(solution)/shard_map/tangent_term/pallas_call | solution.py:33
  37.1 3.8 %collective-permute-start.14 = (bf16[1024,128]{1,0:T(8,128)(2,1)S(1)}, bf16[1024,128]{1,0:T(8,128)(2,1)S(1)}, u32[]{:S(2)}, u32[]{:S(2)}) collective-permute-start(bf16[1024,128]{1,0:T(8,128)(2,1)S(1)} %get-tuple-element.40), channel_id=1, source_target_pairs={{0,12},{4,0},{8,4},{12,8},{1,13},{5,1},{9,5},{13,9},{2,14},{6,2},{... | collective-permute-start | bytes 786440 | tf_op jit(solution)/shard_map/ppermute | solution.py:61
  40.9 1.5 collective-permute-start.16
  42.4 3.7 %attend.1 = (bf16[2,1024,1024]{2,1,0:T(8,128)(2,1)S(1)}, bf16[1024,128]{1,0:T(8,128)(2,1)S(1)}) custom-call(bf16[256,512]{1,0:T(8,128)(2,1)S(1)} %copy-done.5, bf16[256,512]{1,0:T(8,128)(2,1)S(1)} %copy-done.7, bf16[256,512]{1,0:T(8,128)(2,1)S(1)} %copy-done.6, bf16[3,256,128]{2,1,0:T(8,128)(2,1)S(1)} %collective-permute-done.6.refs_8_.refs_3_, ...), custom_call_target="tpu_custom_call" | custom-call | flops 1 | bytes 1 | tf_op jit(solution)/shard_map/attend/pallas_call | solution.py:33
  46.2 0.5 collective-permute-start.11
  46.6 1.5 collective-permute-start.23
  48.1 4.0 %collective-permute-done.14.refs_3_.refs_2_ = bf16[1024,128]{1,0:T(8,128)(2,1)S(1)} collective-permute-done((bf16[1024,128]{1,0:T(8,128)(2,1)S(1)}, bf16[1024,128]{1,0:T(8,128)(2,1)S(1)}, u32[]{:S(2)}, u32[]{:S(2)}) %collective-permute-start.14) | collective-permute-done | bytes 262176 | tf_op jit(solution)/shard_map/ppermute | solution.py:61
  52.3 2.7 %collective-permute-start.10 = (bf16[1024,128]{1,0:T(8,128)(2,1)S(1)}, bf16[1024,128]{1,0:T(8,128)(2,1)S(1)}, u32[]{:S(2)}, u32[]{:S(2)}) collective-permute-start(bf16[1024,128]{1,0:T(8,128)(2,1)S(1)} %get-tuple-element.36.refs_0_), channel_id=1, source_target_pairs={{0,4},{4,8},{8,12},{12,0},{1,5},{5,9},{9,13},{13,1},{2,6},{6,10},{... | collective-permute-start | bytes 786440 | tf_op jit(solution)/shard_map/ppermute | solution.py:61
  54.9 2.4 %collective-permute-done.11.refs_3_ = bf16[1024,128]{1,0:T(8,128)(2,1)S(1)} collective-permute-done((bf16[1024,128]{1,0:T(8,128)(2,1)S(1)}, bf16[1024,128]{1,0:T(8,128)(2,1)S(1)}, u32[]{:S(2)}, u32[]{:S(2)}) %collective-permute-start.11) | collective-permute-done | bytes 262176 | tf_op jit(solution)/shard_map/ppermute | solution.py:61
  57.3 2.4 %collective-permute-start.12 = (bf16[1024,128]{1,0:T(8,128)(2,1)S(1)}, bf16[1024,128]{1,0:T(8,128)(2,1)S(1)}, u32[]{:S(2)}, u32[]{:S(2)}) collective-permute-start(bf16[1024,128]{1,0:T(8,128)(2,1)S(1)} %collective-permute-done.11.refs_3_), channel_id=1, source_target_pairs={{0,12},{4,0},{8,4},{12,8},{1,13},{5,1},{9,5},{13,9},{2,14},{6,2},{... | collective-permute-start | bytes 786440 | tf_op jit(solution)/shard_map/ppermute | solution.py:61
  59.7 5.4 %collective-permute-done.15.refs_1_ = bf16[1024,128]{1,0:T(8,128)(2,1)S(1)} collective-permute-done((bf16[1024,128]{1,0:T(8,128)(2,1)S(1)}, bf16[1024,128]{1,0:T(8,128)(2,1)S(1)}, u32[]{:S(2)}, u32[]{:S(2)}) %collective-permute-start.15) | collective-permute-done | bytes 262176 | tf_op jit(solution)/shard_map/ppermute | solution.py:61
  65.1 1.5 attend_tan.1
  66.6 1.6 %collective-permute-start.17 = (bf16[512,128]{1,0:T(8,128)(2,1)S(1)}, bf16[512,128]{1,0:T(8,128)(2,1)S(1)}, u32[]{:S(2)}, u32[]{:S(2)}) collective-permute-start(bf16[512,128]{1,0:T(8,128)(2,1)S(1)} %get-tuple-element.44), channel_id=1, source_target_pairs={{0,2},{2,0},{1,3},{3,1},{4,6},{6,4},{5,7},{7,5},{8,10},{10,8},{9,1... | collective-permute-start | bytes 393224 | tf_op jit(solution)/shard_map/ppermute | solution.py:65
  68.2 2.5 %collective-permute-done.10.refs_2_.refs_1_ = bf16[1024,128]{1,0:T(8,128)(2,1)S(1)} collective-permute-done((bf16[1024,128]{1,0:T(8,128)(2,1)S(1)}, bf16[1024,128]{1,0:T(8,128)(2,1)S(1)}, u32[]{:S(2)}, u32[]{:S(2)}) %collective-permute-start.10) | collective-permute-done | bytes 262176 | tf_op jit(solution)/shard_map/ppermute | solution.py:61
  70.6 1.0 collective-permute-done.17.refs_1_
  71.7 1.6 %collective-permute-start.19 = (bf16[256,1024]{1,0:T(8,128)(2,1)S(1)}, bf16[256,1024]{1,0:T(8,128)(2,1)S(1)}, u32[]{:S(2)}, u32[]{:S(2)}) collective-permute-start(bf16[256,1024]{1,0:T(8,128)(2,1)S(1)} %get-tuple-element.46), channel_id=1, source_target_pairs={{0,2},{2,0},{1,3},{3,1},{4,6},{6,4},{5,7},{7,5},{8,10},{10,8},{9,1... | collective-permute-start | bytes 1572872 | tf_op jit(solution)/shard_map/ppermute | solution.py:65
  73.3 2.2 %collective-permute-done.12.refs_2_ = bf16[1024,128]{1,0:T(8,128)(2,1)S(1)} collective-permute-done((bf16[1024,128]{1,0:T(8,128)(2,1)S(1)}, bf16[1024,128]{1,0:T(8,128)(2,1)S(1)}, u32[]{:S(2)}, u32[]{:S(2)}) %collective-permute-start.12) | collective-permute-done | bytes 262176 | tf_op jit(solution)/shard_map/ppermute | solution.py:61
  75.5 0.1 cut_rows.1.refs_8_
  75.6 1.6 %collective-permute-start.18 = (bf16[512,512]{1,0:T(8,128)(2,1)S(1)}, bf16[512,512]{1,0:T(8,128)(2,1)S(1)}, u32[]{:S(2)}, u32[]{:S(2)}) collective-permute-start(bf16[512,512]{1,0:T(8,128)(2,1)S(1)} %cut_rows.1.refs_8_), channel_id=1, source_target_pairs={{0,2},{2,0},{1,3},{3,1},{4,6},{6,4},{5,7},{7,5},{8,10},{10,8},{9,1... | collective-permute-start | bytes 1572872 | tf_op jit(solution)/shard_map/ppermute | solution.py:65
  77.2 1.5 %collective-permute-start.24 = (bf16[256,1024]{1,0:T(8,128)(2,1)S(1)}, bf16[256,1024]{1,0:T(8,128)(2,1)S(1)}, u32[]{:S(2)}, u32[]{:S(2)}) collective-permute-start(bf16[256,1024]{1,0:T(8,128)(2,1)S(1)} %collective-permute-done.23.refs_6_.refs_3_.refs_2_), channel_id=1, source_target_pairs={{0,16},{16,0},{1,17},{17,1},{2,18},{18,2},{3,19},{19,3},{4,20},{20... | collective-permute-start | bytes 1572872 | tf_op jit(solution)/shard_map/ppermute | solution.py:65
  78.7 0.9 collective-permute-start.21
  79.6 1.1 collective-permute-start.20
  80.7 10.7 %collective-permute-done.21.refs_4_ = bf16[512,256]{1,0:T(8,128)(2,1)S(1)} collective-permute-done((bf16[512,256]{1,0:T(8,128)(2,1)S(1)}, bf16[512,256]{1,0:T(8,128)(2,1)S(1)}, u32[]{:S(2)}, u32[]{:S(2)}) %collective-permute-start.21) | collective-permute-done | bytes 262176 | tf_op jit(solution)/shard_map/ppermute | solution.py:61
  91.4 3.0 %collective-permute-done.18.refs_4_ = bf16[512,512]{1,0:T(8,128)(2,1)S(1)} collective-permute-done((bf16[512,512]{1,0:T(8,128)(2,1)S(1)}, bf16[512,512]{1,0:T(8,128)(2,1)S(1)}, u32[]{:S(2)}, u32[]{:S(2)}) %collective-permute-start.18) | collective-permute-done | bytes 524320 | tf_op jit(solution)/shard_map/ppermute | solution.py:65
  94.4 1.3 out_term.1.refs_0_.refs_8_
  95.7 2.0 %collective-permute-done.22.refs_3_ = bf16[512,256]{1,0:T(8,128)(2,1)S(1)} collective-permute-done((bf16[512,256]{1,0:T(8,128)(2,1)S(1)}, bf16[512,256]{1,0:T(8,128)(2,1)S(1)}, u32[]{:S(2)}, u32[]{:S(2)}) %collective-permute-start.22) | collective-permute-done | bytes 262176 | tf_op jit(solution)/shard_map/ppermute | solution.py:61
  97.8 1.3 out_sum.1.refs_0_.refs_5_
  99.2 2.6 %collective-permute-done.25.refs_1_ = bf16[512,1024]{1,0:T(8,128)(2,1)S(1)} collective-permute-done((bf16[512,1024]{1,0:T(8,128)(2,1)S(1)}, bf16[512,1024]{1,0:T(8,128)(2,1)S(1)}, u32[]{:S(2)}, u32[]{:S(2)}) %collective-permute-start.25) | collective-permute-done | bytes 1048608 | tf_op jit(solution)/shard_map/ppermute | solution.py:65
  101.8 1.0 grad_far.1
  102.9 0.4 collective-permute-start.28
  103.3 0.5 collective-permute-start.26
  103.8 1.5 grad_term.1
  105.3 3.7 %collective-permute-start.30 = (bf16[512,256]{1,0:T(8,128)(2,1)S(1)}, bf16[512,256]{1,0:T(8,128)(2,1)S(1)}, u32[]{:S(2)}, u32[]{:S(2)}) collective-permute-start(bf16[512,256]{1,0:T(8,128)(2,1)S(1)} %get-tuple-element.54), channel_id=1, source_target_pairs={{0,12},{4,0},{8,4},{12,8},{1,13},{5,1},{9,5},{13,9},{2,14},{6,2},{... | collective-permute-start | bytes 786440 | tf_op jit(solution)/shard_map/ppermute | solution.py:61
  109.0 5.1 %collective-permute-done.28.refs_0_ = bf16[512,256]{1,0:T(8,128)(2,1)S(1)} collective-permute-done((bf16[512,256]{1,0:T(8,128)(2,1)S(1)}, bf16[512,256]{1,0:T(8,128)(2,1)S(1)}, u32[]{:S(2)}, u32[]{:S(2)}) %collective-permute-start.28) | collective-permute-done | bytes 262176 | tf_op jit(solution)/shard_map/ppermute | solution.py:61
  114.2 5.4 %collective-permute-done.30.refs_2_ = bf16[512,256]{1,0:T(8,128)(2,1)S(1)} collective-permute-done((bf16[512,256]{1,0:T(8,128)(2,1)S(1)}, bf16[512,256]{1,0:T(8,128)(2,1)S(1)}, u32[]{:S(2)}, u32[]{:S(2)}) %collective-permute-start.30) | collective-permute-done | bytes 262176 | tf_op jit(solution)/shard_map/ppermute | solution.py:61
  119.6 4.9 %collective-permute-done.29.refs_1_ = bf16[512,256]{1,0:T(8,128)(2,1)S(1)} collective-permute-done((bf16[512,256]{1,0:T(8,128)(2,1)S(1)}, bf16[512,256]{1,0:T(8,128)(2,1)S(1)}, u32[]{:S(2)}, u32[]{:S(2)}) %collective-permute-start.29) | collective-permute-done | bytes 262176 | tf_op jit(solution)/shard_map/ppermute | solution.py:61
  124.6 0.6 collective-permute-start.31
  125.2 1.5 key_grad.2.refs_0_.refs_3_
  126.7 3.0 %collective-permute-done.31.refs_1_ = bf16[512,128]{1,0:T(8,128)(2,1)S(1)} collective-permute-done((bf16[512,128]{1,0:T(8,128)(2,1)S(1)}, bf16[512,128]{1,0:T(8,128)(2,1)S(1)}, u32[]{:S(2)}, u32[]{:S(2)}) %collective-permute-start.31) | collective-permute-done | bytes 131104 | tf_op jit(solution)/shard_map/ppermute | solution.py:65
  129.6 1.5 key_grad.3.refs_7_.refs_1_
  131.1 1.3 collective-permute-start.32
  132.5 0.7 collective-permute-start.34
  133.2 9.8 %collective-permute-done.32.refs_3_ = bf16[1024,128]{1,0:T(8,128)(2,1)S(1)} collective-permute-done((bf16[1024,128]{1,0:T(8,128)(2,1)S(1)}, bf16[1024,128]{1,0:T(8,128)(2,1)S(1)}, u32[]{:S(2)}, u32[]{:S(2)}) %collective-permute-start.32) | collective-permute-done | bytes 262176 | tf_op jit(solution)/shard_map/ppermute | solution.py:61
  143.0 0.7 collective-permute-start.33
  143.7 2.5 %out_product.1.refs_1_ = bf16[512,1024]{1,0:T(8,128)(2,1)} custom-call(bf16[1024,128]{1,0:T(8,128)(2,1)S(1)} %get-tuple-element.36.refs_0_, bf16[1024,128]{1,0:T(8,128)(2,1)S(1)} %collective-permute-done.10.refs_2_.refs_1_, bf16[1024,128]{1,0:T(8,128)(2,1)S(1)} %collective-permute-done.12.refs_2_, bf16[1024,128]{1,0:T(8,128)(2,1)S(1)} %collective-permute-done.11.refs_3_, ...), custom_call_target="tpu_custom_call" | custom-call | flops 1 | bytes 1 | tf_op jit(solution)/shard_map/out_product/pallas_call | solution.py:33
  146.2 1.2 copy-done.1
  147.4 0.6 flip.1.refs_0_.refs_4_
  148.1 1.8 %value_part.1 = (bf16[1024,128]{1,0:T(8,128)(2,1)S(1)}, bf16[1024,128]{1,0:T(8,128)(2,1)S(1)}, bf16[1024,128]{1,0:T(8,128)(2,1)S(1)}) custom-call(bf16[1024,1024]{1,0:T(8,128)(2,1)S(1)} %flip.1.refs_0_.refs_4_, bf16[1024,128]{1,0:T(8,128)(2,1)S(1)} %key_grad.3.refs_7_.refs_1_, bf16[1024,128]{1,0:T(8,128)(2,1)S(1)} %collective-permute-done.34.refs_2_, ...), custom_call_target="tpu_custom_call" | custom-call | flops 1 | bytes 1 | tf_op jit(solution)/shard_map/value_part/pallas_call | solution.py:33
  149.9 1.7 %value_product.1 = bf16[1024,512]{1,0:T(8,128)(2,1)} custom-call(bf16[1024,1024]{1,0:T(8,128)(2,1)S(1)} %flip.1.refs_0_.refs_4_, bf16[1024,128]{1,0:T(8,128)(2,1)S(1)} %collective-permute-done.33.refs_1_, bf16[1024,128]{1,0:T(8,128)(2,1)S(1)} %get-tuple-element.57.refs_2_.refs_5_, bf16[1024,128]{1,0:T(8,128)(2,1)S(1)} %get-tuple-element.58.refs_3_, ...), custom_call_target="tpu_custom_call" | custom-call | flops 1 | bytes 1 | tf_op jit(solution)/shard_map/value_product/pallas_call | solution.py:33
  (47 shorter events, 0.8 us)
Async XLA Ops:
  0.6 32.1 %copy-start = (bf16[512,1024]{1,0:T(8,128)(2,1)S(1)}, bf16[512,1024]{1,0:T(8,128)(2,1)}, u32[]{:S(2)}) copy-start(bf16[512,1024]{1,0:T(8,128)(2,1)} %refs_1_.3) | copy-start | bytes 3145732
  0.6 32.1 %copy-start.2 = (bf16[512,1024]{1,0:T(8,128)(2,1)S(1)}, bf16[512,1024]{1,0:T(8,128)(2,1)}, u32[]{:S(2)}) copy-start(bf16[512,1024]{1,0:T(8,128)(2,1)} %refs_5_.2) | copy-start | bytes 3145732
  1.9 9.4 %collective-permute-start.1 = (bf16[64,1024]{1,0:T(8,128)(2,1)S(1)}, bf16[64,1024]{1,0:T(8,128)(2,1)S(1)}, u32[]{:S(2)}, u32[]{:S(2)}) collective-permute-start(bf16[64,1024]{1,0:T(8,128)(2,1)S(1)} %get-tuple-element.61), channel_id=1, source_target_pairs={{0,4},{4,8},{8,12},{12,0},{1,5},{5,9},{9,13},{13,1},{2,6},{6,10},{... | collective-permute-start | bytes 393224 | tf_op jit(solution)/shard_map/ppermute | solution.py:61
  5.0 16.0 %collective-permute-start = (bf16[64,1024]{1,0:T(8,128)(2,1)S(1)}, bf16[64,1024]{1,0:T(8,128)(2,1)S(1)}, u32[]{:S(2)}, u32[]{:S(2)}) collective-permute-start(bf16[64,1024]{1,0:T(8,128)(2,1)S(1)} %get-tuple-element.62), channel_id=1, source_target_pairs={{0,12},{4,0},{8,4},{12,8},{1,13},{5,1},{9,5},{13,9},{2,14},{6,2},{... | collective-permute-start | bytes 393224 | tf_op jit(solution)/shard_map/ppermute | solution.py:61
  7.1 20.4 %collective-permute-start.2 = (bf16[64,1024]{1,0:T(8,128)(2,1)S(1)}, bf16[64,1024]{1,0:T(8,128)(2,1)S(1)}, u32[]{:S(2)}, u32[]{:S(2)}) collective-permute-start(bf16[64,1024]{1,0:T(8,128)(2,1)S(1)} %get-tuple-element.60), channel_id=1, source_target_pairs={{0,8},{4,12},{8,0},{12,4},{1,9},{5,13},{9,1},{13,5},{2,10},{6,14},... | collective-permute-start | bytes 393224 | tf_op jit(solution)/shard_map/ppermute | solution.py:61
  10.0 25.3 %copy-start.3 = (bf16[256,4096]{1,0:T(8,128)(2,1)S(1)}, bf16[256,4096]{1,0:T(8,128)(2,1)}, u32[]{:S(2)}) copy-start(bf16[256,4096]{1,0:T(8,128)(2,1)} %refs_0_.2) | copy-start | bytes 6291460
  10.0 25.3 %copy-start.4 = (bf16[1024,512]{1,0:T(8,128)(2,1)S(1)}, bf16[1024,512]{1,0:T(8,128)(2,1)}, u32[]{:S(2)}) copy-start(bf16[1024,512]{1,0:T(8,128)(2,1)} %refs_3_.1) | copy-start | bytes 3145732
  11.3 21.4 %collective-permute-start.7 = (bf16[3,256,128]{2,1,0:T(8,128)(2,1)S(1)}, bf16[3,256,128]{2,1,0:T(8,128)(2,1)S(1)}, u32[]{:S(2)}, u32[]{:S(2)}) collective-permute-start(bf16[3,256,128]{2,1,0:T(8,128)(2,1)S(1)} %pad_maximum_fusion.1), channel_id=1, source_target_pairs={{0,8},{4,12},{8,0},{12,4},{1,9},{5,13},{9,1},{13,5},{2,10},{6,14},... | collective-permute-start | bytes 589832 | tf_op jit(solution)/shard_map/ppermute | solution.py:61
  19.5 13.3 %collective-permute-start.6 = (bf16[3,256,128]{2,1,0:T(8,128)(2,1)S(1)}, bf16[3,256,128]{2,1,0:T(8,128)(2,1)S(1)}, u32[]{:S(2)}, u32[]{:S(2)}) collective-permute-start(bf16[3,256,128]{2,1,0:T(8,128)(2,1)S(1)} %pad_maximum_fusion), channel_id=1, source_target_pairs={{0,4},{4,8},{8,12},{12,0},{1,5},{5,9},{9,13},{13,1},{2,6},{6,10},{... | collective-permute-start | bytes 589832 | tf_op jit(solution)/shard_map/ppermute | solution.py:61
  19.5 9.5 %collective-permute-start.4 = (bf16[64,1024]{1,0:T(8,128)(2,1)S(1)}, bf16[64,1024]{1,0:T(8,128)(2,1)S(1)}, u32[]{:S(2)}, u32[]{:S(2)}) collective-permute-start(bf16[64,1024]{1,0:T(8,128)(2,1)S(1)} %collective-permute-done.1.refs_1_), channel_id=1, source_target_pairs={{0,2},{2,0},{1,3},{3,1},{4,6},{6,4},{5,7},{7,5},{8,10},{10,8},{9,1... | collective-permute-start | bytes 393224 | tf_op jit(solution)/shard_map/ppermute | solution.py:65
  21.0 8.0 %collective-permute-start.3 = (bf16[64,1024]{1,0:T(8,128)(2,1)S(1)}, bf16[64,1024]{1,0:T(8,128)(2,1)S(1)}, u32[]{:S(2)}, u32[]{:S(2)}) collective-permute-start(bf16[64,1024]{1,0:T(8,128)(2,1)S(1)} %collective-permute-done.refs_0_), channel_id=1, source_target_pairs={{0,2},{2,0},{1,3},{3,1},{4,6},{6,4},{5,7},{7,5},{8,10},{10,8},{9,1... | collective-permute-start | bytes 393224 | tf_op jit(solution)/shard_map/ppermute | solution.py:65
  27.4 5.3 %collective-permute-start.5 = (bf16[64,1024]{1,0:T(8,128)(2,1)S(1)}, bf16[64,1024]{1,0:T(8,128)(2,1)S(1)}, u32[]{:S(2)}, u32[]{:S(2)}) collective-permute-start(bf16[64,1024]{1,0:T(8,128)(2,1)S(1)} %collective-permute-done.2.refs_2_), channel_id=1, source_target_pairs={{0,2},{2,0},{1,3},{3,1},{4,6},{6,4},{5,7},{7,5},{8,10},{10,8},{9,1... | collective-permute-start | bytes 393224 | tf_op jit(solution)/shard_map/ppermute | solution.py:65
  33.0 2.4 %collective-permute-start.8 = (bf16[6,64,1024]{2,1,0:T(8,128)(2,1)S(1)}, bf16[6,64,1024]{2,1,0:T(8,128)(2,1)S(1)}, u32[]{:S(2)}, u32[]{:S(2)}) collective-permute-start(bf16[6,64,1024]{2,1,0:T(8,128)(2,1)S(1)} %get-tuple-element.33.refs_1_.refs_4_), channel_id=1, source_target_pairs={{0,1},{1,0},{2,3},{3,2},{4,5},{5,4},{6,7},{7,6},{8,9},{9,8},{10,11... | collective-permute-start | bytes 2359304 | tf_op jit(solution)/shard_map/ppermute | solution.py:65
  33.1 9.3 %copy-start.5 = (bf16[256,512]{1,0:T(8,128)(2,1)S(1)}, bf16[256,512]{1,0:T(8,128)(2,1)}, u32[]{:S(2)}) copy-start(bf16[256,512]{1,0:T(8,128)(2,1)} %refs_0_.3) | copy-start | bytes 786436
  33.1 9.3 %copy-start.6 = (bf16[256,512]{1,0:T(8,128)(2,1)S(1)}, bf16[256,512]{1,0:T(8,128)(2,1)}, u32[]{:S(2)}) copy-start(bf16[256,512]{1,0:T(8,128)(2,1)} %refs_2_.2) | copy-start | bytes 786436
  33.1 9.3 %copy-start.7 = (bf16[256,512]{1,0:T(8,128)(2,1)S(1)}, bf16[256,512]{1,0:T(8,128)(2,1)}, u32[]{:S(2)}) copy-start(bf16[256,512]{1,0:T(8,128)(2,1)} %refs_1_.2) | copy-start | bytes 786436
  33.1 9.3 %collective-permute-start.9 = (bf16[3,256,128]{2,1,0:T(8,128)(2,1)S(1)}, bf16[3,256,128]{2,1,0:T(8,128)(2,1)S(1)}, u32[]{:S(2)}, u32[]{:S(2)}) collective-permute-start(bf16[3,256,128]{2,1,0:T(8,128)(2,1)S(1)} %pad_maximum_fusion.2), channel_id=1, source_target_pairs={{0,12},{4,0},{8,4},{12,8},{1,13},{5,1},{9,5},{13,9},{2,14},{6,2},{... | collective-permute-start | bytes 589832 | tf_op jit(solution)/shard_map/ppermute | solution.py:61
  37.0 11.1 %collective-permute-start.13 = (bf16[1024,128]{1,0:T(8,128)(2,1)S(1)}, bf16[1024,128]{1,0:T(8,128)(2,1)S(1)}, u32[]{:S(2)}, u32[]{:S(2)}) collective-permute-start(bf16[1024,128]{1,0:T(8,128)(2,1)S(1)} %get-tuple-element.38), channel_id=1, source_target_pairs={{0,4},{4,8},{8,12},{12,0},{1,5},{5,9},{9,13},{13,1},{2,6},{6,10},{... | collective-permute-start | bytes 786440 | tf_op jit(solution)/shard_map/ppermute | solution.py:61
  37.1 15.0 %collective-permute-start.14 = (bf16[1024,128]{1,0:T(8,128)(2,1)S(1)}, bf16[1024,128]{1,0:T(8,128)(2,1)S(1)}, u32[]{:S(2)}, u32[]{:S(2)}) collective-permute-start(bf16[1024,128]{1,0:T(8,128)(2,1)S(1)} %get-tuple-element.40), channel_id=1, source_target_pairs={{0,12},{4,0},{8,4},{12,8},{1,13},{5,1},{9,5},{13,9},{2,14},{6,2},{... | collective-permute-start | bytes 786440 | tf_op jit(solution)/shard_map/ppermute | solution.py:61
  40.9 18.8 %collective-permute-start.16 = (bf16[256,1024]{1,0:T(8,128)(2,1)S(1)}, bf16[256,1024]{1,0:T(8,128)(2,1)S(1)}, u32[]{:S(2)}, u32[]{:S(2)}) collective-permute-start(bf16[256,1024]{1,0:T(8,128)(2,1)S(1)} %get-tuple-element.42), channel_id=1, source_target_pairs={{0,2},{2,0},{1,3},{3,1},{4,6},{6,4},{5,7},{7,5},{8,10},{10,8},{9,1... | collective-permute-start | bytes 1572872 | tf_op jit(solution)/shard_map/ppermute | solution.py:65
  46.2 11.2 %collective-permute-start.11 = (bf16[1024,128]{1,0:T(8,128)(2,1)S(1)}, bf16[1024,128]{1,0:T(8,128)(2,1)S(1)}, u32[]{:S(2)}, u32[]{:S(2)}) collective-permute-start(bf16[1024,128]{1,0:T(8,128)(2,1)S(1)} %get-tuple-element.36.refs_0_), channel_id=1, source_target_pairs={{0,12},{4,0},{8,4},{12,8},{1,13},{5,1},{9,5},{13,9},{2,14},{6,2},{... | collective-permute-start | bytes 786440 | tf_op jit(solution)/shard_map/ppermute | solution.py:61
  46.6 30.6 %collective-permute-start.23 = (bf16[256,1024]{1,0:T(8,128)(2,1)S(1)}, bf16[256,1024]{1,0:T(8,128)(2,1)S(1)}, u32[]{:S(2)}, u32[]{:S(2)}) collective-permute-start(bf16[256,1024]{1,0:T(8,128)(2,1)S(1)} %get-tuple-element.48), channel_id=1, source_target_pairs={{0,2},{2,0},{1,3},{3,1},{4,6},{6,4},{5,7},{7,5},{8,10},{10,8},{9,1... | collective-permute-start | bytes 1572872 | tf_op jit(solution)/shard_map/ppermute | solution.py:65
  52.2 12.9 %collective-permute-start.15 = (bf16[1024,128]{1,0:T(8,128)(2,1)S(1)}, bf16[1024,128]{1,0:T(8,128)(2,1)S(1)}, u32[]{:S(2)}, u32[]{:S(2)}) collective-permute-start(bf16[1024,128]{1,0:T(8,128)(2,1)S(1)} %add.63.refs_5_), channel_id=1, source_target_pairs={{0,4},{4,8},{8,12},{12,0},{1,5},{5,9},{9,13},{13,1},{2,6},{6,10},{... | collective-permute-start | bytes 786440 | tf_op jit(solution)/shard_map/ppermute | solution.py:61
  52.3 18.4 %collective-permute-start.10 = (bf16[1024,128]{1,0:T(8,128)(2,1)S(1)}, bf16[1024,128]{1,0:T(8,128)(2,1)S(1)}, u32[]{:S(2)}, u32[]{:S(2)}) collective-permute-start(bf16[1024,128]{1,0:T(8,128)(2,1)S(1)} %get-tuple-element.36.refs_0_), channel_id=1, source_target_pairs={{0,4},{4,8},{8,12},{12,0},{1,5},{5,9},{9,13},{13,1},{2,6},{6,10},{... | collective-permute-start | bytes 786440 | tf_op jit(solution)/shard_map/ppermute | solution.py:61
  57.3 18.1 %collective-permute-start.12 = (bf16[1024,128]{1,0:T(8,128)(2,1)S(1)}, bf16[1024,128]{1,0:T(8,128)(2,1)S(1)}, u32[]{:S(2)}, u32[]{:S(2)}) collective-permute-start(bf16[1024,128]{1,0:T(8,128)(2,1)S(1)} %collective-permute-done.11.refs_3_), channel_id=1, source_target_pairs={{0,12},{4,0},{8,4},{12,8},{1,13},{5,1},{9,5},{13,9},{2,14},{6,2},{... | collective-permute-start | bytes 786440 | tf_op jit(solution)/shard_map/ppermute | solution.py:61
  66.6 5.0 %collective-permute-start.17 = (bf16[512,128]{1,0:T(8,128)(2,1)S(1)}, bf16[512,128]{1,0:T(8,128)(2,1)S(1)}, u32[]{:S(2)}, u32[]{:S(2)}) collective-permute-start(bf16[512,128]{1,0:T(8,128)(2,1)S(1)} %get-tuple-element.44), channel_id=1, source_target_pairs={{0,2},{2,0},{1,3},{3,1},{4,6},{6,4},{5,7},{7,5},{8,10},{10,8},{9,1... | collective-permute-start | bytes 393224 | tf_op jit(solution)/shard_map/ppermute | solution.py:65
  71.7 19.7 %collective-permute-start.19 = (bf16[256,1024]{1,0:T(8,128)(2,1)S(1)}, bf16[256,1024]{1,0:T(8,128)(2,1)S(1)}, u32[]{:S(2)}, u32[]{:S(2)}) collective-permute-start(bf16[256,1024]{1,0:T(8,128)(2,1)S(1)} %get-tuple-element.46), channel_id=1, source_target_pairs={{0,2},{2,0},{1,3},{3,1},{4,6},{6,4},{5,7},{7,5},{8,10},{10,8},{9,1... | collective-permute-start | bytes 1572872 | tf_op jit(solution)/shard_map/ppermute | solution.py:65
  75.6 18.8 %collective-permute-start.18 = (bf16[512,512]{1,0:T(8,128)(2,1)S(1)}, bf16[512,512]{1,0:T(8,128)(2,1)S(1)}, u32[]{:S(2)}, u32[]{:S(2)}) collective-permute-start(bf16[512,512]{1,0:T(8,128)(2,1)S(1)} %cut_rows.1.refs_8_), channel_id=1, source_target_pairs={{0,2},{2,0},{1,3},{3,1},{4,6},{6,4},{5,7},{7,5},{8,10},{10,8},{9,1... | collective-permute-start | bytes 1572872 | tf_op jit(solution)/shard_map/ppermute | solution.py:65
  77.2 18.5 %collective-permute-start.24 = (bf16[256,1024]{1,0:T(8,128)(2,1)S(1)}, bf16[256,1024]{1,0:T(8,128)(2,1)S(1)}, u32[]{:S(2)}, u32[]{:S(2)}) collective-permute-start(bf16[256,1024]{1,0:T(8,128)(2,1)S(1)} %collective-permute-done.23.refs_6_.refs_3_.refs_2_), channel_id=1, source_target_pairs={{0,16},{16,0},{1,17},{17,1},{2,18},{18,2},{3,19},{19,3},{4,20},{20... | collective-permute-start | bytes 1572872 | tf_op jit(solution)/shard_map/ppermute | solution.py:65
  78.7 12.7 %collective-permute-start.21 = (bf16[512,256]{1,0:T(8,128)(2,1)S(1)}, bf16[512,256]{1,0:T(8,128)(2,1)S(1)}, u32[]{:S(2)}, u32[]{:S(2)}) collective-permute-start(bf16[512,256]{1,0:T(8,128)(2,1)S(1)} %join.1.refs_4_.refs_1_), channel_id=1, source_target_pairs={{0,12},{4,0},{8,4},{12,8},{1,13},{5,1},{9,5},{13,9},{2,14},{6,2},{... | collective-permute-start | bytes 786440 | tf_op jit(solution)/shard_map/ppermute | solution.py:61
  79.6 16.1 %collective-permute-start.20 = (bf16[512,256]{1,0:T(8,128)(2,1)S(1)}, bf16[512,256]{1,0:T(8,128)(2,1)S(1)}, u32[]{:S(2)}, u32[]{:S(2)}) collective-permute-start(bf16[512,256]{1,0:T(8,128)(2,1)S(1)} %join.1.refs_4_.refs_1_), channel_id=1, source_target_pairs={{0,4},{4,8},{8,12},{12,0},{1,5},{5,9},{9,13},{13,1},{2,6},{6,10},{... | collective-permute-start | bytes 786440 | tf_op jit(solution)/shard_map/ppermute | solution.py:61
  91.4 6.4 %collective-permute-start.22 = (bf16[512,256]{1,0:T(8,128)(2,1)S(1)}, bf16[512,256]{1,0:T(8,128)(2,1)S(1)}, u32[]{:S(2)}, u32[]{:S(2)}) collective-permute-start(bf16[512,256]{1,0:T(8,128)(2,1)S(1)} %collective-permute-done.21.refs_4_), channel_id=1, source_target_pairs={{0,12},{4,0},{8,4},{12,8},{1,13},{5,1},{9,5},{13,9},{2,14},{6,2},{... | collective-permute-start | bytes 786440 | tf_op jit(solution)/shard_map/ppermute | solution.py:61
  99.1 2.7 %collective-permute-start.25 = (bf16[512,1024]{1,0:T(8,128)(2,1)S(1)}, bf16[512,1024]{1,0:T(8,128)(2,1)S(1)}, u32[]{:S(2)}, u32[]{:S(2)}) collective-permute-start(bf16[512,1024]{1,0:T(8,128)(2,1)S(1)} %out_sum.1.refs_0_.refs_5_), channel_id=1, source_target_pairs={{0,1},{1,0},{2,3},{3,2},{4,5},{5,4},{6,7},{7,6},{8,9},{9,8},{10,11... | collective-permute-start | bytes 3145736 | tf_op jit(solution)/shard_map/ppermute | solution.py:65
  102.9 11.2 %collective-permute-start.28 = (bf16[512,256]{1,0:T(8,128)(2,1)S(1)}, bf16[512,256]{1,0:T(8,128)(2,1)S(1)}, u32[]{:S(2)}, u32[]{:S(2)}) collective-permute-start(bf16[512,256]{1,0:T(8,128)(2,1)S(1)} %get-tuple-element.52), channel_id=1, source_target_pairs={{0,4},{4,8},{8,12},{12,0},{1,5},{5,9},{9,13},{13,1},{2,6},{6,10},{... | collective-permute-start | bytes 786440 | tf_op jit(solution)/shard_map/ppermute | solution.py:61
  103.3 21.9 %collective-permute-start.26 = (bf16[256,1024]{1,0:T(8,128)(2,1)S(1)}, bf16[256,1024]{1,0:T(8,128)(2,1)S(1)}, u32[]{:S(2)}, u32[]{:S(2)}) collective-permute-start(bf16[256,1024]{1,0:T(8,128)(2,1)S(1)} %get-tuple-element.50), channel_id=1, source_target_pairs={{0,2},{2,0},{1,3},{3,1},{4,6},{6,4},{5,7},{7,5},{8,10},{10,8},{9,1... | collective-permute-start | bytes 1572872 | tf_op jit(solution)/shard_map/ppermute | solution.py:65
  105.3 14.3 %collective-permute-start.30 = (bf16[512,256]{1,0:T(8,128)(2,1)S(1)}, bf16[512,256]{1,0:T(8,128)(2,1)S(1)}, u32[]{:S(2)}, u32[]{:S(2)}) collective-permute-start(bf16[512,256]{1,0:T(8,128)(2,1)S(1)} %get-tuple-element.54), channel_id=1, source_target_pairs={{0,12},{4,0},{8,4},{12,8},{1,13},{5,1},{9,5},{13,9},{2,14},{6,2},{... | collective-permute-start | bytes 786440 | tf_op jit(solution)/shard_map/ppermute | solution.py:61
  114.1 10.4 %collective-permute-start.29 = (bf16[512,256]{1,0:T(8,128)(2,1)S(1)}, bf16[512,256]{1,0:T(8,128)(2,1)S(1)}, u32[]{:S(2)}, u32[]{:S(2)}) collective-permute-start(bf16[512,256]{1,0:T(8,128)(2,1)S(1)} %add.64.refs_3_), channel_id=1, source_target_pairs={{0,4},{4,8},{8,12},{12,0},{1,5},{5,9},{9,13},{13,1},{2,6},{6,10},{... | collective-permute-start | bytes 786440 | tf_op jit(solution)/shard_map/ppermute | solution.py:61
  124.6 5.0 %collective-permute-start.31 = (bf16[512,128]{1,0:T(8,128)(2,1)S(1)}, bf16[512,128]{1,0:T(8,128)(2,1)S(1)}, u32[]{:S(2)}, u32[]{:S(2)}) collective-permute-start(bf16[512,128]{1,0:T(8,128)(2,1)S(1)} %get-tuple-element.56), channel_id=1, source_target_pairs={{0,2},{2,0},{1,3},{3,1},{4,6},{6,4},{5,7},{7,5},{8,10},{10,8},{9,1... | collective-permute-start | bytes 393224 | tf_op jit(solution)/shard_map/ppermute | solution.py:65
  125.2 18.5 %collective-permute-start.27 = (bf16[256,1024]{1,0:T(8,128)(2,1)S(1)}, bf16[256,1024]{1,0:T(8,128)(2,1)S(1)}, u32[]{:S(2)}, u32[]{:S(2)}) collective-permute-start(bf16[256,1024]{1,0:T(8,128)(2,1)S(1)} %collective-permute-done.26.refs_5_), channel_id=1, source_target_pairs={{0,1},{1,0},{2,3},{3,2},{4,5},{5,4},{6,7},{7,6},{8,9},{9,8},{10,11... | collective-permute-start | bytes 1572872 | tf_op jit(solution)/shard_map/ppermute | solution.py:65
  131.1 11.9 %collective-permute-start.32 = (bf16[1024,128]{1,0:T(8,128)(2,1)S(1)}, bf16[1024,128]{1,0:T(8,128)(2,1)S(1)}, u32[]{:S(2)}, u32[]{:S(2)}) collective-permute-start(bf16[1024,128]{1,0:T(8,128)(2,1)S(1)} %key_grad.3.refs_7_.refs_1_), channel_id=1, source_target_pairs={{0,12},{4,0},{8,4},{12,8},{1,13},{5,1},{9,5},{13,9},{2,14},{6,2},{... | collective-permute-start | bytes 786440 | tf_op jit(solution)/shard_map/ppermute | solution.py:61
  132.5 15.6 %collective-permute-start.34 = (bf16[1024,128]{1,0:T(8,128)(2,1)S(1)}, bf16[1024,128]{1,0:T(8,128)(2,1)S(1)}, u32[]{:S(2)}, u32[]{:S(2)}) collective-permute-start(bf16[1024,128]{1,0:T(8,128)(2,1)S(1)} %key_grad.3.refs_7_.refs_1_), channel_id=1, source_target_pairs={{0,4},{4,8},{8,12},{12,0},{1,5},{5,9},{9,13},{13,1},{2,6},{6,10},{... | collective-permute-start | bytes 786440 | tf_op jit(solution)/shard_map/ppermute | solution.py:61
  143.0 6.9 %collective-permute-start.33 = (bf16[1024,128]{1,0:T(8,128)(2,1)S(1)}, bf16[1024,128]{1,0:T(8,128)(2,1)S(1)}, u32[]{:S(2)}, u32[]{:S(2)}) collective-permute-start(bf16[1024,128]{1,0:T(8,128)(2,1)S(1)} %collective-permute-done.32.refs_3_), channel_id=1, source_target_pairs={{0,12},{4,0},{8,4},{12,8},{1,13},{5,1},{9,5},{13,9},{2,14},{6,2},{... | collective-permute-start | bytes 786440 | tf_op jit(solution)/shard_map/ppermute | solution.py:61
  146.2 1.2 copy-start.1
